TPU v7x, 128 devices: a whole 4x4x4 slice. The times are simulated.
128 devices in a mesh: gx: 16 (over x_hi, y, core), gy: 8 (over x_lo, z).
Axes of the slice: x: 4 (x_hi: 2, x_lo: 2; x = x_hi * 2 + x_lo), y: 4, z: 4, core: 2. Of those that a mesh axis runs over, the one named last changes fastest.
Arguments:
- positions: float32 [3, 64, 32, 4, 128], P(None, 'gx', 'gy'), may hold values from 0 to 128, as said below
- velocity: float32 [3, 64, 32, 4, 128], P(None, 'gx', 'gy'), may hold values from -5 to 5
- density: float32 [64, 32, 4, 128], P('gx', 'gy'), may hold values from 0.98 to 1.02
- masses: float32 [64, 32, 4, 128], P('gx', 'gy'), may hold values from 0.04 to 0.08
- counts: int32 [64, 32, 4], P('gx', 'gy'), may hold values from 0 to 128, as said below
Outputs:
- density_rate: float32 [64, 32, 4, 128], P('gx', 'gy')
- acceleration: float32 [3, 64, 32, 4, 128], P(None, 'gx', 'gy')
Inputs may be any that keep to these rules, and one draw needn't show every extreme that they name: `positions`: the particle in a slot of the block at indices (a, b, c) lies in the cell [2a, 2a + 2) x [2b, 2b + 2) x [2c, 2c + 2); values in slots that are not live are meaningless. `counts`: slots below a block's count are live. The bottom block of every column inside the water column is full.
All inputs are finite; a program needn't handle non-finite values.
Results may differ from a plain program's by a relative error of at most 0.0001.
Values sent between devices are 32-bit elements; how exact they have to be, the bound alone decides.
No kernel may reach another device: no remote copies, remote signals or barrier semaphores. Data moves between devices by JAX's collectives and lax.ppermute only.
A program may use at most 64 MiB of HBM per device.

v0:
```python
import math

import jax
import jax.numpy as jnp
import numpy as np
from jax import lax
from jax.sharding import PartitionSpec as P

KERNEL_GRAD = 105.0 / (16.0 * math.pi)
REGULAR = 0.2
STIFFNESS = 100.0 / 7.0
VISCOUS = 0.5
GRAVITY = 1.0
SOFTEN = 0.01
SYM_PAIRS = ((0, 0), (1, 1), (2, 2), (0, 1), (0, 2), (1, 2))
SYM_INDEX = ((0, 3, 4), (3, 1, 5), (4, 5, 2))
HALF_OFFSETS = tuple(
    [(0, 0, 0)]
    + [(a, 1, c) for a in (-1, 0, 1) for c in (-1, 0, 1)]
    + [(1, 0, c) for c in (-1, 0, 1)]
    + [(0, 0, 1)]
)


def shifted(value, axis, steps):
    count = lax.axis_size(axis)
    first, last = (max(0, -steps), min(count, count - steps))
    return lax.ppermute(value, axis, [(source, source + steps) for source in range(first, last)])


def extended_2(x, sides, width):
    for axis, dim in sides:
        peers, length = (lax.axis_size(axis), x.shape[dim])
        up = [(i, (i + 1) % peers) for i in range(peers - 1)]
        down = [(j, i) for i, j in up]
        last = lax.slice_in_dim(x, length - width, length, axis=dim)
        first = lax.slice_in_dim(x, 0, width, axis=dim)
        before = lax.ppermute(last, axis, up)
        after = lax.ppermute(first, axis, down)
        x = jnp.concatenate([before, x, after], axis=dim)
    return x


def neighbour_tables(local_shape, ext_shape, anchor, offsets):
    width_x, width_y, height = local_shape
    ext_x, ext_y, ext_z = ext_shape
    target_list = []
    partner_list = []
    for a in range(width_x):
        for b in range(width_y):
            for c in range(height):
                pos_a = a + anchor[0]
                pos_b = b + anchor[1]
                pos_c = c + anchor[2]
                target_list.append((pos_a * ext_y + pos_b) * ext_z + pos_c)
                partner_list.append(
                    [
                        ((pos_a + d[0]) * ext_y + pos_b + d[1]) * ext_z + pos_c + d[2]
                        for d in offsets
                    ]
                )
    return (
        jnp.asarray(np.array(target_list, np.int32)),
        jnp.asarray(np.array(partner_list, np.int32)),
    )


def build_state(positions, velocity, density, masses, live_mask):
    press_term = STIFFNESS * (density**7 - 1.0) / (density * density)
    return jnp.concatenate(
        [
            positions,
            velocity,
            (masses * live_mask)[None],
            (live_mask * masses / density)[None],
            density[None],
            press_term[None],
        ],
        0,
    )


def kernel_terms(target, partner):
    delta = target[0:3][None, :, :, None] - partner[:, 0:3][:, :, None, :]
    radius_sq = jnp.sum(delta * delta, axis=1)
    falloff = jnp.maximum(1.0 - 0.5 * jnp.sqrt(radius_sq), 0.0)
    return (delta, radius_sq, KERNEL_GRAD * falloff * falloff * falloff)


def tensor_pair(target, partner):
    delta, radius_sq, kernel_c = kernel_terms(target, partner)
    weight_i = kernel_c * partner[:, 7][:, None, :]
    weight_j = kernel_c * target[7][None, :, None]
    side_i = []
    side_j = []
    for pair_ab in SYM_PAIRS:
        outer = delta[:, pair_ab[0]] * delta[:, pair_ab[1]]
        side_i.append(jnp.sum(weight_i * outer, axis=(0, 2)))
        side_j.append(jnp.sum(weight_j * outer, axis=1))
    return (jnp.stack(side_i, 0), jnp.stack(side_j, 1))


def motion_pair(target, target_corr, partner, partner_corr):
    delta, radius_sq, kernel_c = kernel_terms(target, partner)
    grads = []
    for a in range(3):
        along_i = target_corr[SYM_INDEX[a][0]][None, :, None] * delta[:, 0]
        along_j = partner_corr[:, SYM_INDEX[a][0]][:, None, :] * delta[:, 0]
        for b in (1, 2):
            along_i = along_i + target_corr[SYM_INDEX[a][b]][None, :, None] * delta[:, b]
            along_j = along_j + partner_corr[:, SYM_INDEX[a][b]][:, None, :] * delta[:, b]
        grads.append(-0.5 * kernel_c * (along_i + along_j))
    vel_diff = target[3:6][None, :, :, None] - partner[:, 3:6][:, :, None, :]
    v_dot_g = vel_diff[:, 0] * grads[0] + vel_diff[:, 1] * grads[1] + vel_diff[:, 2] * grads[2]
    v_dot_x = (
        vel_diff[:, 0] * delta[:, 0] + vel_diff[:, 1] * delta[:, 1] + vel_diff[:, 2] * delta[:, 2]
    )
    mean_rho = 0.5 * (target[8][None, :, None] + partner[:, 8][:, None, :])
    viscous = -VISCOUS * jnp.minimum(v_dot_x, 0.0) / (radius_sq + SOFTEN) / mean_rho
    pressure = target[9][None, :, None] + partner[:, 9][:, None, :] + viscous
    mass_j = partner[:, 6][:, None, :]
    mass_i = target[6][None, :, None]
    side_i = [jnp.sum(mass_j * v_dot_g, axis=(0, 2))]
    side_j = [jnp.sum(mass_i * v_dot_g, axis=1)]
    for a in range(3):
        side_i.append(-jnp.sum(mass_j * pressure * grads[a], axis=(0, 2)))
        side_j.append(jnp.sum(mass_i * pressure * grads[a], axis=1))
    return (jnp.stack(side_i, 0), jnp.stack(side_j, 1))


def invert_blocks(moment):
    a = moment[..., 0, :] + REGULAR
    d = moment[..., 1, :] + REGULAR
    f = moment[..., 2, :] + REGULAR
    b = moment[..., 3, :]
    c = moment[..., 4, :]
    e = moment[..., 5, :]
    cof_xx = d * f - e * e
    cof_xy = c * e - b * f
    cof_xz = b * e - c * d
    cof_yy = a * f - c * c
    cof_yz = b * c - a * e
    cof_zz = a * d - b * b
    determinant = a * cof_xx + b * cof_xy + c * cof_xz
    return (
        jnp.stack([cof_xx, cof_yy, cof_zz, cof_xy, cof_xz, cof_yz], -2) / determinant[..., None, :]
    )


def pad_vertical(extended):
    empty_layer = jnp.zeros_like(extended[:, :, :1])
    return jnp.concatenate([empty_layer, extended, empty_layer], 2)


def forward_half(blocks):
    first_row = blocks[:, 0:1]
    arrived_row = shifted(first_row, "gy", -1)
    widened = jnp.concatenate([blocks, arrived_row], 1)
    extended = extended_2(widened, (("gx", 0),), 1)
    return pad_vertical(extended)


def backward_half(totals):
    trimmed = totals[:, :, 1:-1]
    rims = jnp.stack([trimmed[0], trimmed[-1]], 0)
    arrived = extended_2(rims, (("gx", 0),), 1)
    inner = trimmed[1:-1]
    inner = inner.at[0].add(arrived[0]).at[-1].add(arrived[3])
    spill_row = inner[:, -1:]
    returned = shifted(spill_row, "gy", 1)
    return inner[:, :-1].at[:, 0:1].add(returned)


def first_terms(target, partner):
    return tensor_pair(target[0], partner[0])


def second_terms(target, partner):
    return motion_pair(target[0], target[1], partner[0], partner[1])


def sweep_blocks(pair_fn, sources, targets, partners, occupied, credit, channels):
    slot_count = sources[0].shape[-1]
    extent = sources[0].shape[0]

    def block_step(totals, block_item):
        target_id, partner_ids, has_work = block_item
        target = tuple((source[target_id] for source in sources))
        partner = tuple((source[partner_ids] for source in sources))
        own_side, far_side = pair_fn(target, partner)
        totals = totals.at[partner_ids].add(far_side * credit[:, None, None])
        return (totals, own_side)

    start = jnp.zeros((extent, channels, slot_count), jnp.float32)
    totals, own_terms = lax.scan(block_step, start, (targets, partners, occupied))
    return (own_terms, totals)


def body(positions, velocity, density, masses, counts):
    width_x, width_y, height = counts.shape
    slot_count = density.shape[3]
    local_shape = (width_x, width_y, height)
    live_mask = (lax.broadcasted_iota(jnp.int32, density.shape, 3) < counts[..., None]).astype(
        jnp.float32
    )
    blocks = jnp.transpose(
        build_state(positions, velocity, density, masses, live_mask), (1, 2, 3, 0, 4)
    )
    occupied = (counts > 0).reshape(-1)
    extended = forward_half(blocks)
    ext_shape = extended.shape[:3]
    targets, partners = neighbour_tables(local_shape, ext_shape, (1, 0, 1), HALF_OFFSETS)
    credit = jnp.asarray([0.0] + [1.0] * (len(HALF_OFFSETS) - 1), jnp.float32)
    flat_state = extended.reshape(-1, 10, slot_count)
    moment_own, moment_far = sweep_blocks(
        first_terms, (flat_state,), targets, partners, occupied, credit, 6
    )
    moment = moment_own.reshape(local_shape + (6, slot_count)) + backward_half(
        moment_far.reshape(ext_shape + (6, slot_count))
    )
    correction = invert_blocks(moment)
    flat_corr = forward_half(correction).reshape(-1, 6, slot_count)
    rate_own, rate_far = sweep_blocks(
        second_terms, (flat_state, flat_corr), targets, partners, occupied, credit, 4
    )
    rates = rate_own.reshape(local_shape + (4, slot_count)) + backward_half(
        rate_far.reshape(ext_shape + (4, slot_count))
    )
    density_rate = rates[..., 0, :] * live_mask
    acceleration = jnp.transpose(rates[..., 1:4, :], (3, 0, 1, 2, 4)) * live_mask[None]
    acceleration = acceleration.at[2].add(-GRAVITY * live_mask)
    return (density_rate, acceleration)


def solution(mesh):
    return jax.shard_map(
        body,
        mesh=mesh,
        in_specs=(
            P(None, "gx", "gy", None, None),
            P(None, "gx", "gy", None, None),
            P("gx", "gy", None, None),
            P("gx", "gy", None, None),
            P("gx", "gy", None),
        ),
        out_specs=(P("gx", "gy", None, None), P(None, "gx", "gy", None, None)),
        check_vma=False,
    )
```

profile of v0, /device:TPU:6, one launch (start us, length us, event | category | flops | bytes accessed | tf_op | source)
XLA Modules:
  0.0 1241.1 jit_solution(6821174178986644501)
XLA Ops:
  5.8 6.2 collective-permute-start
  12.0 2.0 collective-permute-done
  16.0 7.3 collective-permute-start.2
  26.4 493.3 %while.33 = (s32[]{:T(128)}, f32[180,6,128]{2,1,0:T(8,128)S(1)}, f32[64,6,128]{2,1,0:T(8,128)S(1)}, f32[180,10,128]{2,1,0:T(8,128)S(1)}, s32[]{:T(128)}, /*index...) while((s32[]{:T(128)}, f32[180,6,128]{2,1,0:T(8,128)S(1)}, ...), condition=%wide.region_15.16_spmd.clone, body=%wide.region_0.15_spmd.sunk.clone.sunk | while | flops 10562352 | bytes 8096275 | solution.py:195
  30.8 2.0 fusion.54
  38.5 2.0 fusion.54
  46.2 2.0 fusion.54
  53.9 2.0 fusion.54
  69.4 2.0 fusion.54
  77.1 2.0 fusion.54
  84.8 2.0 fusion.54
  92.5 2.0 fusion.54
  107.9 2.0 fusion.54
  123.3 2.0 fusion.54
  131.0 2.0 fusion.54
  138.7 2.0 fusion.54
  146.4 2.0 fusion.54
  161.8 2.0 fusion.54
  169.5 2.0 fusion.54
  177.3 2.0 fusion.54
  185.0 2.0 fusion.54
  192.7 2.0 fusion.54
  200.4 2.0 fusion.54
  215.8 2.0 fusion.54
  223.5 2.0 fusion.54
  231.2 2.0 fusion.54
  238.9 2.0 fusion.54
  254.3 2.0 fusion.54
  269.7 2.0 fusion.54
  277.4 2.0 fusion.54
  285.2 2.0 fusion.54
  292.9 2.0 fusion.54
  308.3 2.0 fusion.54
  316.0 2.0 fusion.54
  323.7 2.0 fusion.54
  331.4 2.0 fusion.54
  339.1 2.0 fusion.54
  346.8 2.0 fusion.54
  362.2 2.0 fusion.54
  369.9 2.0 fusion.54
  521.8 7.4 collective-permute-start.4
  533.0 6.5 collective-permute-done.5
  539.8 3.9 collective-permute-start.6
  543.8 2.1 collective-permute-done.6
  547.8 7.3 collective-permute-start.8
  557.4 662.9 %while.34 = (s32[]{:T(128)}, f32[180,4,128]{2,1,0:T(4,128)S(1)}, f32[64,4,128]{2,1,0:T(4,128)S(1)}, f32[180,10,128]{2,1,0:T(8,128)S(1)}, f32[180,6,128]{2,1,0:T(...) while((s32[]{:T(128)}, f32[180,4,128]{2,1,0:T(4,128)S(1)}, ...), condition=%wide.region_27.28_spmd.clone, body=%wide.region_16.27_spmd.sunk.clone.sunk | while | flops 20904372 | bytes 27647136 | solution.py:195
  1222.3 7.3 collective-permute-start.10
  1233.3 5.9 collective-permute-done.11
  (3365 shorter events, 841.6 us)
Async XLA Ops:
  5.8 8.3 collective-permute-start
  14.1 9.6 collective-permute-start.1
  16.0 9.5 collective-permute-start.2
  25.6 0.8 copy-start.1
  25.6 0.8 copy-start.2
  519.7 9.4 collective-permute-start.3
  521.8 9.2 collective-permute-start.4
  531.0 8.5 collective-permute-start.5
  539.8 6.0 collective-permute-start.6
  545.8 9.2 collective-permute-start.7
  547.8 9.1 collective-permute-start.8
  557.4 675.8 %copy-start = (s32[4,4,4]{2,1,0:T(4,128)S(1)}, s32[4,4,4]{2,1,0:T(4,128)}, u32[]{:S(2)}) copy-start(s32[4,4,4]{2,1,0:T(4,128)} %param.30) | copy-start | bytes 772
  1220.3 9.3 collective-permute-start.9
  1222.3 9.0 collective-permute-start.10
  1231.3 7.9 collective-permute-start.11
where the time goes:
time: 1250 us; the launch traced here: 1240 us
  other arithmetic  692 us (55%)
  loops' own time  270 us (22%)
  local copies, waits for them, and re-layouts  203 us (16%)
  starting transfers between devices  50.8 us (4%)
  waiting for transfers between devices  23.9 us (2%)
    another operation x2, loops' own time, sweep_blocks(): lax.scan(block_step, start, (targets, partners, occupied))  270 us
    scatter-add x128, other arithmetic, block_step(): totals = totals.at[partner_ids].add(far_side * credit[:, None, None])  134 us
    reduce_sum x64, other arithmetic, tensor_pair(): side_i.append(jnp.sum(weight_i * outer, axis=(0, 2)))  128 us
    add x64, other arithmetic, motion_pair(): vel_diff[:, 0] * grads[0] + vel_diff[:, 1] * grads[1]  120 us
    reduce_sum x64, other arithmetic, motion_pair(): side_i = [jnp.sum(mass_j * v_dot_g, axis=(0, 2))]  110 us
    gather x192, local copies, waits for them, and re-layouts, block_step(): partner = tuple((source[partner_ids] for source in sources))  108 us
    reduce_sum x128, other arithmetic, kernel_terms(): radius_sq = jnp.sum(delta * delta, axis=1)  93 us
    select_n x128, other arithmetic, block_step(): totals = totals.at[partner_ids].add(far_side * credit[:, None, None])  89.7 us
  transfers between devices with their start and end apart: 12, of which 9 were waited for; matrix products, arithmetic and copies ran while one was open for 0% of the time, Pallas kernels for 0%

commit v1 on v0

v1 whole, which is shorter than its diff:
```python
import functools
import math

import jax
import jax.numpy as jnp
import numpy as np
from jax import lax
from jax.experimental import pallas as pl
from jax.experimental.pallas import tpu as pltpu
from jax.sharding import PartitionSpec as P

KERNEL_GRAD = 105.0 / (16.0 * math.pi)
REGULAR = 0.2
STIFFNESS = 100.0 / 7.0
GRAVITY = 1.0
SOFTEN = 0.01
TINY = 1e-12
SYM_PAIRS = ((0, 0), (1, 1), (2, 2), (0, 1), (0, 2), (1, 2))
SYM_INDEX = ((0, 3, 4), (3, 1, 5), (4, 5, 2))
F32 = jnp.float32
BF16 = jnp.bfloat16
LOCAL = 64
TOTAL = 144
KA = 80
M1 = 32
M2 = 128
MW = 48
NB = 9
W_ROWS = 40
LEVEL_PAIRS = ((0, 0), (0, 1), (1, 0), (1, 1), (1, 2), (2, 1), (2, 2), (2, 3), (3, 2), (3, 3))


def column_bases():
    base = np.zeros((6, 6), np.int32)
    for a in range(6):
        for b in range(6):
            if a == 0:
                base[a, b] = 96 + b * 4
            elif a == 5:
                base[a, b] = 120 + b * 4
            elif b == 0:
                base[a, b] = 64 + (a - 1) * 4
            elif b == 5:
                base[a, b] = 80 + (a - 1) * 4
            else:
                base[a, b] = ((a - 1) * 4 + (b - 1)) * 4
    return base


def item_table(columns):
    base = column_bases()
    rows = []
    for c, d in LEVEL_PAIRS:
        for a, b in columns:
            row = [((a - 1) * 4 + (b - 1)) * 4 + c]
            for da in (-1, 0, 1):
                for db in (-1, 0, 1):
                    row.append(base[a + da, b + db] + d)
            rows.append(row)
    return np.asarray(rows, np.int32).reshape(-1)


def split3(x):
    h = x.astype(BF16).astype(F32)
    r = x - h
    m = r.astype(BF16).astype(F32)
    return h, m, r - m


def pair_rows(state, corner, k, with_targets, rows_ref, a_ref, b_ref, rho_ref):
    blk = pl.ds(pl.multiple_of(k * 8, 8), 8)
    x = [state[d, blk, :] - corner[d] for d in range(3)]
    v = [state[3 + d, blk, :] for d in range(3)]
    rho = state[6, blk, :]
    n2 = x[0] * x[0] + x[1] * x[1] + x[2] * x[2]
    xv = x[0] * v[0] + x[1] * v[1] + x[2] * v[2]
    one = jnp.ones_like(n2)
    zero = jnp.zeros_like(n2)
    xs = [split3(t) for t in x]
    vs = [split3(t) for t in v]
    rs = split3(rho)
    n2s = split3(n2)
    xvs = split3(xv)

    def put(group, parts):
        for r, p in enumerate(parts):
            rows_ref[pl.ds((group * 8 + r) * 8, 8), :] = p

    def get(group, b):
        return rows_ref[pl.ds(group * 64 + b, 8, stride=8), :]

    for s in range(3):
        put(s, [xs[d][s] for d in range(3)] + [vs[d][s] for d in range(3)] + [rs[s], one])
    put(3, list(n2s) + list(xvs) + [one, one])
    if with_targets:
        for s in range(3):
            put(4 + s, [-0.5 * xs[d][s] for d in range(3)] + [zero] * 5)
            put(7 + s, [-vs[d][s] for d in range(3)] + [-xs[d][s] for d in range(3)] + [zero] * 2)
        quarter = one * 0.25
        put(10, [-0.5 * xs[d][0] for d in range(3)] + [zero] * 4 + [0.25 * n2s[2]])
        put(11, [-vs[d][0] for d in range(3)] + [-xs[d][0] for d in range(3)] + [zero, xvs[2]])
        put(12, [quarter] * 3 + [zero] * 3 + [0.25 * n2s[0], 0.25 * n2s[1]])
        put(13, [zero] * 3 + [one] * 3 + [xvs[0], xvs[1]])
    pad = jnp.zeros((128 - KA, 128), F32)
    for b in range(8):
        g = [get(s, b) for s in range(4)]
        rows = jnp.concatenate([g[0]] * 3 + [g[1]] * 3 + [g[2]] * 3 + [g[3], pad], 0)
        cols = rows.T
        a_ref[k * 8 + b] = cols[:, :KA].astype(BF16)
        if rho_ref is not None:
            col = cols[:, 6:7] + cols[:, 30:31] + cols[:, 54:55]
            rho_ref[k * 8 + b] = jnp.broadcast_to(col, (128, 128))
        if with_targets:
            r2_rows = [get(10, b), get(5, b), get(6, b)] + [get(4 + s, b) for s in range(3)] * 2
            b_ref[k * 8 + b, :, :128] = jnp.concatenate(r2_rows + [get(12, b)], 0).astype(BF16)
            if rho_ref is not None:
                vx_rows = [get(11, b), get(8, b), get(9, b)] + [get(7 + s, b) for s in range(3)] * 2
                b_ref[k * 8 + b, :, 128:] = jnp.concatenate(vx_rows + [get(13, b)], 0).astype(BF16)


def store_features(rows_ref, out_ref, k, features, rows, first):
    at = first
    for f in features:
        for piece in split3(f):
            rows_ref[pl.ds(at * 8, 8), :] = piece
            at += 1
    return at


def gather_features(rows_ref, out_ref, k, rows):
    for b in range(8):
        out_ref[k * 8 + b] = rows_ref[pl.ds(b, rows, stride=8), :].astype(BF16)


def hi_lo(x):
    hi = x.astype(BF16)
    return hi, (x - hi.astype(F32)).astype(BF16)


def falloff_cubed(s2):
    q = jnp.maximum(1.0 - s2 * lax.rsqrt(s2), 0.0)
    return q * q * q


def pipeline(n, one, two, three):
    one(0, 0)
    one(1, 1)
    two(0, 0)

    def step(s, carry):
        t = 2 * s
        last = n - 1
        three(t, 0)
        two(t + 1, 1)
        one(jnp.minimum(t + 2, last), 0)
        three(t + 1, 1)
        two(jnp.minimum(t + 2, last), 0)
        one(jnp.minimum(t + 3, last), 1)
        return carry

    lax.fori_loop(0, n // 2, step, 0)


def moment_kernel(n_ref, tab, corner_ref, state, corr, a_ref, b_ref, f_ref, rows_ref, r_ref, c_ref, acc, sums):
    corner = [corner_ref[d] for d in range(3)]
    n = n_ref[0]

    def prepare(k, with_targets):
        pair_rows(state, corner, k, with_targets, rows_ref, a_ref, b_ref, None)
        blk = pl.ds(pl.multiple_of(k * 8, 8), 8)
        x = [state[d, blk, :] - corner[d] for d in range(3)]
        vol = state[7, blk, :] / state[6, blk, :]
        vx = [vol * t for t in x]
        features = [vol] + vx + [vx[p] * x[q] for p, q in SYM_PAIRS]
        at = store_features(rows_ref, f_ref, k, features, M1, 0)
        for r in range(at, M1):
            rows_ref[pl.ds(r * 8, 8), :] = jnp.zeros((8, 128), F32)
        gather_features(rows_ref, f_ref, k, M1)

    def first(k, carry):
        prepare(k, True)
        return carry

    def rest(k, carry):
        prepare(k, False)
        return carry

    lax.fori_loop(0, LOCAL // 8, first, 0)
    lax.fori_loop(LOCAL // 8, TOTAL // 8, rest, 0)
    acc[...] = jnp.zeros_like(acc)

    def one(t, p):
        i = tab[t * 10]
        lhs = jnp.concatenate([a_ref[tab[t * 10 + 1 + e]] for e in range(NB)], 0)
        r_ref[p] = jnp.dot(lhs, b_ref[i], preferred_element_type=F32)

    def two(t, p):
        for e in range(NB):
            rows = pl.ds(e * 128, 128)
            c = falloff_cubed(jnp.maximum(r_ref[p, rows, :], TINY))
            hi, lo = hi_lo(c)
            c_ref[p, rows, :128] = hi
            c_ref[p, rows, 128:] = lo

    def three(t, p):
        i = tab[t * 10]
        lhs = jnp.concatenate([f_ref[tab[t * 10 + 1 + e]] for e in range(NB)], 1)
        acc[i] += jnp.dot(lhs, c_ref[p], preferred_element_type=F32)

    pipeline(n, one, two, three)

    def collect(i, carry):
        both = acc[i, :, :128] + acc[i, :, 128:]
        sums[pl.ds(i, M1, stride=LOCAL), :] = both
        return carry

    lax.fori_loop(0, LOCAL, collect, 0)

    def finish(k, carry):
        blk = pl.ds(pl.multiple_of(k * 8, 8), 8)
        x = [state[d, blk, :] - corner[d] for d in range(3)]

        def total(f):
            at = [sums[pl.ds(pl.multiple_of((3 * f + s) * LOCAL + k * 8, 8), 8), :] for s in range(3)]
            return at[0] + (at[1] + at[2])

        t0 = total(0)
        t1 = [total(1 + d) for d in range(3)]
        mom = []
        for e, (p, q) in enumerate(SYM_PAIRS):
            value = (x[p] * t0 - t1[p]) * x[q] + (total(4 + e) - x[p] * t1[q])
            mom.append(KERNEL_GRAD * value)
        a, d, f = (mom[e] + REGULAR for e in range(3))
        b, c, e = mom[3:]
        cof_xx = d * f - e * e
        cof_xy = c * e - b * f
        cof_xz = b * e - c * d
        cof_yy = a * f - c * c
        cof_yz = b * c - a * e
        cof_zz = a * d - b * b
        scale = 1.0 / (a * cof_xx + b * cof_xy + c * cof_xz)
        for r, cof in enumerate((cof_xx, cof_yy, cof_zz, cof_xy, cof_xz, cof_yz)):
            corr[r, blk, :] = cof * scale
        return carry

    lax.fori_loop(0, LOCAL // 8, finish, 0)


def rate_kernel(n_ref, tab, corner_ref, state, corr, rate, a_ref, b_ref, rho_ref, f_ref, rows_ref, r_ref, c_ref, w_ref,
                acc, accw, sums, sumsw):
    corner = [corner_ref[d] for d in range(3)]
    n = n_ref[0]

    def pressure(rho):
        r2 = rho * rho
        return STIFFNESS * (r2 * r2 * r2 * rho - 1.0) / r2

    def times(sym, vec):
        return [sym[SYM_INDEX[p][0]] * vec[0] + sym[SYM_INDEX[p][1]] * vec[1] + sym[SYM_INDEX[p][2]] * vec[2]
                for p in range(3)]

    def prepare(k, with_targets):
        pair_rows(state, corner, k, with_targets, rows_ref, a_ref, b_ref, rho_ref)
        blk = pl.ds(pl.multiple_of(k * 8, 8), 8)
        x = [state[d, blk, :] - corner[d] for d in range(3)]
        v = [state[3 + d, blk, :] for d in range(3)]
        rho = state[6, blk, :]
        m = state[7, blk, :]
        sym = [corr[r, blk, :] for r in range(6)]
        m_sym = [m * t for t in sym]
        m_sym_x = times(m_sym, x)
        m_sym_v = times(m_sym, v)
        prs = pressure(rho)
        mp = m * prs
        mv = [m * t for t in v]
        shared = [m] + [m * t for t in x] + m_sym + m_sym_x
        own = (mv + [mv[p] * x[q] for p in range(3) for q in range(3)] + m_sym_v
               + [v[0] * m_sym_x[0] + v[1] * m_sym_x[1] + v[2] * m_sym_x[2]]
               + [mp] + [mp * t for t in x] + [prs * t for t in m_sym] + [prs * t for t in m_sym_x])
        at = store_features(rows_ref, f_ref, k, shared, M2, 0)
        for r in range(at, W_ROWS):
            rows_ref[pl.ds(r * 8, 8), :] = jnp.zeros((8, 128), F32)
        at = store_features(rows_ref, f_ref, k, own, M2, W_ROWS)
        for r in range(at, M2):
            rows_ref[pl.ds(r * 8, 8), :] = jnp.zeros((8, 128), F32)
        gather_features(rows_ref, f_ref, k, M2)

    def first(k, carry):
        prepare(k, True)
        return carry

    def rest(k, carry):
        prepare(k, False)
        return carry

    lax.fori_loop(0, LOCAL // 8, first, 0)
    lax.fori_loop(LOCAL // 8, TOTAL // 8, rest, 0)
    acc[...] = jnp.zeros_like(acc)
    accw[...] = jnp.zeros_like(accw)

    def one(t, p):
        i = tab[t * 10]
        lhs = jnp.concatenate([a_ref[tab[t * 10 + 1 + e]] for e in range(NB)], 0)
        r_ref[p] = jnp.dot(lhs, b_ref[i], preferred_element_type=F32)

    def two(t, p):
        i = tab[t * 10]
        k8 = pl.multiple_of((i // 8) * 8, 8)
        rho_i = state[6, pl.ds(i, 1), :]
        for e in range(NB):
            j = tab[t * 10 + 1 + e]
            rows = pl.ds(e * 128, 128)
            s2 = jnp.maximum(r_ref[p, rows, :128], TINY)
            c = falloff_cubed(s2)
            hi, lo = hi_lo(c)
            c_ref[p, rows, :128] = hi
            c_ref[p, rows, 128:] = lo
            bottom = (s2 + 0.25 * SOFTEN) * (rho_ref[j] + rho_i)
            w = c * jnp.minimum(r_ref[p, rows, 128:], 0.0) * pltpu.reciprocal(bottom)
            hi, lo = hi_lo(w)
            w_ref[p, rows, :128] = hi
            w_ref[p, rows, 128:] = lo

    def three(t, p):
        i = tab[t * 10]
        lhs = jnp.concatenate([f_ref[tab[t * 10 + 1 + e]] for e in range(NB)], 1)
        acc[i] += jnp.dot(lhs, c_ref[p], preferred_element_type=F32)
        accw[i] += jnp.dot(lhs[:MW], w_ref[p], preferred_element_type=F32)

    pipeline(n, one, two, three)

    def collect(i, carry):
        sums[pl.ds(i, M2, stride=LOCAL), :] = acc[i, :, :128] + acc[i, :, 128:]
        sumsw[pl.ds(i, MW, stride=LOCAL), :] = accw[i, :, :128] + accw[i, :, 128:]
        return carry

    lax.fori_loop(0, LOCAL, collect, 0)

    def finish(k, carry):
        blk = pl.ds(pl.multiple_of(k * 8, 8), 8)
        x = [state[d, blk, :] - corner[d] for d in range(3)]
        v = [state[3 + d, blk, :] for d in range(3)]
        prs = pressure(state[6, blk, :])
        sym = [corr[r, blk, :] for r in range(6)]

        def total(ref, first_row, f):
            at = [ref[pl.ds(pl.multiple_of((first_row + 3 * f + s) * LOCAL + k * 8, 8), 8), :] for s in range(3)]
            return at[0] + (at[1] + at[2])

        shared = [total(sums, 0, f) for f in range(13)]
        own = [total(sums, W_ROWS, f) for f in range(29)]
        visc = [total(sumsw, 0, f) for f in range(13)]
        m0, mx, mk, mkx = shared[0], shared[1:4], shared[4:10], shared[10:13]
        mv, mvx, mkv, mvkx = own[0:3], own[3:12], own[12:15], own[15]
        p0, px, pk, pkx = own[16], own[17:20], own[20:26], own[26:29]
        w0, wx, wk, wkx = visc[0], visc[1:4], visc[4:10], visc[10:13]
        vx = [[v[p] * (x[q] * m0 - mx[q]) - (mv[p] * x[q] - mvx[3 * p + q]) for q in range(3)] for p in range(3)]
        inner = jnp.zeros_like(m0)
        for p in range(3):
            for q in range(3):
                inner = inner + sym[SYM_INDEX[p][q]] * vx[p][q]
        mk_x = times(mk, x)
        for p in range(3):
            inner = inner + v[p] * (mk_x[p] - mkx[p]) - x[p] * mkv[p]
        inner = inner + mvkx
        rate[0, blk, :] = (-0.5 * KERNEL_GRAD) * inner
        near = [prs * (x[p] * m0 - mx[p]) + (x[p] * p0 - px[p]) - 0.25 * (x[p] * w0 - wx[p]) for p in range(3)]
        mine = times(sym, near)
        pk_x = times(pk, x)
        wk_x = times(wk, x)
        for p in range(3):
            far = prs * (mk_x[p] - mkx[p]) + (pk_x[p] - pkx[p]) - 0.25 * (wk_x[p] - wkx[p])
            rate[1 + p, blk, :] = (0.5 * KERNEL_GRAD) * (mine[p] + far)
        return carry

    lax.fori_loop(0, LOCAL // 8, finish, 0)


VMEM = pl.BlockSpec(memory_space=pltpu.VMEM)
SMEM = pl.BlockSpec(memory_space=pltpu.SMEM)
ALL_COLUMNS = tuple((a, b) for a in range(1, 5) for b in range(1, 5))


def run_moments(n, table, corner, state):
    return pl.pallas_call(
        moment_kernel,
        out_shape=jax.ShapeDtypeStruct((6, LOCAL, 128), F32),
        in_specs=[SMEM, SMEM, SMEM, VMEM],
        out_specs=VMEM,
        scratch_shapes=[
            pltpu.VMEM((TOTAL, 128, KA), BF16),
            pltpu.VMEM((LOCAL, KA, 128), BF16),
            pltpu.VMEM((TOTAL, M1, 128), BF16),
            pltpu.VMEM((14 * 64, 128), F32),
            pltpu.VMEM((2, NB * 128, 128), F32),
            pltpu.VMEM((2, NB * 128, 256), BF16),
            pltpu.VMEM((LOCAL, M1, 256), F32),
            pltpu.VMEM((M1 * LOCAL, 128), F32),
        ],
        compiler_params=pltpu.CompilerParams(vmem_limit_bytes=56 * 2**20),
        name="moments",
    )(n, table, corner, state)


def run_rates(n, table, corner, state, corr):
    return pl.pallas_call(
        rate_kernel,
        out_shape=jax.ShapeDtypeStruct((4, LOCAL, 128), F32),
        in_specs=[SMEM, SMEM, SMEM, VMEM, VMEM],
        out_specs=VMEM,
        scratch_shapes=[
            pltpu.VMEM((TOTAL, 128, KA), BF16),
            pltpu.VMEM((LOCAL, KA, 256), BF16),
            pltpu.VMEM((TOTAL, 128, 128), F32),
            pltpu.VMEM((TOTAL, M2, 128), BF16),
            pltpu.VMEM((M2 * 8, 128), F32),
            pltpu.VMEM((2, NB * 128, 256), F32),
            pltpu.VMEM((2, NB * 128, 256), BF16),
            pltpu.VMEM((2, NB * 128, 256), BF16),
            pltpu.VMEM((LOCAL, M2, 256), F32),
            pltpu.VMEM((LOCAL, MW, 256), F32),
            pltpu.VMEM((M2 * LOCAL, 128), F32),
            pltpu.VMEM((MW * LOCAL, 128), F32),
        ],
        compiler_params=pltpu.CompilerParams(vmem_limit_bytes=60 * 2**20),
        name="rates",
    )(n, table, corner, state, corr)


def shifted(value, axis, steps):
    count = lax.axis_size(axis)
    first, last = (max(0, -steps), min(count, count - steps))
    return lax.ppermute(value, axis, [(source, source + steps) for source in range(first, last)])


def with_halo(blocks):
    ch = blocks.shape[0]
    low_y = shifted(blocks[:, :, -1:], "gy", 1)
    high_y = shifted(blocks[:, :, :1], "gy", -1)

    def row(a):
        return jnp.concatenate([low_y[:, a:a + 1], blocks[:, a:a + 1], high_y[:, a:a + 1]], 2)

    low_x = shifted(row(3), "gx", 1)
    high_x = shifted(row(0), "gx", -1)
    return jnp.concatenate([t.reshape(ch, -1, 128) for t in (blocks, low_y, high_y, low_x, high_x)], 1)


def occupied_levels(mass):
    any_live = jnp.max(mass.reshape(TOTAL // 4, 4, 128), axis=(0, 2)) > 0.0
    return jnp.max(jnp.where(any_live, jnp.arange(1, 5, dtype=jnp.int32), 1))


def body(positions, velocity, density, masses, counts):
    shape = density.shape
    live = lax.broadcasted_iota(jnp.int32, shape, 3) < counts[..., None]
    blocks = jnp.concatenate(
        [
            jnp.where(live, positions, 0.0),
            jnp.where(live, velocity, 0.0),
            jnp.where(live, density, 1.0)[None],
            jnp.where(live, masses, 0.0)[None],
        ],
        0,
    )
    state = with_halo(blocks)
    state = state.at[6].set(jnp.where(state[6] > 0.0, state[6], 1.0))
    centre_x = (lax.axis_index("gx") * 8 + 4).astype(F32)
    centre_y = (lax.axis_index("gy") * 8 + 4).astype(F32)
    corner = jnp.stack([centre_x, centre_y, jnp.float32(4.0)])
    table = jnp.asarray(item_table(ALL_COLUMNS))
    n = ((3 * occupied_levels(state[7]) - 2) * 16).reshape(1)
    corr = run_moments(n, table, corner, state)
    corr_all = with_halo(corr.reshape((6,) + shape))
    rates = run_rates(n, table, corner, state, corr_all).reshape((4,) + shape)
    density_rate = jnp.where(live, rates[0], 0.0)
    pull = jnp.asarray([0.0, 0.0, -GRAVITY], F32).reshape(3, 1, 1, 1, 1)
    acceleration = jnp.where(live, rates[1:4] + pull, 0.0)
    return (density_rate, acceleration)


def solution(mesh):
    return jax.shard_map(
        body,
        mesh=mesh,
        in_specs=(
            P(None, "gx", "gy", None, None),
            P(None, "gx", "gy", None, None),
            P("gx", "gy", None, None),
            P("gx", "gy", None, None),
            P("gx", "gy", None),
        ),
        out_specs=(P("gx", "gy", None, None), P(None, "gx", "gy", None, None)),
        check_vma=False,
    )
```

time: 1250 us -> 226 us (0.18)
  other arithmetic: 692 us -> 5.68 us
  loops' own time: 270 us -> 0 us
  local copies, waits for them, and re-layouts: 203 us -> 3.45 us
  Pallas kernels: 0 us -> 165 us
  starting transfers between devices: 50.8 us -> 34.4 us
    reduce_sum x256 -> x0, other arithmetic: 331 us -> none  [the longest x64 128 us: tensor_pair(): side_i.append(jnp.sum(weight_i * outer, axis=(0, 2)))]
    another operation x2 -> x0, loops' own time: 270 us -> none  [sweep_blocks(): lax.scan(block_step, start, (targets, partners, occupied))]
    pallas_call x0 -> x2, Pallas kernels: none -> 165 us  [the longest x1 115 us: run_rates(): pl.pallas_call(rate_kernel, out_shape=jax.ShapeDtypeStruct((4, LOCAL, 128...]
    scatter-add x134 -> x0, other arithmetic: 134 us -> none  [the longest x128 134 us: block_step(): totals = totals.at[partner_ids].add(far_side * credit[:, None, None])]
    add x67 -> x0, other arithmetic: 120 us -> none  [the longest x64 120 us: motion_pair(): vel_diff[:, 0] * grads[0] + vel_diff[:, 1] * grads[1]]
    gather x192 -> x0, local copies, waits for them, and re-layouts: 108 us -> none  [block_step(): partner = tuple((source[partner_ids] for source in sources))]
    select_n x128 -> x4, other arithmetic: 89.7 us -> 3.23 us  [the longest x1 0.95 us: body(): jnp.where(live, positions, 0.0)]
    dynamic_slice x192 -> x0, local copies, waits for them, and re-layouts: 75.9 us -> none  [the longest x128 75.2 us: sweep_blocks(): lax.scan(block_step, start, (targets, partners, occupied))]
  transfers between devices with their start and end apart: 12 -> 8, of which waited for: 9 -> 6; matrix products, arithmetic and copies ran while one was open for 0% -> 0% of each run, Pallas kernels for 0% -> 0%
where the time goes in v1:
time: 226 us; the launch traced here: 222 us
  Pallas kernels  165 us (73%)
  starting transfers between devices  34.4 us (15%)
  waiting for transfers between devices  11.4 us (5%)
  other arithmetic  5.68 us (3%)
  local copies, waits for them, and re-layouts  3.45 us (2%)
    pallas_call x1, Pallas kernels, run_rates(): pl.pallas_call(rate_kernel, out_shape=jax.ShapeDtypeStruct((4, LOCAL, 128...  115 us
    pallas_call x1, Pallas kernels, run_moments(): pl.pallas_call(moment_kernel, out_shape=jax.ShapeDtypeStruct((6, LOCAL, 1...  50.9 us
    ppermute x8, starting transfers between devices, shifted(): lax.ppermute(value, axis, [(source, source + steps) for source in range(f...  34.4 us
    ppermute x8, waiting for transfers between devices, shifted(): lax.ppermute(value, axis, [(source, source + steps) for source in range(f...  11.4 us
  transfers between devices with their start and end apart: 8, of which 6 were waited for; matrix products, arithmetic and copies ran while one was open for 0% of the time, Pallas kernels for 0%

profile of v1, /device:TPU:6, one launch (start us, length us, event | category | flops | bytes accessed | tf_op | source)
XLA Modules:
  0.0 222.0 jit_solution(16157056217957989342)
XLA Ops:
  0.6 0.0 copy-start.4
  0.6 0.0 copy-start.3
  0.6 0.8 iota_compare_fusion
  1.5 0.0 copy-done.4
  1.5 0.9 broadcast_select_fusion.4
  2.4 0.0 copy-done.3
  2.4 0.9 broadcast_select_fusion.1
  3.3 0.1 pad_maximum_fusion
  3.4 6.2 %collective-permute-start.1 = (f32[8,4,1,4,128]{4,3,2,1,0:T(4,128)S(1)}, f32[8,4,1,4,128]{4,3,2,1,0:T(4,128)S(1)}, u32[]{:S(2)}, u32[]{:S(2)}) collective-permute-start(f32[8,4,1,4,128]{4,3,2,1,0:T(4,128)S(1)} %get-tuple-element.16), channel_id=1, source_target_pairs={{1,0},{2,1},{3,2},{4,3},{5,4},{6,5},{7,6},{9,8},{10,9},{11,10},{12... | collective-permute-start | bytes 196616 | tf_op jit(solution)/shard_map/ppermute | solution.py:433
  9.7 1.9 collective-permute-start
  11.6 0.7 pad_maximum_fusion.5.corner_ref
  12.3 0.0 collective-permute-done.1
  12.3 5.6 %collective-permute-done = f32[8,4,1,4,128]{4,3,2,1,0:T(4,128)S(1)} collective-permute-done((f32[8,4,1,4,128]{4,3,2,1,0:T(4,128)S(1)}, f32[8,4,1,4,128]{4,3,2,1,0:T(4,128)S(1)}, u32[]{:S(2)}, u32[]{:S(2)}) %collective-permute-start) | collective-permute-done | bytes 65568 | tf_op jit(solution)/shard_map/ppermute | solution.py:433
  18.0 1.9 collective-permute-start.2
  19.9 7.3 %collective-permute-start.3 = (f32[8,1,6,4,128]{4,3,2,1,0:T(4,128)S(1)}, f32[8,1,6,4,128]{4,3,2,1,0:T(4,128)S(1)}, u32[]{:S(2)}, u32[]{:S(2)}) collective-permute-start(f32[8,1,6,4,128]{4,3,2,1,0:T(4,128)S(1)} %pad_maximum_fusion.2), channel_id=1, source_target_pairs={{8,0},{16,8},{24,16},{32,24},{40,32},{48,40},{56,48},{64,56},{72,6... | collective-permute-start | bytes 294920 | tf_op jit(solution)/shard_map/ppermute | solution.py:433
  27.2 0.3 collective-permute-done.2
  27.5 1.9 collective-permute-done.3
  29.4 0.0 copy-start
  29.4 0.1 slice_reduce_fusion
  29.5 0.1 reduce_max.26
  29.7 0.6 fusion.1
  30.9 0.0 copy-done
  31.0 50.9 %moments.1 = f32[6,64,128]{2,1,0:T(8,128)} custom-call(s32[1]{0:T(128)} %bitcast.10.n_ref, s32[1600]{0:T(1024)} %constant.68.clone.tab, f32[3]{0:T(128)} %pad_maximum_fusion.5.corner_ref, f32[8,144,128]{2,1,0:T(8,128)} %copy-done), custom_call_target="tpu_custom_call" | custom-call | tf_op jit(solution)/shard_map/moments/pallas_call | solution.py:385
  81.8 0.0 copy-start.1
  81.8 0.9 fusion.4
  82.7 0.1 copy-done.1
  82.8 1.9 collective-permute-start.4
  84.8 6.0 %collective-permute-start.5 = (f32[6,4,1,4,128]{4,3,2,0,1:T(4,128)S(1)}, f32[6,4,1,4,128]{4,3,2,0,1:T(4,128)S(1)}, u32[]{:S(2)}, u32[]{:S(2)}) collective-permute-start(f32[6,4,1,4,128]{4,3,2,0,1:T(4,128)S(1)} %copy.22), channel_id=1, source_target_pairs={{1,0},{2,1},{3,2},{4,3},{5,4},{6,5},{7,6},{9,8},{10,9},{11,10},{12... | collective-permute-start | bytes 147464 | tf_op jit(solution)/shard_map/ppermute | solution.py:433
  90.9 0.1 collective-permute-done.4
  90.9 1.6 collective-permute-done.5
  92.6 1.9 collective-permute-start.6
  94.6 7.3 %collective-permute-start.7 = (f32[6,1,6,4,128]{4,3,2,0,1:T(4,128)S(1)}, f32[6,1,6,4,128]{4,3,2,0,1:T(4,128)S(1)}, u32[]{:S(2)}, u32[]{:S(2)}) collective-permute-start(f32[6,1,6,4,128]{4,3,2,0,1:T(4,128)S(1)} %pad_maximum_fusion.4), channel_id=1, source_target_pairs={{8,0},{16,8},{24,16},{32,24},{40,32},{48,40},{56,48},{64,56},{72,6... | collective-permute-start | bytes 221192 | tf_op jit(solution)/shard_map/ppermute | solution.py:433
  101.9 0.0 collective-permute-done.6
  101.9 1.9 collective-permute-done.7
  103.8 0.0 copy-start.2
  103.8 0.8 copy-done.2
  104.6 114.6 %rates.1 = f32[4,64,128]{2,1,0:T(8,128)} custom-call(s32[1]{0:T(128)} %bitcast.10.n_ref, s32[1600]{0:T(1024)} %constant.68.clone.tab, f32[3]{0:T(128)} %pad_maximum_fusion.5.corner_ref, f32[8,144,128]{2,1,0:T(8,128)} %copy-done, f32[6,144,128]{2,1,0:T(8,128)} %copy-done.2), custom_call_target="tpu_custom_call" | custom-call | tf_op jit(solution)/shard_map/rates/pallas_call | solution.py:406
  219.1 0.0 slice-start
  219.1 0.0 slice-start.1
  219.1 0.8 slice-done
  219.9 0.7 broadcast_select_fusion.2
  220.6 0.0 copy-start.5
  220.6 0.0 slice-done.1
  220.6 0.7 copy-done.5
  221.3 0.7 add_select_fusion
  (27 shorter events, 0.3 us)
Async XLA Ops:
  0.6 0.9 copy-start.4
  0.6 1.7 copy-start.3
  3.4 8.9 %collective-permute-start.1 = (f32[8,4,1,4,128]{4,3,2,1,0:T(4,128)S(1)}, f32[8,4,1,4,128]{4,3,2,1,0:T(4,128)S(1)}, u32[]{:S(2)}, u32[]{:S(2)}) collective-permute-start(f32[8,4,1,4,128]{4,3,2,1,0:T(4,128)S(1)} %get-tuple-element.16), channel_id=1, source_target_pairs={{1,0},{2,1},{3,2},{4,3},{5,4},{6,5},{7,6},{9,8},{10,9},{11,10},{12... | collective-permute-start | bytes 196616 | tf_op jit(solution)/shard_map/ppermute | solution.py:433
  9.7 8.3 %collective-permute-start = (f32[8,4,1,4,128]{4,3,2,1,0:T(4,128)S(1)}, f32[8,4,1,4,128]{4,3,2,1,0:T(4,128)S(1)}, u32[]{:S(2)}, u32[]{:S(2)}) collective-permute-start(f32[8,4,1,4,128]{4,3,2,1,0:T(4,128)S(1)} %get-tuple-element.17), channel_id=1, source_target_pairs={{0,1},{1,2},{2,3},{3,4},{4,5},{5,6},{6,7},{8,9},{9,10},{10,11},{11... | collective-permute-start | bytes 196616 | tf_op jit(solution)/shard_map/ppermute | solution.py:433
  18.0 9.5 %collective-permute-start.2 = (f32[8,1,6,4,128]{4,3,2,1,0:T(4,128)S(1)}, f32[8,1,6,4,128]{4,3,2,1,0:T(4,128)S(1)}, u32[]{:S(2)}, u32[]{:S(2)}) collective-permute-start(f32[8,1,6,4,128]{4,3,2,1,0:T(4,128)S(1)} %pad_maximum_fusion.1), channel_id=1, source_target_pairs={{0,8},{8,16},{16,24},{24,32},{32,40},{40,48},{48,56},{56,64},{64,7... | collective-permute-start | bytes 294920 | tf_op jit(solution)/shard_map/ppermute | solution.py:433
  19.9 9.5 %collective-permute-start.3 = (f32[8,1,6,4,128]{4,3,2,1,0:T(4,128)S(1)}, f32[8,1,6,4,128]{4,3,2,1,0:T(4,128)S(1)}, u32[]{:S(2)}, u32[]{:S(2)}) collective-permute-start(f32[8,1,6,4,128]{4,3,2,1,0:T(4,128)S(1)} %pad_maximum_fusion.2), channel_id=1, source_target_pairs={{8,0},{16,8},{24,16},{32,24},{40,32},{48,40},{56,48},{64,56},{72,6... | collective-permute-start | bytes 294920 | tf_op jit(solution)/shard_map/ppermute | solution.py:433
  29.4 1.6 copy-start
  81.8 1.0 copy-start.1
  82.8 8.1 %collective-permute-start.4 = (f32[6,4,1,4,128]{4,3,2,0,1:T(4,128)S(1)}, f32[6,4,1,4,128]{4,3,2,0,1:T(4,128)S(1)}, u32[]{:S(2)}, u32[]{:S(2)}) collective-permute-start(f32[6,4,1,4,128]{4,3,2,0,1:T(4,128)S(1)} %copy.21), channel_id=1, source_target_pairs={{0,1},{1,2},{2,3},{3,4},{4,5},{5,6},{6,7},{8,9},{9,10},{10,11},{11... | collective-permute-start | bytes 147464 | tf_op jit(solution)/shard_map/ppermute | solution.py:433
  84.8 7.8 %collective-permute-start.5 = (f32[6,4,1,4,128]{4,3,2,0,1:T(4,128)S(1)}, f32[6,4,1,4,128]{4,3,2,0,1:T(4,128)S(1)}, u32[]{:S(2)}, u32[]{:S(2)}) collective-permute-start(f32[6,4,1,4,128]{4,3,2,0,1:T(4,128)S(1)} %copy.22), channel_id=1, source_target_pairs={{1,0},{2,1},{3,2},{4,3},{5,4},{6,5},{7,6},{9,8},{10,9},{11,10},{12... | collective-permute-start | bytes 147464 | tf_op jit(solution)/shard_map/ppermute | solution.py:433
  92.6 9.3 %collective-permute-start.6 = (f32[6,1,6,4,128]{4,3,2,0,1:T(4,128)S(1)}, f32[6,1,6,4,128]{4,3,2,0,1:T(4,128)S(1)}, u32[]{:S(2)}, u32[]{:S(2)}) collective-permute-start(f32[6,1,6,4,128]{4,3,2,0,1:T(4,128)S(1)} %pad_maximum_fusion.3), channel_id=1, source_target_pairs={{0,8},{8,16},{16,24},{24,32},{32,40},{40,48},{48,56},{56,64},{64,7... | collective-permute-start | bytes 221192 | tf_op jit(solution)/shard_map/ppermute | solution.py:433
  94.6 9.2 %collective-permute-start.7 = (f32[6,1,6,4,128]{4,3,2,0,1:T(4,128)S(1)}, f32[6,1,6,4,128]{4,3,2,0,1:T(4,128)S(1)}, u32[]{:S(2)}, u32[]{:S(2)}) collective-permute-start(f32[6,1,6,4,128]{4,3,2,0,1:T(4,128)S(1)} %pad_maximum_fusion.4), channel_id=1, source_target_pairs={{8,0},{16,8},{24,16},{32,24},{40,32},{48,40},{56,48},{64,56},{72,6... | collective-permute-start | bytes 221192 | tf_op jit(solution)/shard_map/ppermute | solution.py:433
  103.8 0.8 copy-start.2
  219.1 0.8 slice-start
  219.1 1.5 slice-start.1
  220.6 0.7 copy-start.5

commit v2 on v1

--- a/solution.py
+++ b/solution.py
@@ -60,6 +60,17 @@
     return np.asarray(rows, np.int32).reshape(-1)
 
 
+def spread_matrix():
+    out = np.zeros((32, 256), np.float32)
+    for g in range(9):
+        for r in range(8):
+            out[(g // 3) * 8 + r, g * 8 + r] = 1.0
+    for r in range(8):
+        out[24 + r, 72 + r] = 1.0
+    out[[6, 14, 22], 128:] = 1.0
+    return out
+
+
 def split3(x):
     h = x.astype(BF16).astype(F32)
     r = x - h
@@ -67,7 +78,7 @@
     return h, m, r - m
 
 
-def pair_rows(state, corner, k, with_targets, rows_ref, a_ref, b_ref, rho_ref):
+def pair_rows(state, corner, spread, k, with_targets, rows_ref, a_ref, b_ref, rho_ref):
     blk = pl.ds(pl.multiple_of(k * 8, 8), 8)
     x = [state[d, blk, :] - corner[d] for d in range(3)]
     v = [state[3 + d, blk, :] for d in range(3)]
@@ -101,15 +112,13 @@
         put(11, [-vs[d][0] for d in range(3)] + [-xs[d][0] for d in range(3)] + [zero, xvs[2]])
         put(12, [quarter] * 3 + [zero] * 3 + [0.25 * n2s[0], 0.25 * n2s[1]])
         put(13, [zero] * 3 + [one] * 3 + [xvs[0], xvs[1]])
-    pad = jnp.zeros((128 - KA, 128), F32)
+    cols = [jnp.concatenate([get(s, b) for s in range(4)], 0).T.astype(BF16) for b in range(8)]
+    both = jnp.dot(jnp.concatenate(cols, 0), spread, preferred_element_type=F32)
     for b in range(8):
-        g = [get(s, b) for s in range(4)]
-        rows = jnp.concatenate([g[0]] * 3 + [g[1]] * 3 + [g[2]] * 3 + [g[3], pad], 0)
-        cols = rows.T
-        a_ref[k * 8 + b] = cols[:, :KA].astype(BF16)
+        rows = slice(b * 128, b * 128 + 128)
+        a_ref[k * 8 + b] = both[rows, :KA].astype(BF16)
         if rho_ref is not None:
-            col = cols[:, 6:7] + cols[:, 30:31] + cols[:, 54:55]
-            rho_ref[k * 8 + b] = jnp.broadcast_to(col, (128, 128))
+            rho_ref[k * 8 + b] = both[rows, 128:]
         if with_targets:
             r2_rows = [get(10, b), get(5, b), get(6, b)] + [get(4 + s, b) for s in range(3)] * 2
             b_ref[k * 8 + b, :, :128] = jnp.concatenate(r2_rows + [get(12, b)], 0).astype(BF16)
@@ -142,31 +151,30 @@
     return q * q * q
 
 
-def pipeline(n, one, two, three):
+CHUNKS = ((0, 2), (2, 4), (4, 6), (6, 8), (8, 9))
+
+
+def for_items(n, one, rest):
     one(0, 0)
     one(1, 1)
-    two(0, 0)
 
     def step(s, carry):
-        t = 2 * s
-        last = n - 1
-        three(t, 0)
-        two(t + 1, 1)
-        one(jnp.minimum(t + 2, last), 0)
-        three(t + 1, 1)
-        two(jnp.minimum(t + 2, last), 0)
-        one(jnp.minimum(t + 3, last), 1)
-        return carry
-
-    lax.fori_loop(0, n // 2, step, 0)
-
-
-def moment_kernel(n_ref, tab, corner_ref, state, corr, a_ref, b_ref, f_ref, rows_ref, r_ref, c_ref, acc, sums):
+        t = 4 * s
+        for e in range(4):
+            one(jnp.minimum(t + e + 2, n - 1), (e + 2) % 4)
+            rest(t + e, e)
+        return carry
+
+    lax.fori_loop(0, n // 4, step, 0)
+
+
+def moment_kernel(n_ref, tab, corner_ref, spread_ref, state, corr, a_ref, b_ref, f_ref, rows_ref, r_ref, acc):
     corner = [corner_ref[d] for d in range(3)]
     n = n_ref[0]
+    spread = spread_ref[...]
 
     def prepare(k, with_targets):
-        pair_rows(state, corner, k, with_targets, rows_ref, a_ref, b_ref, None)
+        pair_rows(state, corner, spread, k, with_targets, rows_ref, a_ref, b_ref, None)
         blk = pl.ds(pl.multiple_of(k * 8, 8), 8)
         x = [state[d, blk, :] - corner[d] for d in range(3)]
         vol = state[7, blk, :] / state[6, blk, :]
@@ -181,47 +189,39 @@
         prepare(k, True)
         return carry
 
-    def rest(k, carry):
+    def others(k, carry):
         prepare(k, False)
         return carry
 
     lax.fori_loop(0, LOCAL // 8, first, 0)
-    lax.fori_loop(LOCAL // 8, TOTAL // 8, rest, 0)
+    lax.fori_loop(LOCAL // 8, TOTAL // 8, others, 0)
     acc[...] = jnp.zeros_like(acc)
 
     def one(t, p):
+        for c in CHUNKS:
+            lhs = jnp.concatenate([a_ref[tab[t * 10 + 1 + e]] for e in range(*c)], 0)
+            rows = pl.ds(c[0] * 128, (c[1] - c[0]) * 128)
+            r_ref[p, rows, :] = jnp.dot(lhs, b_ref[tab[t * 10]], preferred_element_type=F32)
+
+    def rest(t, p):
         i = tab[t * 10]
-        lhs = jnp.concatenate([a_ref[tab[t * 10 + 1 + e]] for e in range(NB)], 0)
-        r_ref[p] = jnp.dot(lhs, b_ref[i], preferred_element_type=F32)
-
-    def two(t, p):
-        for e in range(NB):
-            rows = pl.ds(e * 128, 128)
-            c = falloff_cubed(jnp.maximum(r_ref[p, rows, :], TINY))
-            hi, lo = hi_lo(c)
-            c_ref[p, rows, :128] = hi
-            c_ref[p, rows, 128:] = lo
-
-    def three(t, p):
-        i = tab[t * 10]
-        lhs = jnp.concatenate([f_ref[tab[t * 10 + 1 + e]] for e in range(NB)], 1)
-        acc[i] += jnp.dot(lhs, c_ref[p], preferred_element_type=F32)
-
-    pipeline(n, one, two, three)
-
-    def collect(i, carry):
-        both = acc[i, :, :128] + acc[i, :, 128:]
-        sums[pl.ds(i, M1, stride=LOCAL), :] = both
-        return carry
-
-    lax.fori_loop(0, LOCAL, collect, 0)
+        partner = [tab[t * 10 + 1 + e] for e in range(NB)]
+        weights = []
+        for c in CHUNKS:
+            s2 = jnp.maximum(r_ref[p, pl.ds(c[0] * 128, (c[1] - c[0]) * 128), :], TINY)
+            weights.append(jnp.concatenate(hi_lo(falloff_cubed(s2)), 1))
+        lhs = jnp.concatenate([f_ref[j] for j in partner], 1)
+        part = jnp.dot(lhs, jnp.concatenate(weights, 0), preferred_element_type=F32)
+        acc[pl.ds(pl.multiple_of(i * M1, M1), M1), :] += part[:, :128] + part[:, 128:]
+
+    for_items(n, one, rest)
 
     def finish(k, carry):
         blk = pl.ds(pl.multiple_of(k * 8, 8), 8)
         x = [state[d, blk, :] - corner[d] for d in range(3)]
 
         def total(f):
-            at = [sums[pl.ds(pl.multiple_of((3 * f + s) * LOCAL + k * 8, 8), 8), :] for s in range(3)]
+            at = [acc[pl.ds(k * (8 * M1) + 3 * f + s, 8, stride=M1), :] for s in range(3)]
             return at[0] + (at[1] + at[2])
 
         t0 = total(0)
@@ -246,10 +246,11 @@
     lax.fori_loop(0, LOCAL // 8, finish, 0)
 
 
-def rate_kernel(n_ref, tab, corner_ref, state, corr, rate, a_ref, b_ref, rho_ref, f_ref, rows_ref, r_ref, c_ref, w_ref,
-                acc, accw, sums, sumsw):
+def rate_kernel(n_ref, tab, corner_ref, spread_ref, state, corr, rate, a_ref, b_ref, rho_ref, f_ref, rows_ref, r_ref, acc,
+                accw):
     corner = [corner_ref[d] for d in range(3)]
     n = n_ref[0]
+    spread = spread_ref[...]
 
     def pressure(rho):
         r2 = rho * rho
@@ -260,7 +261,7 @@
                 for p in range(3)]
 
     def prepare(k, with_targets):
-        pair_rows(state, corner, k, with_targets, rows_ref, a_ref, b_ref, rho_ref)
+        pair_rows(state, corner, spread, k, with_targets, rows_ref, a_ref, b_ref, rho_ref)
         blk = pl.ds(pl.multiple_of(k * 8, 8), 8)
         x = [state[d, blk, :] - corner[d] for d in range(3)]
         v = [state[3 + d, blk, :] for d in range(3)]
@@ -289,52 +290,43 @@
         prepare(k, True)
         return carry
 
-    def rest(k, carry):
+    def others(k, carry):
         prepare(k, False)
         return carry
 
     lax.fori_loop(0, LOCAL // 8, first, 0)
-    lax.fori_loop(LOCAL // 8, TOTAL // 8, rest, 0)
+    lax.fori_loop(LOCAL // 8, TOTAL // 8, others, 0)
     acc[...] = jnp.zeros_like(acc)
     accw[...] = jnp.zeros_like(accw)
 
     def one(t, p):
+        for c in CHUNKS:
+            lhs = jnp.concatenate([a_ref[tab[t * 10 + 1 + e]] for e in range(*c)], 0)
+            rows = pl.ds(c[0] * 128, (c[1] - c[0]) * 128)
+            r_ref[p, rows, :] = jnp.dot(lhs, b_ref[tab[t * 10]], preferred_element_type=F32)
+
+    def rest(t, p):
         i = tab[t * 10]
-        lhs = jnp.concatenate([a_ref[tab[t * 10 + 1 + e]] for e in range(NB)], 0)
-        r_ref[p] = jnp.dot(lhs, b_ref[i], preferred_element_type=F32)
-
-    def two(t, p):
-        i = tab[t * 10]
-        k8 = pl.multiple_of((i // 8) * 8, 8)
+        partner = [tab[t * 10 + 1 + e] for e in range(NB)]
         rho_i = state[6, pl.ds(i, 1), :]
-        for e in range(NB):
-            j = tab[t * 10 + 1 + e]
-            rows = pl.ds(e * 128, 128)
-            s2 = jnp.maximum(r_ref[p, rows, :128], TINY)
-            c = falloff_cubed(s2)
-            hi, lo = hi_lo(c)
-            c_ref[p, rows, :128] = hi
-            c_ref[p, rows, 128:] = lo
-            bottom = (s2 + 0.25 * SOFTEN) * (rho_ref[j] + rho_i)
-            w = c * jnp.minimum(r_ref[p, rows, 128:], 0.0) * pltpu.reciprocal(bottom)
-            hi, lo = hi_lo(w)
-            w_ref[p, rows, :128] = hi
-            w_ref[p, rows, 128:] = lo
-
-    def three(t, p):
-        i = tab[t * 10]
-        lhs = jnp.concatenate([f_ref[tab[t * 10 + 1 + e]] for e in range(NB)], 1)
-        acc[i] += jnp.dot(lhs, c_ref[p], preferred_element_type=F32)
-        accw[i] += jnp.dot(lhs[:MW], w_ref[p], preferred_element_type=F32)
-
-    pipeline(n, one, two, three)
-
-    def collect(i, carry):
-        sums[pl.ds(i, M2, stride=LOCAL), :] = acc[i, :, :128] + acc[i, :, 128:]
-        sumsw[pl.ds(i, MW, stride=LOCAL), :] = accw[i, :, :128] + accw[i, :, 128:]
-        return carry
-
-    lax.fori_loop(0, LOCAL, collect, 0)
+        weights = []
+        viscous = []
+        for c in CHUNKS:
+            both = r_ref[p, pl.ds(c[0] * 128, (c[1] - c[0]) * 128), :]
+            s2 = jnp.maximum(both[:, :128], TINY)
+            fall = falloff_cubed(s2)
+            weights.append(jnp.concatenate(hi_lo(fall), 1))
+            rho_j = jnp.concatenate([rho_ref[partner[e]] for e in range(*c)], 0)
+            bottom = (s2 + 0.25 * SOFTEN) * (rho_j + rho_i)
+            w = fall * jnp.minimum(both[:, 128:], 0.0) * pltpu.reciprocal(bottom)
+            viscous.append(jnp.concatenate(hi_lo(w), 1))
+        lhs = jnp.concatenate([f_ref[j] for j in partner], 1)
+        part = jnp.dot(lhs, jnp.concatenate(weights, 0), preferred_element_type=F32)
+        acc[pl.ds(pl.multiple_of(i * M2, M2), M2), :] += part[:, :128] + part[:, 128:]
+        part = jnp.dot(lhs[:MW], jnp.concatenate(viscous, 0), preferred_element_type=F32)
+        accw[pl.ds(pl.multiple_of(i * MW, MW), MW), :] += part[:, :128] + part[:, 128:]
+
+    for_items(n, one, rest)
 
     def finish(k, carry):
         blk = pl.ds(pl.multiple_of(k * 8, 8), 8)
@@ -343,13 +335,13 @@
         prs = pressure(state[6, blk, :])
         sym = [corr[r, blk, :] for r in range(6)]
 
-        def total(ref, first_row, f):
-            at = [ref[pl.ds(pl.multiple_of((first_row + 3 * f + s) * LOCAL + k * 8, 8), 8), :] for s in range(3)]
+        def total(ref, height, first_row, f):
+            at = [ref[pl.ds(k * (8 * height) + first_row + 3 * f + s, 8, stride=height), :] for s in range(3)]
             return at[0] + (at[1] + at[2])
 
-        shared = [total(sums, 0, f) for f in range(13)]
-        own = [total(sums, W_ROWS, f) for f in range(29)]
-        visc = [total(sumsw, 0, f) for f in range(13)]
+        shared = [total(acc, M2, 0, f) for f in range(13)]
+        own = [total(acc, M2, W_ROWS, f) for f in range(29)]
+        visc = [total(accw, MW, 0, f) for f in range(13)]
         m0, mx, mk, mkx = shared[0], shared[1:4], shared[4:10], shared[10:13]
         mv, mvx, mkv, mvkx = own[0:3], own[3:12], own[12:15], own[15]
         p0, px, pk, pkx = own[16], own[17:20], own[20:26], own[26:29]
@@ -385,28 +377,26 @@
     return pl.pallas_call(
         moment_kernel,
         out_shape=jax.ShapeDtypeStruct((6, LOCAL, 128), F32),
-        in_specs=[SMEM, SMEM, SMEM, VMEM],
+        in_specs=[SMEM, SMEM, SMEM, VMEM, VMEM],
         out_specs=VMEM,
         scratch_shapes=[
             pltpu.VMEM((TOTAL, 128, KA), BF16),
             pltpu.VMEM((LOCAL, KA, 128), BF16),
             pltpu.VMEM((TOTAL, M1, 128), BF16),
             pltpu.VMEM((14 * 64, 128), F32),
-            pltpu.VMEM((2, NB * 128, 128), F32),
-            pltpu.VMEM((2, NB * 128, 256), BF16),
-            pltpu.VMEM((LOCAL, M1, 256), F32),
-            pltpu.VMEM((M1 * LOCAL, 128), F32),
+            pltpu.VMEM((4, NB * 128, 128), F32),
+            pltpu.VMEM((LOCAL * M1, 128), F32),
         ],
         compiler_params=pltpu.CompilerParams(vmem_limit_bytes=56 * 2**20),
         name="moments",
-    )(n, table, corner, state)
+    )(n, table, corner, jnp.asarray(spread_matrix(), BF16), state)
 
 
 def run_rates(n, table, corner, state, corr):
     return pl.pallas_call(
         rate_kernel,
         out_shape=jax.ShapeDtypeStruct((4, LOCAL, 128), F32),
-        in_specs=[SMEM, SMEM, SMEM, VMEM, VMEM],
+        in_specs=[SMEM, SMEM, SMEM, VMEM, VMEM, VMEM],
         out_specs=VMEM,
         scratch_shapes=[
             pltpu.VMEM((TOTAL, 128, KA), BF16),
@@ -414,17 +404,13 @@
             pltpu.VMEM((TOTAL, 128, 128), F32),
             pltpu.VMEM((TOTAL, M2, 128), BF16),
             pltpu.VMEM((M2 * 8, 128), F32),
-            pltpu.VMEM((2, NB * 128, 256), F32),
-            pltpu.VMEM((2, NB * 128, 256), BF16),
-            pltpu.VMEM((2, NB * 128, 256), BF16),
-            pltpu.VMEM((LOCAL, M2, 256), F32),
-            pltpu.VMEM((LOCAL, MW, 256), F32),
-            pltpu.VMEM((M2 * LOCAL, 128), F32),
-            pltpu.VMEM((MW * LOCAL, 128), F32),
+            pltpu.VMEM((4, NB * 128, 256), F32),
+            pltpu.VMEM((LOCAL * M2, 128), F32),
+            pltpu.VMEM((LOCAL * MW, 128), F32),
         ],
         compiler_params=pltpu.CompilerParams(vmem_limit_bytes=60 * 2**20),
         name="rates",
-    )(n, table, corner, state, corr)
+    )(n, table, corner, jnp.asarray(spread_matrix(), BF16), state, corr)
 
 
 def shifted(value, axis, steps):

time: 226 us -> 168 us (0.74)
  the two profiles are of different devices: /device:TPU:6 before, /device:TPU:121 now
where the time goes in v2:
time: 168 us; the launch traced here: 167 us
  Pallas kernels  108 us (64%)
  starting transfers between devices  28.5 us (17%)
  waiting for transfers between devices  20.4 us (12%)
  other arithmetic  5.68 us (3%)
  local copies, waits for them, and re-layouts  3.45 us (2%)
    pallas_call x1, Pallas kernels, run_rates(): pl.pallas_call(rate_kernel, out_shape=jax.ShapeDtypeStruct((4, LOCAL, 128...  68.6 us
    pallas_call x1, Pallas kernels, run_moments(): pl.pallas_call(moment_kernel, out_shape=jax.ShapeDtypeStruct((6, LOCAL, 1...  39.1 us
    ppermute x8, starting transfers between devices, shifted(): lax.ppermute(value, axis, [(source, source + steps) for source in range(f...  28.5 us
    ppermute x8, waiting for transfers between devices, shifted(): lax.ppermute(value, axis, [(source, source + steps) for source in range(f...  20.4 us
  transfers between devices with their start and end apart: 8, of which 4 were waited for; matrix products, arithmetic and copies ran while one was open for 0% of the time, Pallas kernels for 0%

profile of v2, /device:TPU:121, one launch (start us, length us, event | category | flops | bytes accessed | tf_op | source)
XLA Modules:
  0.0 167.3 jit_solution(13591633459108984354)
XLA Ops:
  0.6 0.0 copy-start.4
  0.6 0.0 copy-start.3
  0.6 0.8 iota_compare_fusion
  1.5 0.0 copy-done.4
  1.5 0.9 broadcast_select_fusion.4
  2.4 0.0 copy-done.3
  2.4 0.9 broadcast_select_fusion.1
  3.3 0.1 pad_maximum_fusion
  3.4 2.0 %collective-permute-start.1 = (f32[8,4,1,4,128]{4,3,2,1,0:T(4,128)S(1)}, f32[8,4,1,4,128]{4,3,2,1,0:T(4,128)S(1)}, u32[]{:S(2)}, u32[]{:S(2)}) collective-permute-start(f32[8,4,1,4,128]{4,3,2,1,0:T(4,128)S(1)} %get-tuple-element.16), channel_id=1, source_target_pairs={{1,0},{2,1},{3,2},{4,3},{5,4},{6,5},{7,6},{9,8},{10,9},{11,10},{12... | collective-permute-start | bytes 196616 | tf_op jit(solution)/shard_map/ppermute | solution.py:419
  5.5 5.4 %collective-permute-start = (f32[8,4,1,4,128]{4,3,2,1,0:T(4,128)S(1)}, f32[8,4,1,4,128]{4,3,2,1,0:T(4,128)S(1)}, u32[]{:S(2)}, u32[]{:S(2)}) collective-permute-start(f32[8,4,1,4,128]{4,3,2,1,0:T(4,128)S(1)} %get-tuple-element.17), channel_id=1, source_target_pairs={{0,1},{1,2},{2,3},{3,4},{4,5},{5,6},{6,7},{8,9},{9,10},{10,11},{11... | collective-permute-start | bytes 196616 | tf_op jit(solution)/shard_map/ppermute | solution.py:419
  10.9 0.7 pad_maximum_fusion.5.corner_ref
  11.6 0.0 collective-permute-done.1
  11.6 0.6 collective-permute-done
  12.2 6.0 %collective-permute-start.2 = (f32[8,1,6,4,128]{4,3,2,1,0:T(4,128)S(1)}, f32[8,1,6,4,128]{4,3,2,1,0:T(4,128)S(1)}, u32[]{:S(2)}, u32[]{:S(2)}) collective-permute-start(f32[8,1,6,4,128]{4,3,2,1,0:T(4,128)S(1)} %pad_maximum_fusion.1), channel_id=1, source_target_pairs={{0,8},{8,16},{16,24},{24,32},{32,40},{40,48},{48,56},{56,64},{64,7... | collective-permute-start | bytes 294920 | tf_op jit(solution)/shard_map/ppermute | solution.py:419
  18.2 1.9 %collective-permute-start.3 = (f32[8,1,6,4,128]{4,3,2,1,0:T(4,128)S(1)}, f32[8,1,6,4,128]{4,3,2,1,0:T(4,128)S(1)}, u32[]{:S(2)}, u32[]{:S(2)}) collective-permute-start(f32[8,1,6,4,128]{4,3,2,1,0:T(4,128)S(1)} %pad_maximum_fusion.2), channel_id=1, source_target_pairs={{8,0},{16,8},{24,16},{32,24},{40,32},{48,40},{56,48},{64,56},{72,6... | collective-permute-start | bytes 294920 | tf_op jit(solution)/shard_map/ppermute | solution.py:419
  20.2 0.0 collective-permute-done.2
  20.2 7.6 %collective-permute-done.3 = f32[8,1,6,4,128]{4,3,2,1,0:T(4,128)S(1)} collective-permute-done((f32[8,1,6,4,128]{4,3,2,1,0:T(4,128)S(1)}, f32[8,1,6,4,128]{4,3,2,1,0:T(4,128)S(1)}, u32[]{:S(2)}, u32[]{:S(2)}) %collective-permute-start.3) | collective-permute-done | bytes 98336 | tf_op jit(solution)/shard_map/ppermute | solution.py:419
  27.8 0.0 copy-start
  27.8 0.1 slice_reduce_fusion
  27.9 0.1 reduce_max.26
  28.1 0.6 fusion.1
  29.4 0.0 copy-done
  29.4 39.1 %moments.1 = f32[6,64,128]{2,1,0:T(8,128)} custom-call(s32[1]{0:T(128)} %bitcast.10.n_ref, s32[1600]{0:T(1024)} %constant.70.clone.tab, f32[3]{0:T(128)} %pad_maximum_fusion.5.corner_ref, bf16[32,256]{1,0:T(8,128)(2,1)} %constant.71.clone.spread_ref, f32[8,144,128]{2,1,0:T(8,128)} %copy-done), custom_call_target="tpu_custom_call" | custom-call | tf_op jit(solution)/shard_map/moments/pallas_call | solution.py:377
  68.5 0.0 copy-start.1
  68.5 0.9 fusion.4
  69.3 0.1 copy-done.1
  69.5 5.5 %collective-permute-start.4 = (f32[6,4,1,4,128]{4,3,2,0,1:T(4,128)S(1)}, f32[6,4,1,4,128]{4,3,2,0,1:T(4,128)S(1)}, u32[]{:S(2)}, u32[]{:S(2)}) collective-permute-start(f32[6,4,1,4,128]{4,3,2,0,1:T(4,128)S(1)} %copy.23), channel_id=1, source_target_pairs={{0,1},{1,2},{2,3},{3,4},{4,5},{5,6},{6,7},{8,9},{9,10},{10,11},{11... | collective-permute-start | bytes 147464 | tf_op jit(solution)/shard_map/ppermute | solution.py:419
  75.0 1.9 %collective-permute-start.5 = (f32[6,4,1,4,128]{4,3,2,0,1:T(4,128)S(1)}, f32[6,4,1,4,128]{4,3,2,0,1:T(4,128)S(1)}, u32[]{:S(2)}, u32[]{:S(2)}) collective-permute-start(f32[6,4,1,4,128]{4,3,2,0,1:T(4,128)S(1)} %copy.24), channel_id=1, source_target_pairs={{1,0},{2,1},{3,2},{4,3},{5,4},{6,5},{7,6},{9,8},{10,9},{11,10},{12... | collective-permute-start | bytes 147464 | tf_op jit(solution)/shard_map/ppermute | solution.py:419
  76.9 0.0 collective-permute-done.4
  77.0 5.0 %collective-permute-done.5 = f32[6,4,1,4,128]{4,3,2,0,1:T(4,128)S(1)} collective-permute-done((f32[6,4,1,4,128]{4,3,2,0,1:T(4,128)S(1)}, f32[6,4,1,4,128]{4,3,2,0,1:T(4,128)S(1)}, u32[]{:S(2)}, u32[]{:S(2)}) %collective-permute-start.5) | collective-permute-done | bytes 49184 | tf_op jit(solution)/shard_map/ppermute | solution.py:419
  82.0 3.9 %collective-permute-start.6 = (f32[6,1,6,4,128]{4,3,2,0,1:T(4,128)S(1)}, f32[6,1,6,4,128]{4,3,2,0,1:T(4,128)S(1)}, u32[]{:S(2)}, u32[]{:S(2)}) collective-permute-start(f32[6,1,6,4,128]{4,3,2,0,1:T(4,128)S(1)} %pad_maximum_fusion.3), channel_id=1, source_target_pairs={{0,8},{8,16},{16,24},{24,32},{32,40},{40,48},{48,56},{56,64},{64,7... | collective-permute-start | bytes 221192 | tf_op jit(solution)/shard_map/ppermute | solution.py:419
  85.9 1.9 %collective-permute-start.7 = (f32[6,1,6,4,128]{4,3,2,0,1:T(4,128)S(1)}, f32[6,1,6,4,128]{4,3,2,0,1:T(4,128)S(1)}, u32[]{:S(2)}, u32[]{:S(2)}) collective-permute-start(f32[6,1,6,4,128]{4,3,2,0,1:T(4,128)S(1)} %pad_maximum_fusion.4), channel_id=1, source_target_pairs={{8,0},{16,8},{24,16},{32,24},{40,32},{48,40},{56,48},{64,56},{72,6... | collective-permute-start | bytes 221192 | tf_op jit(solution)/shard_map/ppermute | solution.py:419
  87.9 0.0 collective-permute-done.6
  87.9 7.3 %collective-permute-done.7 = f32[6,1,6,4,128]{4,3,2,0,1:T(4,128)S(1)} collective-permute-done((f32[6,1,6,4,128]{4,3,2,0,1:T(4,128)S(1)}, f32[6,1,6,4,128]{4,3,2,0,1:T(4,128)S(1)}, u32[]{:S(2)}, u32[]{:S(2)}) %collective-permute-start.7) | collective-permute-done | bytes 73760 | tf_op jit(solution)/shard_map/ppermute | solution.py:419
  95.2 0.0 copy-start.2
  95.2 0.8 copy-done.2
  95.9 68.6 %rates.1 = f32[4,64,128]{2,1,0:T(8,128)} custom-call(s32[1]{0:T(128)} %bitcast.10.n_ref, s32[1600]{0:T(1024)} %constant.70.clone.tab, f32[3]{0:T(128)} %pad_maximum_fusion.5.corner_ref, bf16[32,256]{1,0:T(8,128)(2,1)} %constant.71.clone.spread_ref, f32[8,144,128]{2,1,0:T(8,128)} %copy-done, f32[6,144,128]{2,1,0:T(8,128)} %copy-done.2), custom_call_target="tpu_custom_call" | custom-call | tf_op jit(solution)/shard_map/rates/pallas_call | solution.py:396
  164.5 0.0 slice-start
  164.5 0.0 slice-start.1
  164.5 0.8 slice-done
  165.3 0.7 broadcast_select_fusion.2
  166.0 0.0 copy-start.5
  166.0 0.0 slice-done.1
  166.0 0.7 copy-done.5
  166.6 0.7 add_select_fusion
  (27 shorter events, 0.3 us)
Async XLA Ops:
  0.6 0.9 copy-start.4
  0.6 1.7 %copy-start.3 = (f32[3,4,4,4,128]{4,3,2,1,0:T(4,128)S(1)}, f32[3,4,4,4,128]{4,3,2,1,0:T(4,128)}, u32[]{:S(2)}) copy-start(f32[3,4,4,4,128]{4,3,2,1,0:T(4,128)} %param.11) | copy-start | bytes 294916
  3.4 8.1 %collective-permute-start.1 = (f32[8,4,1,4,128]{4,3,2,1,0:T(4,128)S(1)}, f32[8,4,1,4,128]{4,3,2,1,0:T(4,128)S(1)}, u32[]{:S(2)}, u32[]{:S(2)}) collective-permute-start(f32[8,4,1,4,128]{4,3,2,1,0:T(4,128)S(1)} %get-tuple-element.16), channel_id=1, source_target_pairs={{1,0},{2,1},{3,2},{4,3},{5,4},{6,5},{7,6},{9,8},{10,9},{11,10},{12... | collective-permute-start | bytes 196616 | tf_op jit(solution)/shard_map/ppermute | solution.py:419
  5.5 6.7 %collective-permute-start = (f32[8,4,1,4,128]{4,3,2,1,0:T(4,128)S(1)}, f32[8,4,1,4,128]{4,3,2,1,0:T(4,128)S(1)}, u32[]{:S(2)}, u32[]{:S(2)}) collective-permute-start(f32[8,4,1,4,128]{4,3,2,1,0:T(4,128)S(1)} %get-tuple-element.17), channel_id=1, source_target_pairs={{0,1},{1,2},{2,3},{3,4},{4,5},{5,6},{6,7},{8,9},{9,10},{10,11},{11... | collective-permute-start | bytes 196616 | tf_op jit(solution)/shard_map/ppermute | solution.py:419
  12.2 8.0 %collective-permute-start.2 = (f32[8,1,6,4,128]{4,3,2,1,0:T(4,128)S(1)}, f32[8,1,6,4,128]{4,3,2,1,0:T(4,128)S(1)}, u32[]{:S(2)}, u32[]{:S(2)}) collective-permute-start(f32[8,1,6,4,128]{4,3,2,1,0:T(4,128)S(1)} %pad_maximum_fusion.1), channel_id=1, source_target_pairs={{0,8},{8,16},{16,24},{24,32},{32,40},{40,48},{48,56},{56,64},{64,7... | collective-permute-start | bytes 294920 | tf_op jit(solution)/shard_map/ppermute | solution.py:419
  18.2 9.5 %collective-permute-start.3 = (f32[8,1,6,4,128]{4,3,2,1,0:T(4,128)S(1)}, f32[8,1,6,4,128]{4,3,2,1,0:T(4,128)S(1)}, u32[]{:S(2)}, u32[]{:S(2)}) collective-permute-start(f32[8,1,6,4,128]{4,3,2,1,0:T(4,128)S(1)} %pad_maximum_fusion.2), channel_id=1, source_target_pairs={{8,0},{16,8},{24,16},{32,24},{40,32},{48,40},{56,48},{64,56},{72,6... | collective-permute-start | bytes 294920 | tf_op jit(solution)/shard_map/ppermute | solution.py:419
  27.8 1.6 copy-start
  68.5 1.0 copy-start.1
  69.5 7.5 %collective-permute-start.4 = (f32[6,4,1,4,128]{4,3,2,0,1:T(4,128)S(1)}, f32[6,4,1,4,128]{4,3,2,0,1:T(4,128)S(1)}, u32[]{:S(2)}, u32[]{:S(2)}) collective-permute-start(f32[6,4,1,4,128]{4,3,2,0,1:T(4,128)S(1)} %copy.23), channel_id=1, source_target_pairs={{0,1},{1,2},{2,3},{3,4},{4,5},{5,6},{6,7},{8,9},{9,10},{10,11},{11... | collective-permute-start | bytes 147464 | tf_op jit(solution)/shard_map/ppermute | solution.py:419
  75.0 6.9 %collective-permute-start.5 = (f32[6,4,1,4,128]{4,3,2,0,1:T(4,128)S(1)}, f32[6,4,1,4,128]{4,3,2,0,1:T(4,128)S(1)}, u32[]{:S(2)}, u32[]{:S(2)}) collective-permute-start(f32[6,4,1,4,128]{4,3,2,0,1:T(4,128)S(1)} %copy.24), channel_id=1, source_target_pairs={{1,0},{2,1},{3,2},{4,3},{5,4},{6,5},{7,6},{9,8},{10,9},{11,10},{12... | collective-permute-start | bytes 147464 | tf_op jit(solution)/shard_map/ppermute | solution.py:419
  82.0 5.9 %collective-permute-start.6 = (f32[6,1,6,4,128]{4,3,2,0,1:T(4,128)S(1)}, f32[6,1,6,4,128]{4,3,2,0,1:T(4,128)S(1)}, u32[]{:S(2)}, u32[]{:S(2)}) collective-permute-start(f32[6,1,6,4,128]{4,3,2,0,1:T(4,128)S(1)} %pad_maximum_fusion.3), channel_id=1, source_target_pairs={{0,8},{8,16},{16,24},{24,32},{32,40},{40,48},{48,56},{56,64},{64,7... | collective-permute-start | bytes 221192 | tf_op jit(solution)/shard_map/ppermute | solution.py:419
  85.9 9.3 %collective-permute-start.7 = (f32[6,1,6,4,128]{4,3,2,0,1:T(4,128)S(1)}, f32[6,1,6,4,128]{4,3,2,0,1:T(4,128)S(1)}, u32[]{:S(2)}, u32[]{:S(2)}) collective-permute-start(f32[6,1,6,4,128]{4,3,2,0,1:T(4,128)S(1)} %pad_maximum_fusion.4), channel_id=1, source_target_pairs={{8,0},{16,8},{24,16},{32,24},{40,32},{48,40},{56,48},{64,56},{72,6... | collective-permute-start | bytes 221192 | tf_op jit(solution)/shard_map/ppermute | solution.py:419
  95.2 0.8 copy-start.2
  164.5 0.8 slice-start
  164.5 1.5 slice-start.1
  166.0 0.7 copy-start.5

commit v3 on v2

--- a/solution.py
+++ b/solution.py
@@ -78,40 +78,41 @@
     return h, m, r - m
 
 
+def fixed_rows(rows_ref):
+    rows_ref[...] = jnp.zeros_like(rows_ref)
+    rows_ref[pl.ds(7 * 8, 8), :] = jnp.ones((8, 128), F32)
+
+
 def pair_rows(state, corner, spread, k, with_targets, rows_ref, a_ref, b_ref, rho_ref):
     blk = pl.ds(pl.multiple_of(k * 8, 8), 8)
     x = [state[d, blk, :] - corner[d] for d in range(3)]
     v = [state[3 + d, blk, :] for d in range(3)]
-    rho = state[6, blk, :]
-    n2 = x[0] * x[0] + x[1] * x[1] + x[2] * x[2]
-    xv = x[0] * v[0] + x[1] * v[1] + x[2] * v[2]
-    one = jnp.ones_like(n2)
-    zero = jnp.zeros_like(n2)
+    n2s = split3(x[0] * x[0] + x[1] * x[1] + x[2] * x[2])
+    xvs = split3(x[0] * v[0] + x[1] * v[1] + x[2] * v[2])
     xs = [split3(t) for t in x]
     vs = [split3(t) for t in v]
-    rs = split3(rho)
-    n2s = split3(n2)
-    xvs = split3(xv)
-
-    def put(group, parts):
+    rs = split3(state[6, blk, :])
+
+    def put(group, row, parts):
         for r, p in enumerate(parts):
-            rows_ref[pl.ds((group * 8 + r) * 8, 8), :] = p
+            rows_ref[pl.ds((group * 8 + row + r) * 8, 8), :] = p
 
     def get(group, b):
         return rows_ref[pl.ds(group * 64 + b, 8, stride=8), :]
 
     for s in range(3):
-        put(s, [xs[d][s] for d in range(3)] + [vs[d][s] for d in range(3)] + [rs[s], one])
-    put(3, list(n2s) + list(xvs) + [one, one])
+        put(s, 0, [xs[d][s] for d in range(3)] + [vs[d][s] for d in range(3)] + [rs[s]])
+    put(3, 0, n2s + xvs)
     if with_targets:
         for s in range(3):
-            put(4 + s, [-0.5 * xs[d][s] for d in range(3)] + [zero] * 5)
-            put(7 + s, [-vs[d][s] for d in range(3)] + [-xs[d][s] for d in range(3)] + [zero] * 2)
-        quarter = one * 0.25
-        put(10, [-0.5 * xs[d][0] for d in range(3)] + [zero] * 4 + [0.25 * n2s[2]])
-        put(11, [-vs[d][0] for d in range(3)] + [-xs[d][0] for d in range(3)] + [zero, xvs[2]])
-        put(12, [quarter] * 3 + [zero] * 3 + [0.25 * n2s[0], 0.25 * n2s[1]])
-        put(13, [zero] * 3 + [one] * 3 + [xvs[0], xvs[1]])
+            put(4 + s, 0, [-0.5 * xs[d][s] for d in range(3)])
+            put(4 + s, 7, [0.25 * n2s[s]])
+            if rho_ref is not None:
+                put(7 + s, 0, [-vs[d][s] for d in range(3)] + [-xs[d][s] for d in range(3)])
+                put(7 + s, 7, [xvs[s]])
+        row = lax.broadcasted_iota(jnp.int32, (8, 128), 0)
+        quarters = jnp.where(row < 3, 0.25, 0.0)
+        ones = jnp.where((row >= 3) & (row < 6), 1.0, 0.0)
     cols = [jnp.concatenate([get(s, b) for s in range(4)], 0).T.astype(BF16) for b in range(8)]
     both = jnp.dot(jnp.concatenate(cols, 0), spread, preferred_element_type=F32)
     for b in range(8):
@@ -120,20 +121,51 @@
         if rho_ref is not None:
             rho_ref[k * 8 + b] = both[rows, 128:]
         if with_targets:
-            r2_rows = [get(10, b), get(5, b), get(6, b)] + [get(4 + s, b) for s in range(3)] * 2
-            b_ref[k * 8 + b, :, :128] = jnp.concatenate(r2_rows + [get(12, b)], 0).astype(BF16)
+            r2_rows = [get(4 + s, b) for s in range(3)] * 3
+            b_ref[k * 8 + b, :, :128] = jnp.concatenate(r2_rows + [quarters], 0).astype(BF16)
             if rho_ref is not None:
-                vx_rows = [get(11, b), get(8, b), get(9, b)] + [get(7 + s, b) for s in range(3)] * 2
-                b_ref[k * 8 + b, :, 128:] = jnp.concatenate(vx_rows + [get(13, b)], 0).astype(BF16)
-
-
-def store_features(rows_ref, out_ref, k, features, rows, first):
-    at = first
+                vx_rows = [get(7 + s, b) for s in range(3)] * 3
+                b_ref[k * 8 + b, :, 128:] = jnp.concatenate(vx_rows + [ones], 0).astype(BF16)
+
+
+def gather_blocks(parts, state):
+    at = 0
+    for part in parts:
+        for k in range(part.shape[1] // 8):
+            yield part, pl.ds(k * 8, 8), pl.ds(at, 8)
+            at += 8
+
+
+def load_state(parts, state):
+    peak = jnp.zeros((8, 128), F32)
+    for part, src, dst in gather_blocks(parts, state):
+        mass = part[7, src, :]
+        live = mass > 0.0
+        for d in range(6):
+            state[d, dst, :] = jnp.where(live, part[d, src, :], 0.0)
+        state[6, dst, :] = jnp.where(live, part[6, src, :], 1.0)
+        state[7, dst, :] = mass
+        peak = jnp.maximum(peak, mass)
+    level = (lax.broadcasted_iota(jnp.int32, (8, 128), 0) % 4 + 1).astype(F32)
+    return jnp.max(jnp.where(peak > 0.0, level, 1.0)).astype(jnp.int32)
+
+
+def centre():
+    return [(lax.axis_index("gx") * 8 + 4).astype(F32), (lax.axis_index("gy") * 8 + 4).astype(F32), 4.0]
+
+
+def unfold(src, height, k, rows_ref):
+    for b in range(8):
+        for g in range(height // 8):
+            rows = pl.ds(pl.multiple_of((k * 8 + b) * height, height) + g * 8, 8)
+            rows_ref[pl.ds(g * 64 + b, 8, stride=8), :] = src[rows, :]
+
+
+def store_features(rows_ref, features, at):
     for f in features:
         for piece in split3(f):
             rows_ref[pl.ds(at * 8, 8), :] = piece
             at += 1
-    return at
 
 
 def gather_features(rows_ref, out_ref, k, rows):
@@ -168,10 +200,14 @@
     lax.fori_loop(0, n // 4, step, 0)
 
 
-def moment_kernel(n_ref, tab, corner_ref, spread_ref, state, corr, a_ref, b_ref, f_ref, rows_ref, r_ref, acc):
-    corner = [corner_ref[d] for d in range(3)]
-    n = n_ref[0]
+def moment_kernel(tab, spread_ref, local, low_y, high_y, low_x, high_x, corr, state, a_ref, b_ref, f_ref, rows_ref,
+                  feat_ref, r_ref, acc):
+    corner = centre()
+    levels = load_state((local, low_y, high_y, low_x, high_x), state)
+    n = (3 * levels - 2) * 16
     spread = spread_ref[...]
+    fixed_rows(rows_ref)
+    feat_ref[...] = jnp.zeros_like(feat_ref)
 
     def prepare(k, with_targets):
         pair_rows(state, corner, spread, k, with_targets, rows_ref, a_ref, b_ref, None)
@@ -180,10 +216,8 @@
         vol = state[7, blk, :] / state[6, blk, :]
         vx = [vol * t for t in x]
         features = [vol] + vx + [vx[p] * x[q] for p, q in SYM_PAIRS]
-        at = store_features(rows_ref, f_ref, k, features, M1, 0)
-        for r in range(at, M1):
-            rows_ref[pl.ds(r * 8, 8), :] = jnp.zeros((8, 128), F32)
-        gather_features(rows_ref, f_ref, k, M1)
+        store_features(feat_ref, features, 0)
+        gather_features(feat_ref, f_ref, k, M1)
 
     def first(k, carry):
         prepare(k, True)
@@ -217,11 +251,12 @@
     for_items(n, one, rest)
 
     def finish(k, carry):
+        unfold(acc, M1, k, feat_ref)
         blk = pl.ds(pl.multiple_of(k * 8, 8), 8)
         x = [state[d, blk, :] - corner[d] for d in range(3)]
 
         def total(f):
-            at = [acc[pl.ds(k * (8 * M1) + 3 * f + s, 8, stride=M1), :] for s in range(3)]
+            at = [feat_ref[pl.ds((3 * f + s) * 8, 8), :] for s in range(3)]
             return at[0] + (at[1] + at[2])
 
         t0 = total(0)
@@ -246,11 +281,17 @@
     lax.fori_loop(0, LOCAL // 8, finish, 0)
 
 
-def rate_kernel(n_ref, tab, corner_ref, spread_ref, state, corr, rate, a_ref, b_ref, rho_ref, f_ref, rows_ref, r_ref, acc,
-                accw):
-    corner = [corner_ref[d] for d in range(3)]
-    n = n_ref[0]
+def rate_kernel(tab, spread_ref, local, low_y, high_y, low_x, high_x, corr0, corr1, corr2, corr3, corr4, rate, accel,
+                state, corr, a_ref, b_ref, rho_ref, f_ref, rows_ref, feat_ref, featw_ref, r_ref, acc, accw):
+    corner = centre()
+    levels = load_state((local, low_y, high_y, low_x, high_x), state)
+    n = (3 * levels - 2) * 16
     spread = spread_ref[...]
+    fixed_rows(rows_ref)
+    feat_ref[...] = jnp.zeros_like(feat_ref)
+    for part, src, dst in gather_blocks((corr0, corr1, corr2, corr3, corr4), corr):
+        for d in range(6):
+            corr[d, dst, :] = part[d, src, :]
 
     def pressure(rho):
         r2 = rho * rho
@@ -278,13 +319,9 @@
         own = (mv + [mv[p] * x[q] for p in range(3) for q in range(3)] + m_sym_v
                + [v[0] * m_sym_x[0] + v[1] * m_sym_x[1] + v[2] * m_sym_x[2]]
                + [mp] + [mp * t for t in x] + [prs * t for t in m_sym] + [prs * t for t in m_sym_x])
-        at = store_features(rows_ref, f_ref, k, shared, M2, 0)
-        for r in range(at, W_ROWS):
-            rows_ref[pl.ds(r * 8, 8), :] = jnp.zeros((8, 128), F32)
-        at = store_features(rows_ref, f_ref, k, own, M2, W_ROWS)
-        for r in range(at, M2):
-            rows_ref[pl.ds(r * 8, 8), :] = jnp.zeros((8, 128), F32)
-        gather_features(rows_ref, f_ref, k, M2)
+        store_features(feat_ref, shared, 0)
+        store_features(feat_ref, own, W_ROWS)
+        gather_features(feat_ref, f_ref, k, M2)
 
     def first(k, carry):
         prepare(k, True)
@@ -329,19 +366,21 @@
     for_items(n, one, rest)
 
     def finish(k, carry):
+        unfold(acc, M2, k, feat_ref)
+        unfold(accw, MW, k, featw_ref)
         blk = pl.ds(pl.multiple_of(k * 8, 8), 8)
         x = [state[d, blk, :] - corner[d] for d in range(3)]
         v = [state[3 + d, blk, :] for d in range(3)]
         prs = pressure(state[6, blk, :])
         sym = [corr[r, blk, :] for r in range(6)]
 
-        def total(ref, height, first_row, f):
-            at = [ref[pl.ds(k * (8 * height) + first_row + 3 * f + s, 8, stride=height), :] for s in range(3)]
+        def total(ref, first_row, f):
+            at = [ref[pl.ds((first_row + 3 * f + s) * 8, 8), :] for s in range(3)]
             return at[0] + (at[1] + at[2])
 
-        shared = [total(acc, M2, 0, f) for f in range(13)]
-        own = [total(acc, M2, W_ROWS, f) for f in range(29)]
-        visc = [total(accw, MW, 0, f) for f in range(13)]
+        shared = [total(feat_ref, 0, f) for f in range(13)]
+        own = [total(feat_ref, W_ROWS, f) for f in range(29)]
+        visc = [total(featw_ref, 0, f) for f in range(13)]
         m0, mx, mk, mkx = shared[0], shared[1:4], shared[4:10], shared[10:13]
         mv, mvx, mkv, mvkx = own[0:3], own[3:12], own[12:15], own[15]
         p0, px, pk, pkx = own[16], own[17:20], own[20:26], own[26:29]
@@ -355,14 +394,16 @@
         for p in range(3):
             inner = inner + v[p] * (mk_x[p] - mkx[p]) - x[p] * mkv[p]
         inner = inner + mvkx
-        rate[0, blk, :] = (-0.5 * KERNEL_GRAD) * inner
+        live = state[7, blk, :] > 0.0
+        rate[blk, :] = jnp.where(live, (-0.5 * KERNEL_GRAD) * inner, 0.0)
         near = [prs * (x[p] * m0 - mx[p]) + (x[p] * p0 - px[p]) - 0.25 * (x[p] * w0 - wx[p]) for p in range(3)]
         mine = times(sym, near)
         pk_x = times(pk, x)
         wk_x = times(wk, x)
         for p in range(3):
             far = prs * (mk_x[p] - mkx[p]) + (pk_x[p] - pkx[p]) - 0.25 * (wk_x[p] - wkx[p])
-            rate[1 + p, blk, :] = (0.5 * KERNEL_GRAD) * (mine[p] + far)
+            pull = -GRAVITY if p == 2 else 0.0
+            accel[p, blk, :] = jnp.where(live, (0.5 * KERNEL_GRAD) * (mine[p] + far) + pull, 0.0)
         return carry
 
     lax.fori_loop(0, LOCAL // 8, finish, 0)
@@ -373,96 +414,82 @@
 ALL_COLUMNS = tuple((a, b) for a in range(1, 5) for b in range(1, 5))
 
 
-def run_moments(n, table, corner, state):
+def run_moments(table, strips):
     return pl.pallas_call(
         moment_kernel,
         out_shape=jax.ShapeDtypeStruct((6, LOCAL, 128), F32),
-        in_specs=[SMEM, SMEM, SMEM, VMEM, VMEM],
+        in_specs=[SMEM] + [VMEM] * 6,
         out_specs=VMEM,
         scratch_shapes=[
+            pltpu.VMEM((8, TOTAL, 128), F32),
             pltpu.VMEM((TOTAL, 128, KA), BF16),
             pltpu.VMEM((LOCAL, KA, 128), BF16),
             pltpu.VMEM((TOTAL, M1, 128), BF16),
-            pltpu.VMEM((14 * 64, 128), F32),
+            pltpu.VMEM((10 * 64, 128), F32),
+            pltpu.VMEM((M1 * 8, 128), F32),
             pltpu.VMEM((4, NB * 128, 128), F32),
             pltpu.VMEM((LOCAL * M1, 128), F32),
         ],
         compiler_params=pltpu.CompilerParams(vmem_limit_bytes=56 * 2**20),
         name="moments",
-    )(n, table, corner, jnp.asarray(spread_matrix(), BF16), state)
-
-
-def run_rates(n, table, corner, state, corr):
+    )(table, jnp.asarray(spread_matrix(), BF16), *strips)
+
+
+def run_rates(table, strips, corr_strips):
     return pl.pallas_call(
         rate_kernel,
-        out_shape=jax.ShapeDtypeStruct((4, LOCAL, 128), F32),
-        in_specs=[SMEM, SMEM, SMEM, VMEM, VMEM, VMEM],
-        out_specs=VMEM,
+        out_shape=(jax.ShapeDtypeStruct((LOCAL, 128), F32), jax.ShapeDtypeStruct((3, LOCAL, 128), F32)),
+        in_specs=[SMEM] + [VMEM] * 11,
+        out_specs=(VMEM, VMEM),
         scratch_shapes=[
+            pltpu.VMEM((8, TOTAL, 128), F32),
+            pltpu.VMEM((6, TOTAL, 128), F32),
             pltpu.VMEM((TOTAL, 128, KA), BF16),
             pltpu.VMEM((LOCAL, KA, 256), BF16),
             pltpu.VMEM((TOTAL, 128, 128), F32),
             pltpu.VMEM((TOTAL, M2, 128), BF16),
+            pltpu.VMEM((10 * 64, 128), F32),
             pltpu.VMEM((M2 * 8, 128), F32),
+            pltpu.VMEM((MW * 8, 128), F32),
             pltpu.VMEM((4, NB * 128, 256), F32),
             pltpu.VMEM((LOCAL * M2, 128), F32),
             pltpu.VMEM((LOCAL * MW, 128), F32),
         ],
         compiler_params=pltpu.CompilerParams(vmem_limit_bytes=60 * 2**20),
         name="rates",
-    )(n, table, corner, jnp.asarray(spread_matrix(), BF16), state, corr)
-
-
-def shifted(value, axis, steps):
+    )(table, jnp.asarray(spread_matrix(), BF16), *strips, *corr_strips)
+
+
+def exchange(first, last, axis):
     count = lax.axis_size(axis)
-    first, last = (max(0, -steps), min(count, count - steps))
-    return lax.ppermute(value, axis, [(source, source + steps) for source in range(first, last)])
+    odd = lax.axis_index(axis) % 2 == 1
+    inner = [(i, i ^ 1) for i in range(count)]
+    outer = [(i, i + 1) for i in range(1, count - 1, 2)] + [(i + 1, i) for i in range(1, count - 1, 2)]
+    across = lax.ppermute(jnp.where(odd, last, first), axis, outer)
+    within = lax.ppermute(jnp.where(odd, first, last), axis, inner)
+    return jnp.where(odd, within, across), jnp.where(odd, across, within)
 
 
 def with_halo(blocks):
-    ch = blocks.shape[0]
-    low_y = shifted(blocks[:, :, -1:], "gy", 1)
-    high_y = shifted(blocks[:, :, :1], "gy", -1)
+    low_y, high_y = exchange(blocks[:, :, :1], blocks[:, :, -1:], "gy")
 
     def row(a):
         return jnp.concatenate([low_y[:, a:a + 1], blocks[:, a:a + 1], high_y[:, a:a + 1]], 2)
 
-    low_x = shifted(row(3), "gx", 1)
-    high_x = shifted(row(0), "gx", -1)
-    return jnp.concatenate([t.reshape(ch, -1, 128) for t in (blocks, low_y, high_y, low_x, high_x)], 1)
-
-
-def occupied_levels(mass):
-    any_live = jnp.max(mass.reshape(TOTAL // 4, 4, 128), axis=(0, 2)) > 0.0
-    return jnp.max(jnp.where(any_live, jnp.arange(1, 5, dtype=jnp.int32), 1))
+    low_x, high_x = exchange(row(0), row(3), "gx")
+    return [t.reshape(blocks.shape[0], -1, 128) for t in (blocks, low_y, high_y, low_x, high_x)]
 
 
 def body(positions, velocity, density, masses, counts):
     shape = density.shape
     live = lax.broadcasted_iota(jnp.int32, shape, 3) < counts[..., None]
-    blocks = jnp.concatenate(
-        [
-            jnp.where(live, positions, 0.0),
-            jnp.where(live, velocity, 0.0),
-            jnp.where(live, density, 1.0)[None],
-            jnp.where(live, masses, 0.0)[None],
-        ],
-        0,
-    )
-    state = with_halo(blocks)
-    state = state.at[6].set(jnp.where(state[6] > 0.0, state[6], 1.0))
-    centre_x = (lax.axis_index("gx") * 8 + 4).astype(F32)
-    centre_y = (lax.axis_index("gy") * 8 + 4).astype(F32)
-    corner = jnp.stack([centre_x, centre_y, jnp.float32(4.0)])
+    mass = jnp.where(live, masses, 0.0)
+    strips = with_halo(jnp.concatenate([positions, velocity, density[None], mass[None]], 0))
     table = jnp.asarray(item_table(ALL_COLUMNS))
-    n = ((3 * occupied_levels(state[7]) - 2) * 16).reshape(1)
-    corr = run_moments(n, table, corner, state)
-    corr_all = with_halo(corr.reshape((6,) + shape))
-    rates = run_rates(n, table, corner, state, corr_all).reshape((4,) + shape)
-    density_rate = jnp.where(live, rates[0], 0.0)
-    pull = jnp.asarray([0.0, 0.0, -GRAVITY], F32).reshape(3, 1, 1, 1, 1)
-    acceleration = jnp.where(live, rates[1:4] + pull, 0.0)
-    return (density_rate, acceleration)
+    corr = run_moments(table, strips)
+    corr_strips = with_halo(corr.reshape((6,) + shape))
+    rate, accel = run_rates(table, strips, corr_strips)
+    return (rate.reshape(shape), accel.reshape((3,) + shape))
 
 
 def solution(mesh):

time: 168 us -> 151 us (0.90)
  the two profiles are of different devices: /device:TPU:121 before, /device:TPU:6 now
where the time goes in v3:
time: 151 us; the launch traced here: 150 us
  Pallas kernels  107 us (71%)
  waiting for transfers between devices  18.3 us (12%)
  starting transfers between devices  16.4 us (11%)
  other arithmetic  4.19 us (3%)
  local copies, waits for them, and re-layouts  3.43 us (2%)
    pallas_call x1, Pallas kernels, run_rates(): pl.pallas_call(rate_kernel, out_shape=(jax.ShapeDtypeStruct((LOCAL, 128),...  68.2 us
    pallas_call x1, Pallas kernels, run_moments(): pl.pallas_call(moment_kernel, out_shape=jax.ShapeDtypeStruct((6, LOCAL, 1...  39.1 us
    ppermute x4, waiting for transfers between devices, exchange(): across = lax.ppermute(jnp.where(odd, last, first), axis, outer)  16.2 us
    ppermute x4, starting transfers between devices, exchange(): across = lax.ppermute(jnp.where(odd, last, first), axis, outer)  15.9 us
  transfers between devices with their start and end apart: 8, of which 5 were waited for; matrix products, arithmetic and copies ran while one was open for 1% of the time, Pallas kernels for 0%

profile of v3, /device:TPU:6, one launch (start us, length us, event | category | flops | bytes accessed | tf_op | source)
XLA Modules:
  0.0 150.4 jit_solution(6416017712829569653)
XLA Ops:
  0.6 0.0 copy-start.3
  0.7 0.9 fusion.7
  1.5 0.0 copy-done.3
  1.5 1.0 pad_maximum_fusion.1
  2.6 6.2 %collective-permute-start.1 = (f32[8,4,1,4,128]{4,3,2,1,0:T(4,128)S(1)}, f32[8,4,1,4,128]{4,3,2,1,0:T(4,128)S(1)}, u32[]{:S(2)}, u32[]{:S(2)}) collective-permute-start(f32[8,4,1,4,128]{4,3,2,1,0:T(4,128)S(1)} %get-tuple-element.8), channel_id=1, source_target_pairs={{1,2},{3,4},{5,6},{2,1},{4,3},{6,5},{9,10},{11,12},{13,14},{10,9},... | collective-permute-start | bytes 196616 | tf_op jit(solution)/shard_map/ppermute | solution.py:468
  8.8 0.0 copy-start.6
  8.8 0.0 copy-start.7
  8.8 0.1 collective-permute-start
  8.9 0.6 copy-done.6
  9.5 0.0 copy-done.7
  9.5 0.1 fusion
  9.6 1.4 collective-permute-done.1
  11.0 2.1 %collective-permute-done = f32[8,4,1,4,128]{4,3,2,1,0:T(4,128)S(1)} collective-permute-done((f32[8,4,1,4,128]{4,3,2,1,0:T(4,128)S(1)}, f32[8,4,1,4,128]{4,3,2,1,0:T(4,128)S(1)}, u32[]{:S(2)}, u32[]{:S(2)}) %collective-permute-start) | collective-permute-done | bytes 65568 | tf_op jit(solution)/shard_map/ppermute | solution.py:469
  13.2 0.0 copy-start.1
  13.2 0.0 copy-start.2
  13.2 0.6 copy-done.1
  13.8 0.0 copy-done.2
  13.8 0.0 copy-start.4
  13.8 0.0 copy-start.5
  13.9 3.5 %collective-permute-start.3 = (f32[8,1,6,4,128]{4,3,2,1,0:T(4,128)S(1)}, f32[8,1,6,4,128]{4,3,2,1,0:T(4,128)S(1)}, u32[]{:S(2)}, u32[]{:S(2)}) collective-permute-start(f32[8,1,6,4,128]{4,3,2,1,0:T(4,128)S(1)} %get-tuple-element.16), channel_id=1, source_target_pairs={{8,16},{24,32},{40,48},{56,64},{72,80},{88,96},{104,112},{16,8},{3... | collective-permute-start | bytes 294920 | tf_op jit(solution)/shard_map/ppermute | solution.py:468
  17.4 0.2 collective-permute-start.2
  17.6 0.0 copy-done.4
  17.6 0.0 copy-done.5
  17.6 0.7 pad_maximum_fusion.local
  18.3 5.1 %collective-permute-done.3 = f32[8,1,6,4,128]{4,3,2,1,0:T(4,128)S(1)} collective-permute-done((f32[8,1,6,4,128]{4,3,2,1,0:T(4,128)S(1)}, f32[8,1,6,4,128]{4,3,2,1,0:T(4,128)S(1)}, u32[]{:S(2)}, u32[]{:S(2)}) %collective-permute-start.3) | collective-permute-done | bytes 98336 | tf_op jit(solution)/shard_map/ppermute | solution.py:468
  23.4 0.0 collective-permute-done.2
  23.4 0.7 broadcast_select_fusion
  24.1 39.1 %moments.1.corr0 = f32[6,64,128]{2,1,0:T(8,128)} custom-call(s32[1600]{0:T(1024)} %constant.37.clone.tab, bf16[32,256]{1,0:T(8,128)(2,1)} %constant.38.clone.spread_ref, f32[8,64,128]{2,1,0:T(8,128)} %pad_maximum_fusion.local, f32[8,16,128]{2,1,0:T(8,128)} %bitcast.38, f32[8,16,128]{2,1,0:T(8,128)} %bitcast.36, f32[8,24,128]{2,1,0:T(8,128)} %bitcast.34, ...), custom_call_target="tpu_custom_call" | custom-call | tf_op jit(solution)/shard_map/moments/pallas_call | solution.py:418
  63.2 0.0 copy-start
  63.2 0.9 fusion.2
  64.1 3.9 %collective-permute-start.5 = (f32[6,4,1,4,128]{4,3,2,0,1:T(4,128)S(1)}, f32[6,4,1,4,128]{4,3,2,0,1:T(4,128)S(1)}, u32[]{:S(2)}, u32[]{:S(2)}) collective-permute-start(f32[6,4,1,4,128]{4,3,2,0,1:T(4,128)S(1)} %get-tuple-element.26), channel_id=1, source_target_pairs={{1,2},{3,4},{5,6},{2,1},{4,3},{6,5},{9,10},{11,12},{13,14},{10,9},... | collective-permute-start | bytes 147464 | tf_op jit(solution)/shard_map/ppermute | solution.py:468
  68.0 0.1 collective-permute-start.4
  68.1 0.0 copy-done
  68.1 4.1 %collective-permute-done.5 = f32[6,4,1,4,128]{4,3,2,0,1:T(4,128)S(1)} collective-permute-done((f32[6,4,1,4,128]{4,3,2,0,1:T(4,128)S(1)}, f32[6,4,1,4,128]{4,3,2,0,1:T(4,128)S(1)}, u32[]{:S(2)}, u32[]{:S(2)}) %collective-permute-start.5) | collective-permute-done | bytes 49184 | tf_op jit(solution)/shard_map/ppermute | solution.py:468
  72.2 0.0 collective-permute-done.4
  72.3 2.3 %collective-permute-start.7 = (f32[6,1,6,4,128]{4,3,2,0,1:T(4,128)S(1)}, f32[6,1,6,4,128]{4,3,2,0,1:T(4,128)S(1)}, u32[]{:S(2)}, u32[]{:S(2)}) collective-permute-start(f32[6,1,6,4,128]{4,3,2,0,1:T(4,128)S(1)} %get-tuple-element.20), channel_id=1, source_target_pairs={{8,16},{24,32},{40,48},{56,64},{72,80},{88,96},{104,112},{16,8},{3... | collective-permute-start | bytes 221192 | tf_op jit(solution)/shard_map/ppermute | solution.py:468
  74.6 0.1 collective-permute-start.6
  74.7 0.6 copy.13
  75.4 0.6 copy.12
  76.0 5.6 %collective-permute-done.7 = f32[6,1,6,4,128]{4,3,2,0,1:T(4,128)S(1)} collective-permute-done((f32[6,1,6,4,128]{4,3,2,0,1:T(4,128)S(1)}, f32[6,1,6,4,128]{4,3,2,0,1:T(4,128)S(1)}, u32[]{:S(2)}, u32[]{:S(2)}) %collective-permute-start.7) | collective-permute-done | bytes 73760 | tf_op jit(solution)/shard_map/ppermute | solution.py:468
  81.6 0.0 collective-permute-done.6
  81.6 0.7 broadcast_select_fusion.4
  82.3 68.2 %rates.1 = (f32[64,128]{1,0:T(8,128)}, f32[3,64,128]{2,1,0:T(8,128)}) custom-call(s32[1600]{0:T(1024)} %constant.37.clone.tab, bf16[32,256]{1,0:T(8,128)(2,1)} %constant.38.clone.spread_ref, f32[8,64,128]{2,1,0:T(8,128)} %pad_maximum_fusion.local, f32[8,16,128]{2,1,0:T(8,128)} %bitcast.39, f32[8,16,128]{2,1,0:T(8,128)} %bitcast.37, f32[8,24,128]{2,1,0:T(8,128)} %bitcast.35, ...), custom_call_target="tpu_custom_call" | custom-call | tf_op jit(solution)/shard_map/rates/pallas_call | solution.py:439
  (11 shorter events, 0.2 us)
Async XLA Ops:
  0.6 0.9 copy-start.3
  2.6 8.4 %collective-permute-start.1 = (f32[8,4,1,4,128]{4,3,2,1,0:T(4,128)S(1)}, f32[8,4,1,4,128]{4,3,2,1,0:T(4,128)S(1)}, u32[]{:S(2)}, u32[]{:S(2)}) collective-permute-start(f32[8,4,1,4,128]{4,3,2,1,0:T(4,128)S(1)} %get-tuple-element.8), channel_id=1, source_target_pairs={{1,2},{3,4},{5,6},{2,1},{4,3},{6,5},{9,10},{11,12},{13,14},{10,9},... | collective-permute-start | bytes 196616 | tf_op jit(solution)/shard_map/ppermute | solution.py:468
  8.8 0.8 copy-start.6
  8.8 0.8 copy-start.7
  8.8 4.3 %collective-permute-start = (f32[8,4,1,4,128]{4,3,2,1,0:T(4,128)S(1)}, f32[8,4,1,4,128]{4,3,2,1,0:T(4,128)S(1)}, u32[]{:S(2)}, u32[]{:S(2)}) collective-permute-start(f32[8,4,1,4,128]{4,3,2,1,0:T(4,128)S(1)} %get-tuple-element.9), channel_id=1, source_target_pairs={{0,1},{1,0},{2,3},{3,2},{4,5},{5,4},{6,7},{7,6},{8,9},{9,8},{10,11... | collective-permute-start | bytes 196616 | tf_op jit(solution)/shard_map/ppermute | solution.py:469
  13.2 0.6 copy-start.1
  13.2 0.6 copy-start.2
  13.8 3.7 %copy-start.4 = (f32[3,4,4,4,128]{4,3,2,1,0:T(4,128)S(1)}, f32[3,4,4,4,128]{4,3,2,1,0:T(4,128)}, u32[]{:S(2)}) copy-start(f32[3,4,4,4,128]{4,3,2,1,0:T(4,128)} %param.8) | copy-start | bytes 294916
  13.8 3.7 %copy-start.5 = (f32[4,4,4,128]{3,2,1,0:T(4,128)S(1)}, f32[4,4,4,128]{3,2,1,0:T(4,128)}, u32[]{:S(2)}) copy-start(f32[4,4,4,128]{3,2,1,0:T(4,128)} %param.10) | copy-start | bytes 98308
  13.9 9.5 %collective-permute-start.3 = (f32[8,1,6,4,128]{4,3,2,1,0:T(4,128)S(1)}, f32[8,1,6,4,128]{4,3,2,1,0:T(4,128)S(1)}, u32[]{:S(2)}, u32[]{:S(2)}) collective-permute-start(f32[8,1,6,4,128]{4,3,2,1,0:T(4,128)S(1)} %get-tuple-element.16), channel_id=1, source_target_pairs={{8,16},{24,32},{40,48},{56,64},{72,80},{88,96},{104,112},{16,8},{3... | collective-permute-start | bytes 294920 | tf_op jit(solution)/shard_map/ppermute | solution.py:468
  17.4 6.1 %collective-permute-start.2 = (f32[8,1,6,4,128]{4,3,2,1,0:T(4,128)S(1)}, f32[8,1,6,4,128]{4,3,2,1,0:T(4,128)S(1)}, u32[]{:S(2)}, u32[]{:S(2)}) collective-permute-start(f32[8,1,6,4,128]{4,3,2,1,0:T(4,128)S(1)} %get-tuple-element.17), channel_id=1, source_target_pairs={{0,8},{8,0},{16,24},{24,16},{32,40},{40,32},{48,56},{56,48},{64,72... | collective-permute-start | bytes 294920 | tf_op jit(solution)/shard_map/ppermute | solution.py:469
  63.2 4.9 %copy-start = (f32[6,64,128]{2,1,0:T(8,128)S(1)}, f32[6,64,128]{2,1,0:T(8,128)}, u32[]{:S(2)}) copy-start(f32[6,64,128]{2,1,0:T(8,128)} %moments.1.corr0) | copy-start | bytes 589828
  64.1 8.1 %collective-permute-start.5 = (f32[6,4,1,4,128]{4,3,2,0,1:T(4,128)S(1)}, f32[6,4,1,4,128]{4,3,2,0,1:T(4,128)S(1)}, u32[]{:S(2)}, u32[]{:S(2)}) collective-permute-start(f32[6,4,1,4,128]{4,3,2,0,1:T(4,128)S(1)} %get-tuple-element.26), channel_id=1, source_target_pairs={{1,2},{3,4},{5,6},{2,1},{4,3},{6,5},{9,10},{11,12},{13,14},{10,9},... | collective-permute-start | bytes 147464 | tf_op jit(solution)/shard_map/ppermute | solution.py:468
  68.0 4.2 %collective-permute-start.4 = (f32[6,4,1,4,128]{4,3,2,0,1:T(4,128)S(1)}, f32[6,4,1,4,128]{4,3,2,0,1:T(4,128)S(1)}, u32[]{:S(2)}, u32[]{:S(2)}) collective-permute-start(f32[6,4,1,4,128]{4,3,2,0,1:T(4,128)S(1)} %get-tuple-element.27), channel_id=1, source_target_pairs={{0,1},{1,0},{2,3},{3,2},{4,5},{5,4},{6,7},{7,6},{8,9},{9,8},{10,11... | collective-permute-start | bytes 147464 | tf_op jit(solution)/shard_map/ppermute | solution.py:469
  72.3 9.3 %collective-permute-start.7 = (f32[6,1,6,4,128]{4,3,2,0,1:T(4,128)S(1)}, f32[6,1,6,4,128]{4,3,2,0,1:T(4,128)S(1)}, u32[]{:S(2)}, u32[]{:S(2)}) collective-permute-start(f32[6,1,6,4,128]{4,3,2,0,1:T(4,128)S(1)} %get-tuple-element.20), channel_id=1, source_target_pairs={{8,16},{24,32},{40,48},{56,64},{72,80},{88,96},{104,112},{16,8},{3... | collective-permute-start | bytes 221192 | tf_op jit(solution)/shard_map/ppermute | solution.py:468
  74.6 6.9 %collective-permute-start.6 = (f32[6,1,6,4,128]{4,3,2,0,1:T(4,128)S(1)}, f32[6,1,6,4,128]{4,3,2,0,1:T(4,128)S(1)}, u32[]{:S(2)}, u32[]{:S(2)}) collective-permute-start(f32[6,1,6,4,128]{4,3,2,0,1:T(4,128)S(1)} %get-tuple-element.21), channel_id=1, source_target_pairs={{0,8},{8,0},{16,24},{24,16},{32,40},{40,32},{48,56},{56,48},{64,72... | collective-permute-start | bytes 221192 | tf_op jit(solution)/shard_map/ppermute | solution.py:469

commit v4 on v3

--- a/solution.py
+++ b/solution.py
@@ -186,18 +186,18 @@
 CHUNKS = ((0, 2), (2, 4), (4, 6), (6, 8), (8, 9))
 
 
-def for_items(n, one, rest):
+def for_items(n, width, one, rest):
     one(0, 0)
     one(1, 1)
 
     def step(s, carry):
-        t = 4 * s
-        for e in range(4):
+        t = width * s
+        for e in range(width):
             one(jnp.minimum(t + e + 2, n - 1), (e + 2) % 4)
-            rest(t + e, e)
-        return carry
-
-    lax.fori_loop(0, n // 4, step, 0)
+            rest(t + e, e % 4)
+        return carry
+
+    lax.fori_loop(0, n // width, step, 0)
 
 
 def moment_kernel(tab, spread_ref, local, low_y, high_y, low_x, high_x, corr, state, a_ref, b_ref, f_ref, rows_ref,
@@ -248,7 +248,7 @@
         part = jnp.dot(lhs, jnp.concatenate(weights, 0), preferred_element_type=F32)
         acc[pl.ds(pl.multiple_of(i * M1, M1), M1), :] += part[:, :128] + part[:, 128:]
 
-    for_items(n, one, rest)
+    for_items(n, 16, one, rest)
 
     def finish(k, carry):
         unfold(acc, M1, k, feat_ref)
@@ -363,7 +363,7 @@
         part = jnp.dot(lhs[:MW], jnp.concatenate(viscous, 0), preferred_element_type=F32)
         accw[pl.ds(pl.multiple_of(i * MW, MW), MW), :] += part[:, :128] + part[:, 128:]
 
-    for_items(n, one, rest)
+    for_items(n, 8, one, rest)
 
     def finish(k, carry):
         unfold(acc, M2, k, feat_ref)

time: 151 us -> 146 us (0.967)
  Pallas kernels: 107 us -> 102 us
    pallas_call x1, Pallas kernels: 68.2 us -> 65.2 us  [run_rates(): pl.pallas_call(rate_kernel, out_shape=(jax.ShapeDtypeStruct((LOCAL, 128),...]
    pallas_call x1, Pallas kernels: 39.1 us -> 36.9 us  [run_moments(): pl.pallas_call(moment_kernel, out_shape=jax.ShapeDtypeStruct((6, LOCAL, 1...]
where the time goes in v4:
time: 146 us; the launch traced here: 145 us
  Pallas kernels  102 us (70%)
  waiting for transfers between devices  18.3 us (13%)
  starting transfers between devices  16.4 us (11%)
  other arithmetic  4.19 us (3%)
  local copies, waits for them, and re-layouts  3.43 us (2%)
    pallas_call x1, Pallas kernels, run_rates(): pl.pallas_call(rate_kernel, out_shape=(jax.ShapeDtypeStruct((LOCAL, 128),...  65.2 us
    pallas_call x1, Pallas kernels, run_moments(): pl.pallas_call(moment_kernel, out_shape=jax.ShapeDtypeStruct((6, LOCAL, 1...  36.9 us
    ppermute x4, waiting for transfers between devices, exchange(): across = lax.ppermute(jnp.where(odd, last, first), axis, outer)  16.2 us
    ppermute x4, starting transfers between devices, exchange(): across = lax.ppermute(jnp.where(odd, last, first), axis, outer)  15.9 us
  transfers between devices with their start and end apart: 8, of which 5 were waited for; matrix products, arithmetic and copies ran while one was open for 1% of the time, Pallas kernels for 0%

profile of v4, /device:TPU:6, one launch (start us, length us, event | category | flops | bytes accessed | tf_op | source)
XLA Modules:
  0.0 145.3 jit_solution(9937423825199249657)
XLA Ops:
  0.6 0.0 copy-start.3
  0.7 0.9 fusion.7
  1.5 0.0 copy-done.3
  1.5 1.0 pad_maximum_fusion.1
  2.6 6.2 %collective-permute-start.1 = (f32[8,4,1,4,128]{4,3,2,1,0:T(4,128)S(1)}, f32[8,4,1,4,128]{4,3,2,1,0:T(4,128)S(1)}, u32[]{:S(2)}, u32[]{:S(2)}) collective-permute-start(f32[8,4,1,4,128]{4,3,2,1,0:T(4,128)S(1)} %get-tuple-element.8), channel_id=1, source_target_pairs={{1,2},{3,4},{5,6},{2,1},{4,3},{6,5},{9,10},{11,12},{13,14},{10,9},... | collective-permute-start | bytes 196616 | tf_op jit(solution)/shard_map/ppermute | solution.py:468
  8.8 0.0 copy-start.6
  8.8 0.0 copy-start.7
  8.8 0.1 collective-permute-start
  8.9 0.6 copy-done.6
  9.5 0.0 copy-done.7
  9.5 0.1 fusion
  9.6 1.4 collective-permute-done.1
  11.0 2.1 %collective-permute-done = f32[8,4,1,4,128]{4,3,2,1,0:T(4,128)S(1)} collective-permute-done((f32[8,4,1,4,128]{4,3,2,1,0:T(4,128)S(1)}, f32[8,4,1,4,128]{4,3,2,1,0:T(4,128)S(1)}, u32[]{:S(2)}, u32[]{:S(2)}) %collective-permute-start) | collective-permute-done | bytes 65568 | tf_op jit(solution)/shard_map/ppermute | solution.py:469
  13.2 0.0 copy-start.1
  13.2 0.0 copy-start.2
  13.2 0.6 copy-done.1
  13.8 0.0 copy-done.2
  13.8 0.0 copy-start.4
  13.8 0.0 copy-start.5
  13.9 3.5 %collective-permute-start.3 = (f32[8,1,6,4,128]{4,3,2,1,0:T(4,128)S(1)}, f32[8,1,6,4,128]{4,3,2,1,0:T(4,128)S(1)}, u32[]{:S(2)}, u32[]{:S(2)}) collective-permute-start(f32[8,1,6,4,128]{4,3,2,1,0:T(4,128)S(1)} %get-tuple-element.16), channel_id=1, source_target_pairs={{8,16},{24,32},{40,48},{56,64},{72,80},{88,96},{104,112},{16,8},{3... | collective-permute-start | bytes 294920 | tf_op jit(solution)/shard_map/ppermute | solution.py:468
  17.4 0.2 collective-permute-start.2
  17.6 0.0 copy-done.4
  17.6 0.0 copy-done.5
  17.6 0.7 pad_maximum_fusion.local
  18.3 5.1 %collective-permute-done.3 = f32[8,1,6,4,128]{4,3,2,1,0:T(4,128)S(1)} collective-permute-done((f32[8,1,6,4,128]{4,3,2,1,0:T(4,128)S(1)}, f32[8,1,6,4,128]{4,3,2,1,0:T(4,128)S(1)}, u32[]{:S(2)}, u32[]{:S(2)}) %collective-permute-start.3) | collective-permute-done | bytes 98336 | tf_op jit(solution)/shard_map/ppermute | solution.py:468
  23.4 0.0 collective-permute-done.2
  23.4 0.7 broadcast_select_fusion
  24.1 36.9 %moments.1.corr0 = f32[6,64,128]{2,1,0:T(8,128)} custom-call(s32[1600]{0:T(1024)} %constant.37.clone.tab, bf16[32,256]{1,0:T(8,128)(2,1)} %constant.38.clone.spread_ref, f32[8,64,128]{2,1,0:T(8,128)} %pad_maximum_fusion.local, f32[8,16,128]{2,1,0:T(8,128)} %bitcast.38, f32[8,16,128]{2,1,0:T(8,128)} %bitcast.36, f32[8,24,128]{2,1,0:T(8,128)} %bitcast.34, ...), custom_call_target="tpu_custom_call" | custom-call | tf_op jit(solution)/shard_map/moments/pallas_call | solution.py:418
  61.0 0.0 copy-start
  61.0 0.9 fusion.2
  61.9 3.9 %collective-permute-start.5 = (f32[6,4,1,4,128]{4,3,2,0,1:T(4,128)S(1)}, f32[6,4,1,4,128]{4,3,2,0,1:T(4,128)S(1)}, u32[]{:S(2)}, u32[]{:S(2)}) collective-permute-start(f32[6,4,1,4,128]{4,3,2,0,1:T(4,128)S(1)} %get-tuple-element.26), channel_id=1, source_target_pairs={{1,2},{3,4},{5,6},{2,1},{4,3},{6,5},{9,10},{11,12},{13,14},{10,9},... | collective-permute-start | bytes 147464 | tf_op jit(solution)/shard_map/ppermute | solution.py:468
  65.8 0.1 collective-permute-start.4
  65.9 0.0 copy-done
  66.0 4.1 %collective-permute-done.5 = f32[6,4,1,4,128]{4,3,2,0,1:T(4,128)S(1)} collective-permute-done((f32[6,4,1,4,128]{4,3,2,0,1:T(4,128)S(1)}, f32[6,4,1,4,128]{4,3,2,0,1:T(4,128)S(1)}, u32[]{:S(2)}, u32[]{:S(2)}) %collective-permute-start.5) | collective-permute-done | bytes 49184 | tf_op jit(solution)/shard_map/ppermute | solution.py:468
  70.0 0.0 collective-permute-done.4
  70.1 2.3 %collective-permute-start.7 = (f32[6,1,6,4,128]{4,3,2,0,1:T(4,128)S(1)}, f32[6,1,6,4,128]{4,3,2,0,1:T(4,128)S(1)}, u32[]{:S(2)}, u32[]{:S(2)}) collective-permute-start(f32[6,1,6,4,128]{4,3,2,0,1:T(4,128)S(1)} %get-tuple-element.20), channel_id=1, source_target_pairs={{8,16},{24,32},{40,48},{56,64},{72,80},{88,96},{104,112},{16,8},{3... | collective-permute-start | bytes 221192 | tf_op jit(solution)/shard_map/ppermute | solution.py:468
  72.5 0.1 collective-permute-start.6
  72.6 0.6 copy.13
  73.2 0.6 copy.12
  73.8 5.6 %collective-permute-done.7 = f32[6,1,6,4,128]{4,3,2,0,1:T(4,128)S(1)} collective-permute-done((f32[6,1,6,4,128]{4,3,2,0,1:T(4,128)S(1)}, f32[6,1,6,4,128]{4,3,2,0,1:T(4,128)S(1)}, u32[]{:S(2)}, u32[]{:S(2)}) %collective-permute-start.7) | collective-permute-done | bytes 73760 | tf_op jit(solution)/shard_map/ppermute | solution.py:468
  79.4 0.0 collective-permute-done.6
  79.4 0.7 broadcast_select_fusion.4
  80.1 65.2 %rates.1 = (f32[64,128]{1,0:T(8,128)}, f32[3,64,128]{2,1,0:T(8,128)}) custom-call(s32[1600]{0:T(1024)} %constant.37.clone.tab, bf16[32,256]{1,0:T(8,128)(2,1)} %constant.38.clone.spread_ref, f32[8,64,128]{2,1,0:T(8,128)} %pad_maximum_fusion.local, f32[8,16,128]{2,1,0:T(8,128)} %bitcast.39, f32[8,16,128]{2,1,0:T(8,128)} %bitcast.37, f32[8,24,128]{2,1,0:T(8,128)} %bitcast.35, ...), custom_call_target="tpu_custom_call" | custom-call | tf_op jit(solution)/shard_map/rates/pallas_call | solution.py:439
  (11 shorter events, 0.2 us)
Async XLA Ops:
  0.6 0.9 copy-start.3
  2.6 8.4 %collective-permute-start.1 = (f32[8,4,1,4,128]{4,3,2,1,0:T(4,128)S(1)}, f32[8,4,1,4,128]{4,3,2,1,0:T(4,128)S(1)}, u32[]{:S(2)}, u32[]{:S(2)}) collective-permute-start(f32[8,4,1,4,128]{4,3,2,1,0:T(4,128)S(1)} %get-tuple-element.8), channel_id=1, source_target_pairs={{1,2},{3,4},{5,6},{2,1},{4,3},{6,5},{9,10},{11,12},{13,14},{10,9},... | collective-permute-start | bytes 196616 | tf_op jit(solution)/shard_map/ppermute | solution.py:468
  8.8 0.8 copy-start.6
  8.8 0.8 copy-start.7
  8.8 4.3 %collective-permute-start = (f32[8,4,1,4,128]{4,3,2,1,0:T(4,128)S(1)}, f32[8,4,1,4,128]{4,3,2,1,0:T(4,128)S(1)}, u32[]{:S(2)}, u32[]{:S(2)}) collective-permute-start(f32[8,4,1,4,128]{4,3,2,1,0:T(4,128)S(1)} %get-tuple-element.9), channel_id=1, source_target_pairs={{0,1},{1,0},{2,3},{3,2},{4,5},{5,4},{6,7},{7,6},{8,9},{9,8},{10,11... | collective-permute-start | bytes 196616 | tf_op jit(solution)/shard_map/ppermute | solution.py:469
  13.2 0.6 copy-start.1
  13.2 0.6 copy-start.2
  13.8 3.7 %copy-start.4 = (f32[3,4,4,4,128]{4,3,2,1,0:T(4,128)S(1)}, f32[3,4,4,4,128]{4,3,2,1,0:T(4,128)}, u32[]{:S(2)}) copy-start(f32[3,4,4,4,128]{4,3,2,1,0:T(4,128)} %param.8) | copy-start | bytes 294916
  13.8 3.7 %copy-start.5 = (f32[4,4,4,128]{3,2,1,0:T(4,128)S(1)}, f32[4,4,4,128]{3,2,1,0:T(4,128)}, u32[]{:S(2)}) copy-start(f32[4,4,4,128]{3,2,1,0:T(4,128)} %param.10) | copy-start | bytes 98308
  13.9 9.5 %collective-permute-start.3 = (f32[8,1,6,4,128]{4,3,2,1,0:T(4,128)S(1)}, f32[8,1,6,4,128]{4,3,2,1,0:T(4,128)S(1)}, u32[]{:S(2)}, u32[]{:S(2)}) collective-permute-start(f32[8,1,6,4,128]{4,3,2,1,0:T(4,128)S(1)} %get-tuple-element.16), channel_id=1, source_target_pairs={{8,16},{24,32},{40,48},{56,64},{72,80},{88,96},{104,112},{16,8},{3... | collective-permute-start | bytes 294920 | tf_op jit(solution)/shard_map/ppermute | solution.py:468
  17.4 6.1 %collective-permute-start.2 = (f32[8,1,6,4,128]{4,3,2,1,0:T(4,128)S(1)}, f32[8,1,6,4,128]{4,3,2,1,0:T(4,128)S(1)}, u32[]{:S(2)}, u32[]{:S(2)}) collective-permute-start(f32[8,1,6,4,128]{4,3,2,1,0:T(4,128)S(1)} %get-tuple-element.17), channel_id=1, source_target_pairs={{0,8},{8,0},{16,24},{24,16},{32,40},{40,32},{48,56},{56,48},{64,72... | collective-permute-start | bytes 294920 | tf_op jit(solution)/shard_map/ppermute | solution.py:469
  61.0 4.9 %copy-start = (f32[6,64,128]{2,1,0:T(8,128)S(1)}, f32[6,64,128]{2,1,0:T(8,128)}, u32[]{:S(2)}) copy-start(f32[6,64,128]{2,1,0:T(8,128)} %moments.1.corr0) | copy-start | bytes 589828
  61.9 8.1 %collective-permute-start.5 = (f32[6,4,1,4,128]{4,3,2,0,1:T(4,128)S(1)}, f32[6,4,1,4,128]{4,3,2,0,1:T(4,128)S(1)}, u32[]{:S(2)}, u32[]{:S(2)}) collective-permute-start(f32[6,4,1,4,128]{4,3,2,0,1:T(4,128)S(1)} %get-tuple-element.26), channel_id=1, source_target_pairs={{1,2},{3,4},{5,6},{2,1},{4,3},{6,5},{9,10},{11,12},{13,14},{10,9},... | collective-permute-start | bytes 147464 | tf_op jit(solution)/shard_map/ppermute | solution.py:468
  65.8 4.2 %collective-permute-start.4 = (f32[6,4,1,4,128]{4,3,2,0,1:T(4,128)S(1)}, f32[6,4,1,4,128]{4,3,2,0,1:T(4,128)S(1)}, u32[]{:S(2)}, u32[]{:S(2)}) collective-permute-start(f32[6,4,1,4,128]{4,3,2,0,1:T(4,128)S(1)} %get-tuple-element.27), channel_id=1, source_target_pairs={{0,1},{1,0},{2,3},{3,2},{4,5},{5,4},{6,7},{7,6},{8,9},{9,8},{10,11... | collective-permute-start | bytes 147464 | tf_op jit(solution)/shard_map/ppermute | solution.py:469
  70.1 9.3 %collective-permute-start.7 = (f32[6,1,6,4,128]{4,3,2,0,1:T(4,128)S(1)}, f32[6,1,6,4,128]{4,3,2,0,1:T(4,128)S(1)}, u32[]{:S(2)}, u32[]{:S(2)}) collective-permute-start(f32[6,1,6,4,128]{4,3,2,0,1:T(4,128)S(1)} %get-tuple-element.20), channel_id=1, source_target_pairs={{8,16},{24,32},{40,48},{56,64},{72,80},{88,96},{104,112},{16,8},{3... | collective-permute-start | bytes 221192 | tf_op jit(solution)/shard_map/ppermute | solution.py:468
  72.5 6.9 %collective-permute-start.6 = (f32[6,1,6,4,128]{4,3,2,0,1:T(4,128)S(1)}, f32[6,1,6,4,128]{4,3,2,0,1:T(4,128)S(1)}, u32[]{:S(2)}, u32[]{:S(2)}) collective-permute-start(f32[6,1,6,4,128]{4,3,2,0,1:T(4,128)S(1)} %get-tuple-element.21), channel_id=1, source_target_pairs={{0,8},{8,0},{16,24},{24,16},{32,40},{40,32},{48,56},{56,48},{64,72... | collective-permute-start | bytes 221192 | tf_op jit(solution)/shard_map/ppermute | solution.py:469

commit v5 on v4

--- a/solution.py
+++ b/solution.py
@@ -20,7 +20,9 @@
 F32 = jnp.float32
 BF16 = jnp.bfloat16
 LOCAL = 64
-TOTAL = 144
+SPAN = 40
+TOTAL = 4 * SPAN
+ROW = 11
 KA = 80
 M1 = 32
 M2 = 128
@@ -30,32 +32,33 @@
 LEVEL_PAIRS = ((0, 0), (0, 1), (1, 0), (1, 1), (1, 2), (2, 1), (2, 2), (2, 3), (3, 2), (3, 3))
 
 
-def column_bases():
-    base = np.zeros((6, 6), np.int32)
+def column_slots():
+    slot = np.zeros((6, 6), np.int32)
     for a in range(6):
         for b in range(6):
             if a == 0:
-                base[a, b] = 96 + b * 4
+                slot[a, b] = 24 + b
             elif a == 5:
-                base[a, b] = 120 + b * 4
+                slot[a, b] = 30 + b
             elif b == 0:
-                base[a, b] = 64 + (a - 1) * 4
+                slot[a, b] = 16 + a - 1
             elif b == 5:
-                base[a, b] = 80 + (a - 1) * 4
+                slot[a, b] = 20 + a - 1
             else:
-                base[a, b] = ((a - 1) * 4 + (b - 1)) * 4
-    return base
+                slot[a, b] = (a - 1) * 4 + (b - 1)
+    return slot
 
 
 def item_table(columns):
-    base = column_bases()
+    slot = column_slots()
     rows = []
     for c, d in LEVEL_PAIRS:
         for a, b in columns:
-            row = [((a - 1) * 4 + (b - 1)) * 4 + c]
+            row = [c * 16 + slot[a, b]]
             for da in (-1, 0, 1):
                 for db in (-1, 0, 1):
-                    row.append(base[a + da, b + db] + d)
+                    row.append(d * SPAN + slot[a + da, b + db])
+            row.append(c * SPAN + slot[a, b])
             rows.append(row)
     return np.asarray(rows, np.int32).reshape(-1)
 
@@ -83,7 +86,7 @@
     rows_ref[pl.ds(7 * 8, 8), :] = jnp.ones((8, 128), F32)
 
 
-def pair_rows(state, corner, spread, k, with_targets, rows_ref, a_ref, b_ref, rho_ref):
+def pair_rows(state, corner, spread, k, target, rows_ref, a_ref, b_ref, rho_ref):
     blk = pl.ds(pl.multiple_of(k * 8, 8), 8)
     x = [state[d, blk, :] - corner[d] for d in range(3)]
     v = [state[3 + d, blk, :] for d in range(3)]
@@ -103,7 +106,7 @@
     for s in range(3):
         put(s, 0, [xs[d][s] for d in range(3)] + [vs[d][s] for d in range(3)] + [rs[s]])
     put(3, 0, n2s + xvs)
-    if with_targets:
+    if target is not None:
         for s in range(3):
             put(4 + s, 0, [-0.5 * xs[d][s] for d in range(3)])
             put(4 + s, 7, [0.25 * n2s[s]])
@@ -120,34 +123,62 @@
         a_ref[k * 8 + b] = both[rows, :KA].astype(BF16)
         if rho_ref is not None:
             rho_ref[k * 8 + b] = both[rows, 128:]
-        if with_targets:
+        if target is not None:
             r2_rows = [get(4 + s, b) for s in range(3)] * 3
-            b_ref[k * 8 + b, :, :128] = jnp.concatenate(r2_rows + [quarters], 0).astype(BF16)
+            b_ref[target * 8 + b, :, :128] = jnp.concatenate(r2_rows + [quarters], 0).astype(BF16)
             if rho_ref is not None:
                 vx_rows = [get(7 + s, b) for s in range(3)] * 3
-                b_ref[k * 8 + b, :, 128:] = jnp.concatenate(vx_rows + [ones], 0).astype(BF16)
-
-
-def gather_blocks(parts, state):
-    at = 0
-    for part in parts:
-        for k in range(part.shape[1] // 8):
-            yield part, pl.ds(k * 8, 8), pl.ds(at, 8)
-            at += 8
+                b_ref[target * 8 + b, :, 128:] = jnp.concatenate(vx_rows + [ones], 0).astype(BF16)
+
+
+def by_level(parts):
+    for level in range(4):
+        at = level * SPAN
+        for part in parts:
+            columns = part.shape[1] // 4
+            for first in range(0, columns, 8):
+                width = min(8, columns - first)
+                src = pl.ds(first * 4 + level, width, stride=4)
+                yield part, src, pl.ds(at, width), level
+                at += width
 
 
 def load_state(parts, state):
-    peak = jnp.zeros((8, 128), F32)
-    for part, src, dst in gather_blocks(parts, state):
+    for d in range(8):
+        for level in range(4):
+            pad = pl.ds(level * SPAN + 36, 4)
+            state[d, pad, :] = jnp.full((4, 128), 1.0 if d == 6 else 0.0, F32)
+    peak = {}
+    for part, src, dst, level in by_level(parts):
         mass = part[7, src, :]
         live = mass > 0.0
         for d in range(6):
             state[d, dst, :] = jnp.where(live, part[d, src, :], 0.0)
         state[6, dst, :] = jnp.where(live, part[6, src, :], 1.0)
         state[7, dst, :] = mass
-        peak = jnp.maximum(peak, mass)
-    level = (lax.broadcasted_iota(jnp.int32, (8, 128), 0) % 4 + 1).astype(F32)
-    return jnp.max(jnp.where(peak > 0.0, level, 1.0)).astype(jnp.int32)
+        height = jnp.where(live, level + 1.0, 1.0)
+        peak[height.shape] = jnp.maximum(peak[height.shape], height) if height.shape in peak else height
+    tops = [jnp.max(p) for p in peak.values()]
+    return functools.reduce(jnp.maximum, tops).astype(jnp.int32)
+
+
+def for_chunks(levels, prepare):
+    def first(q, carry):
+        prepare(lax.div(q, 2) * 5 + lax.rem(q, 2), q)
+        return carry
+
+    def others(q, carry):
+        prepare(lax.div(q, 3) * 5 + 2 + lax.rem(q, 3), None)
+        return carry
+
+    lax.fori_loop(0, 2 * levels, first, 0)
+    lax.fori_loop(0, 3 * levels, others, 0)
+
+
+def target_chunk(q):
+    level, half = lax.div(q, 2), lax.rem(q, 2)
+    blk = pl.ds(pl.multiple_of((level * 5 + half) * 8, 8), 8)
+    return blk, pl.ds(half * 32 + level, 8, stride=4)
 
 
 def centre():
@@ -209,8 +240,8 @@
     fixed_rows(rows_ref)
     feat_ref[...] = jnp.zeros_like(feat_ref)
 
-    def prepare(k, with_targets):
-        pair_rows(state, corner, spread, k, with_targets, rows_ref, a_ref, b_ref, None)
+    def prepare(k, target):
+        pair_rows(state, corner, spread, k, target, rows_ref, a_ref, b_ref, None)
         blk = pl.ds(pl.multiple_of(k * 8, 8), 8)
         x = [state[d, blk, :] - corner[d] for d in range(3)]
         vol = state[7, blk, :] / state[6, blk, :]
@@ -219,27 +250,19 @@
         store_features(feat_ref, features, 0)
         gather_features(feat_ref, f_ref, k, M1)
 
-    def first(k, carry):
-        prepare(k, True)
-        return carry
-
-    def others(k, carry):
-        prepare(k, False)
-        return carry
-
-    lax.fori_loop(0, LOCAL // 8, first, 0)
-    lax.fori_loop(LOCAL // 8, TOTAL // 8, others, 0)
+    for_chunks(levels, prepare)
     acc[...] = jnp.zeros_like(acc)
+    corr[...] = jnp.zeros_like(corr)
 
     def one(t, p):
         for c in CHUNKS:
-            lhs = jnp.concatenate([a_ref[tab[t * 10 + 1 + e]] for e in range(*c)], 0)
+            lhs = jnp.concatenate([a_ref[tab[t * ROW + 1 + e]] for e in range(*c)], 0)
             rows = pl.ds(c[0] * 128, (c[1] - c[0]) * 128)
-            r_ref[p, rows, :] = jnp.dot(lhs, b_ref[tab[t * 10]], preferred_element_type=F32)
+            r_ref[p, rows, :] = jnp.dot(lhs, b_ref[tab[t * ROW]], preferred_element_type=F32)
 
     def rest(t, p):
-        i = tab[t * 10]
-        partner = [tab[t * 10 + 1 + e] for e in range(NB)]
+        i = tab[t * ROW]
+        partner = [tab[t * ROW + 1 + e] for e in range(NB)]
         weights = []
         for c in CHUNKS:
             s2 = jnp.maximum(r_ref[p, pl.ds(c[0] * 128, (c[1] - c[0]) * 128), :], TINY)
@@ -252,7 +275,7 @@
 
     def finish(k, carry):
         unfold(acc, M1, k, feat_ref)
-        blk = pl.ds(pl.multiple_of(k * 8, 8), 8)
+        blk, out = target_chunk(k)
         x = [state[d, blk, :] - corner[d] for d in range(3)]
 
         def total(f):
@@ -275,10 +298,10 @@
         cof_zz = a * d - b * b
         scale = 1.0 / (a * cof_xx + b * cof_xy + c * cof_xz)
         for r, cof in enumerate((cof_xx, cof_yy, cof_zz, cof_xy, cof_xz, cof_yz)):
-            corr[r, blk, :] = cof * scale
+            corr[r, out, :] = cof * scale
         return carry
 
-    lax.fori_loop(0, LOCAL // 8, finish, 0)
+    lax.fori_loop(0, 2 * levels, finish, 0)
 
 
 def rate_kernel(tab, spread_ref, local, low_y, high_y, low_x, high_x, corr0, corr1, corr2, corr3, corr4, rate, accel,
@@ -289,7 +312,10 @@
     spread = spread_ref[...]
     fixed_rows(rows_ref)
     feat_ref[...] = jnp.zeros_like(feat_ref)
-    for part, src, dst in gather_blocks((corr0, corr1, corr2, corr3, corr4), corr):
+    for d in range(6):
+        for level in range(4):
+            corr[d, pl.ds(level * SPAN + 36, 4), :] = jnp.zeros((4, 128), F32)
+    for part, src, dst, level in by_level((corr0, corr1, corr2, corr3, corr4)):
         for d in range(6):
             corr[d, dst, :] = part[d, src, :]
 
@@ -301,8 +327,8 @@
         return [sym[SYM_INDEX[p][0]] * vec[0] + sym[SYM_INDEX[p][1]] * vec[1] + sym[SYM_INDEX[p][2]] * vec[2]
                 for p in range(3)]
 
-    def prepare(k, with_targets):
-        pair_rows(state, corner, spread, k, with_targets, rows_ref, a_ref, b_ref, rho_ref)
+    def prepare(k, target):
+        pair_rows(state, corner, spread, k, target, rows_ref, a_ref, b_ref, rho_ref)
         blk = pl.ds(pl.multiple_of(k * 8, 8), 8)
         x = [state[d, blk, :] - corner[d] for d in range(3)]
         v = [state[3 + d, blk, :] for d in range(3)]
@@ -323,29 +349,22 @@
         store_features(feat_ref, own, W_ROWS)
         gather_features(feat_ref, f_ref, k, M2)
 
-    def first(k, carry):
-        prepare(k, True)
-        return carry
-
-    def others(k, carry):
-        prepare(k, False)
-        return carry
-
-    lax.fori_loop(0, LOCAL // 8, first, 0)
-    lax.fori_loop(LOCAL // 8, TOTAL // 8, others, 0)
+    for_chunks(levels, prepare)
     acc[...] = jnp.zeros_like(acc)
+    rate[...] = jnp.zeros_like(rate)
+    accel[...] = jnp.zeros_like(accel)
     accw[...] = jnp.zeros_like(accw)
 
     def one(t, p):
         for c in CHUNKS:
-            lhs = jnp.concatenate([a_ref[tab[t * 10 + 1 + e]] for e in range(*c)], 0)
+            lhs = jnp.concatenate([a_ref[tab[t * ROW + 1 + e]] for e in range(*c)], 0)
             rows = pl.ds(c[0] * 128, (c[1] - c[0]) * 128)
-            r_ref[p, rows, :] = jnp.dot(lhs, b_ref[tab[t * 10]], preferred_element_type=F32)
+            r_ref[p, rows, :] = jnp.dot(lhs, b_ref[tab[t * ROW]], preferred_element_type=F32)
 
     def rest(t, p):
-        i = tab[t * 10]
-        partner = [tab[t * 10 + 1 + e] for e in range(NB)]
-        rho_i = state[6, pl.ds(i, 1), :]
+        i = tab[t * ROW]
+        partner = [tab[t * ROW + 1 + e] for e in range(NB)]
+        rho_i = state[6, pl.ds(tab[t * ROW + 10], 1), :]
         weights = []
         viscous = []
         for c in CHUNKS:
@@ -368,7 +387,7 @@
     def finish(k, carry):
         unfold(acc, M2, k, feat_ref)
         unfold(accw, MW, k, featw_ref)
-        blk = pl.ds(pl.multiple_of(k * 8, 8), 8)
+        blk, out = target_chunk(k)
         x = [state[d, blk, :] - corner[d] for d in range(3)]
         v = [state[3 + d, blk, :] for d in range(3)]
         prs = pressure(state[6, blk, :])
@@ -395,7 +414,7 @@
             inner = inner + v[p] * (mk_x[p] - mkx[p]) - x[p] * mkv[p]
         inner = inner + mvkx
         live = state[7, blk, :] > 0.0
-        rate[blk, :] = jnp.where(live, (-0.5 * KERNEL_GRAD) * inner, 0.0)
+        rate[out, :] = jnp.where(live, (-0.5 * KERNEL_GRAD) * inner, 0.0)
         near = [prs * (x[p] * m0 - mx[p]) + (x[p] * p0 - px[p]) - 0.25 * (x[p] * w0 - wx[p]) for p in range(3)]
         mine = times(sym, near)
         pk_x = times(pk, x)
@@ -403,10 +422,10 @@
         for p in range(3):
             far = prs * (mk_x[p] - mkx[p]) + (pk_x[p] - pkx[p]) - 0.25 * (wk_x[p] - wkx[p])
             pull = -GRAVITY if p == 2 else 0.0
-            accel[p, blk, :] = jnp.where(live, (0.5 * KERNEL_GRAD) * (mine[p] + far) + pull, 0.0)
+            accel[p, out, :] = jnp.where(live, (0.5 * KERNEL_GRAD) * (mine[p] + far) + pull, 0.0)
         return carry
 
-    lax.fori_loop(0, LOCAL // 8, finish, 0)
+    lax.fori_loop(0, 2 * levels, finish, 0)
 
 
 VMEM = pl.BlockSpec(memory_space=pltpu.VMEM)

time: 146 us -> 143 us (0.979)
  Pallas kernels: 102 us -> 99.7 us
where the time goes in v5:
time: 143 us
  Pallas kernels  99.7 us (70%)
  waiting for transfers between devices  18.3 us (13%)
  starting transfers between devices  16.4 us (11%)
  other arithmetic  4.19 us (3%)
  local copies, waits for them, and re-layouts  3.43 us (2%)
    pallas_call x1, Pallas kernels, run_rates(): pl.pallas_call(rate_kernel, out_shape=(jax.ShapeDtypeStruct((LOCAL, 128),...  64.2 us
    pallas_call x1, Pallas kernels, run_moments(): pl.pallas_call(moment_kernel, out_shape=jax.ShapeDtypeStruct((6, LOCAL, 1...  35.5 us
    ppermute x4, waiting for transfers between devices, exchange(): across = lax.ppermute(jnp.where(odd, last, first), axis, outer)  16.2 us
    ppermute x4, starting transfers between devices, exchange(): across = lax.ppermute(jnp.where(odd, last, first), axis, outer)  15.9 us
  transfers between devices with their start and end apart: 8, of which 5 were waited for; matrix products, arithmetic and copies ran while one was open for 1% of the time, Pallas kernels for 0%

profile of v5, /device:TPU:6, one launch (start us, length us, event | category | flops | bytes accessed | tf_op | source)
XLA Modules:
  0.0 142.9 jit_solution(3197579908723895794)
XLA Ops:
  0.6 0.0 copy-start.3
  0.7 0.9 fusion.7
  1.5 0.0 copy-done.3
  1.5 1.0 pad_maximum_fusion.1
  2.6 6.2 %collective-permute-start.1 = (f32[8,4,1,4,128]{4,3,2,1,0:T(4,128)S(1)}, f32[8,4,1,4,128]{4,3,2,1,0:T(4,128)S(1)}, u32[]{:S(2)}, u32[]{:S(2)}) collective-permute-start(f32[8,4,1,4,128]{4,3,2,1,0:T(4,128)S(1)} %get-tuple-element.8), channel_id=1, source_target_pairs={{1,2},{3,4},{5,6},{2,1},{4,3},{6,5},{9,10},{11,12},{13,14},{10,9},... | collective-permute-start | bytes 196616 | tf_op jit(solution)/shard_map/ppermute | solution.py:487
  8.8 0.0 copy-start.6
  8.8 0.0 copy-start.7
  8.8 0.1 collective-permute-start
  8.9 0.6 copy-done.6
  9.5 0.0 copy-done.7
  9.5 0.1 fusion
  9.6 1.4 collective-permute-done.1
  11.0 2.1 %collective-permute-done = f32[8,4,1,4,128]{4,3,2,1,0:T(4,128)S(1)} collective-permute-done((f32[8,4,1,4,128]{4,3,2,1,0:T(4,128)S(1)}, f32[8,4,1,4,128]{4,3,2,1,0:T(4,128)S(1)}, u32[]{:S(2)}, u32[]{:S(2)}) %collective-permute-start) | collective-permute-done | bytes 65568 | tf_op jit(solution)/shard_map/ppermute | solution.py:488
  13.2 0.0 copy-start.1
  13.2 0.0 copy-start.2
  13.2 0.6 copy-done.1
  13.8 0.0 copy-done.2
  13.8 0.0 copy-start.4
  13.8 0.0 copy-start.5
  13.9 3.5 %collective-permute-start.3 = (f32[8,1,6,4,128]{4,3,2,1,0:T(4,128)S(1)}, f32[8,1,6,4,128]{4,3,2,1,0:T(4,128)S(1)}, u32[]{:S(2)}, u32[]{:S(2)}) collective-permute-start(f32[8,1,6,4,128]{4,3,2,1,0:T(4,128)S(1)} %get-tuple-element.16), channel_id=1, source_target_pairs={{8,16},{24,32},{40,48},{56,64},{72,80},{88,96},{104,112},{16,8},{3... | collective-permute-start | bytes 294920 | tf_op jit(solution)/shard_map/ppermute | solution.py:487
  17.4 0.2 collective-permute-start.2
  17.6 0.0 copy-done.4
  17.6 0.0 copy-done.5
  17.6 0.7 pad_maximum_fusion.local
  18.3 5.1 %collective-permute-done.3 = f32[8,1,6,4,128]{4,3,2,1,0:T(4,128)S(1)} collective-permute-done((f32[8,1,6,4,128]{4,3,2,1,0:T(4,128)S(1)}, f32[8,1,6,4,128]{4,3,2,1,0:T(4,128)S(1)}, u32[]{:S(2)}, u32[]{:S(2)}) %collective-permute-start.3) | collective-permute-done | bytes 98336 | tf_op jit(solution)/shard_map/ppermute | solution.py:487
  23.4 0.0 collective-permute-done.2
  23.4 0.7 broadcast_select_fusion
  24.1 35.5 %moments.1.corr0 = f32[6,64,128]{2,1,0:T(8,128)} custom-call(s32[1760]{0:T(1024)} %constant.37.clone.tab, bf16[32,256]{1,0:T(8,128)(2,1)} %constant.38.clone.spread_ref, f32[8,64,128]{2,1,0:T(8,128)} %pad_maximum_fusion.local, f32[8,16,128]{2,1,0:T(8,128)} %bitcast.38, f32[8,16,128]{2,1,0:T(8,128)} %bitcast.36, f32[8,24,128]{2,1,0:T(8,128)} %bitcast.34, ...), custom_call_target="tpu_custom_call" | custom-call | tf_op jit(solution)/shard_map/moments/pallas_call | solution.py:437
  59.6 0.0 copy-start
  59.6 0.9 fusion.2
  60.5 3.9 %collective-permute-start.5 = (f32[6,4,1,4,128]{4,3,2,0,1:T(4,128)S(1)}, f32[6,4,1,4,128]{4,3,2,0,1:T(4,128)S(1)}, u32[]{:S(2)}, u32[]{:S(2)}) collective-permute-start(f32[6,4,1,4,128]{4,3,2,0,1:T(4,128)S(1)} %get-tuple-element.26), channel_id=1, source_target_pairs={{1,2},{3,4},{5,6},{2,1},{4,3},{6,5},{9,10},{11,12},{13,14},{10,9},... | collective-permute-start | bytes 147464 | tf_op jit(solution)/shard_map/ppermute | solution.py:487
  64.5 0.1 collective-permute-start.4
  64.5 0.0 copy-done
  64.6 4.1 %collective-permute-done.5 = f32[6,4,1,4,128]{4,3,2,0,1:T(4,128)S(1)} collective-permute-done((f32[6,4,1,4,128]{4,3,2,0,1:T(4,128)S(1)}, f32[6,4,1,4,128]{4,3,2,0,1:T(4,128)S(1)}, u32[]{:S(2)}, u32[]{:S(2)}) %collective-permute-start.5) | collective-permute-done | bytes 49184 | tf_op jit(solution)/shard_map/ppermute | solution.py:487
  68.6 0.0 collective-permute-done.4
  68.7 2.3 %collective-permute-start.7 = (f32[6,1,6,4,128]{4,3,2,0,1:T(4,128)S(1)}, f32[6,1,6,4,128]{4,3,2,0,1:T(4,128)S(1)}, u32[]{:S(2)}, u32[]{:S(2)}) collective-permute-start(f32[6,1,6,4,128]{4,3,2,0,1:T(4,128)S(1)} %get-tuple-element.20), channel_id=1, source_target_pairs={{8,16},{24,32},{40,48},{56,64},{72,80},{88,96},{104,112},{16,8},{3... | collective-permute-start | bytes 221192 | tf_op jit(solution)/shard_map/ppermute | solution.py:487
  71.1 0.1 collective-permute-start.6
  71.2 0.6 copy.13
  71.8 0.6 copy.12
  72.4 5.6 %collective-permute-done.7 = f32[6,1,6,4,128]{4,3,2,0,1:T(4,128)S(1)} collective-permute-done((f32[6,1,6,4,128]{4,3,2,0,1:T(4,128)S(1)}, f32[6,1,6,4,128]{4,3,2,0,1:T(4,128)S(1)}, u32[]{:S(2)}, u32[]{:S(2)}) %collective-permute-start.7) | collective-permute-done | bytes 73760 | tf_op jit(solution)/shard_map/ppermute | solution.py:487
  78.0 0.0 collective-permute-done.6
  78.0 0.7 broadcast_select_fusion.4
  78.7 64.2 %rates.1 = (f32[64,128]{1,0:T(8,128)}, f32[3,64,128]{2,1,0:T(8,128)}) custom-call(s32[1760]{0:T(1024)} %constant.37.clone.tab, bf16[32,256]{1,0:T(8,128)(2,1)} %constant.38.clone.spread_ref, f32[8,64,128]{2,1,0:T(8,128)} %pad_maximum_fusion.local, f32[8,16,128]{2,1,0:T(8,128)} %bitcast.39, f32[8,16,128]{2,1,0:T(8,128)} %bitcast.37, f32[8,24,128]{2,1,0:T(8,128)} %bitcast.35, ...), custom_call_target="tpu_custom_call" | custom-call | tf_op jit(solution)/shard_map/rates/pallas_call | solution.py:458
  (11 shorter events, 0.2 us)
Async XLA Ops:
  0.6 0.9 copy-start.3
  2.6 8.4 %collective-permute-start.1 = (f32[8,4,1,4,128]{4,3,2,1,0:T(4,128)S(1)}, f32[8,4,1,4,128]{4,3,2,1,0:T(4,128)S(1)}, u32[]{:S(2)}, u32[]{:S(2)}) collective-permute-start(f32[8,4,1,4,128]{4,3,2,1,0:T(4,128)S(1)} %get-tuple-element.8), channel_id=1, source_target_pairs={{1,2},{3,4},{5,6},{2,1},{4,3},{6,5},{9,10},{11,12},{13,14},{10,9},... | collective-permute-start | bytes 196616 | tf_op jit(solution)/shard_map/ppermute | solution.py:487
  8.8 0.8 copy-start.6
  8.8 0.8 copy-start.7
  8.8 4.3 %collective-permute-start = (f32[8,4,1,4,128]{4,3,2,1,0:T(4,128)S(1)}, f32[8,4,1,4,128]{4,3,2,1,0:T(4,128)S(1)}, u32[]{:S(2)}, u32[]{:S(2)}) collective-permute-start(f32[8,4,1,4,128]{4,3,2,1,0:T(4,128)S(1)} %get-tuple-element.9), channel_id=1, source_target_pairs={{0,1},{1,0},{2,3},{3,2},{4,5},{5,4},{6,7},{7,6},{8,9},{9,8},{10,11... | collective-permute-start | bytes 196616 | tf_op jit(solution)/shard_map/ppermute | solution.py:488
  13.2 0.6 copy-start.1
  13.2 0.6 copy-start.2
  13.8 3.7 %copy-start.4 = (f32[3,4,4,4,128]{4,3,2,1,0:T(4,128)S(1)}, f32[3,4,4,4,128]{4,3,2,1,0:T(4,128)}, u32[]{:S(2)}) copy-start(f32[3,4,4,4,128]{4,3,2,1,0:T(4,128)} %param.8) | copy-start | bytes 294916
  13.8 3.7 %copy-start.5 = (f32[4,4,4,128]{3,2,1,0:T(4,128)S(1)}, f32[4,4,4,128]{3,2,1,0:T(4,128)}, u32[]{:S(2)}) copy-start(f32[4,4,4,128]{3,2,1,0:T(4,128)} %param.10) | copy-start | bytes 98308
  13.9 9.5 %collective-permute-start.3 = (f32[8,1,6,4,128]{4,3,2,1,0:T(4,128)S(1)}, f32[8,1,6,4,128]{4,3,2,1,0:T(4,128)S(1)}, u32[]{:S(2)}, u32[]{:S(2)}) collective-permute-start(f32[8,1,6,4,128]{4,3,2,1,0:T(4,128)S(1)} %get-tuple-element.16), channel_id=1, source_target_pairs={{8,16},{24,32},{40,48},{56,64},{72,80},{88,96},{104,112},{16,8},{3... | collective-permute-start | bytes 294920 | tf_op jit(solution)/shard_map/ppermute | solution.py:487
  17.4 6.1 %collective-permute-start.2 = (f32[8,1,6,4,128]{4,3,2,1,0:T(4,128)S(1)}, f32[8,1,6,4,128]{4,3,2,1,0:T(4,128)S(1)}, u32[]{:S(2)}, u32[]{:S(2)}) collective-permute-start(f32[8,1,6,4,128]{4,3,2,1,0:T(4,128)S(1)} %get-tuple-element.17), channel_id=1, source_target_pairs={{0,8},{8,0},{16,24},{24,16},{32,40},{40,32},{48,56},{56,48},{64,72... | collective-permute-start | bytes 294920 | tf_op jit(solution)/shard_map/ppermute | solution.py:488
  59.6 4.9 %copy-start = (f32[6,64,128]{2,1,0:T(8,128)S(1)}, f32[6,64,128]{2,1,0:T(8,128)}, u32[]{:S(2)}) copy-start(f32[6,64,128]{2,1,0:T(8,128)} %moments.1.corr0) | copy-start | bytes 589828
  60.5 8.1 %collective-permute-start.5 = (f32[6,4,1,4,128]{4,3,2,0,1:T(4,128)S(1)}, f32[6,4,1,4,128]{4,3,2,0,1:T(4,128)S(1)}, u32[]{:S(2)}, u32[]{:S(2)}) collective-permute-start(f32[6,4,1,4,128]{4,3,2,0,1:T(4,128)S(1)} %get-tuple-element.26), channel_id=1, source_target_pairs={{1,2},{3,4},{5,6},{2,1},{4,3},{6,5},{9,10},{11,12},{13,14},{10,9},... | collective-permute-start | bytes 147464 | tf_op jit(solution)/shard_map/ppermute | solution.py:487
  64.5 4.2 %collective-permute-start.4 = (f32[6,4,1,4,128]{4,3,2,0,1:T(4,128)S(1)}, f32[6,4,1,4,128]{4,3,2,0,1:T(4,128)S(1)}, u32[]{:S(2)}, u32[]{:S(2)}) collective-permute-start(f32[6,4,1,4,128]{4,3,2,0,1:T(4,128)S(1)} %get-tuple-element.27), channel_id=1, source_target_pairs={{0,1},{1,0},{2,3},{3,2},{4,5},{5,4},{6,7},{7,6},{8,9},{9,8},{10,11... | collective-permute-start | bytes 147464 | tf_op jit(solution)/shard_map/ppermute | solution.py:488
  68.7 9.3 %collective-permute-start.7 = (f32[6,1,6,4,128]{4,3,2,0,1:T(4,128)S(1)}, f32[6,1,6,4,128]{4,3,2,0,1:T(4,128)S(1)}, u32[]{:S(2)}, u32[]{:S(2)}) collective-permute-start(f32[6,1,6,4,128]{4,3,2,0,1:T(4,128)S(1)} %get-tuple-element.20), channel_id=1, source_target_pairs={{8,16},{24,32},{40,48},{56,64},{72,80},{88,96},{104,112},{16,8},{3... | collective-permute-start | bytes 221192 | tf_op jit(solution)/shard_map/ppermute | solution.py:487
  71.1 6.9 %collective-permute-start.6 = (f32[6,1,6,4,128]{4,3,2,0,1:T(4,128)S(1)}, f32[6,1,6,4,128]{4,3,2,0,1:T(4,128)S(1)}, u32[]{:S(2)}, u32[]{:S(2)}) collective-permute-start(f32[6,1,6,4,128]{4,3,2,0,1:T(4,128)S(1)} %get-tuple-element.21), channel_id=1, source_target_pairs={{0,8},{8,0},{16,24},{24,16},{32,40},{40,32},{48,56},{56,48},{64,72... | collective-permute-start | bytes 221192 | tf_op jit(solution)/shard_map/ppermute | solution.py:488

commit v6 on v5

--- a/solution.py
+++ b/solution.py
@@ -214,7 +214,7 @@
     return q * q * q
 
 
-CHUNKS = ((0, 2), (2, 4), (4, 6), (6, 8), (8, 9))
+CHUNKS = ((0, NB),)
 
 
 def for_items(n, width, one, rest):

time: 143 us -> 135 us (0.944)
  Pallas kernels: 99.7 us -> 91.4 us
    pallas_call x1, Pallas kernels: 64.2 us -> 59.6 us  [run_rates(): pl.pallas_call(rate_kernel, out_shape=(jax.ShapeDtypeStruct((LOCAL, 128),...]
    pallas_call x1, Pallas kernels: 35.5 us -> 31.7 us  [run_moments(): pl.pallas_call(moment_kernel, out_shape=jax.ShapeDtypeStruct((6, LOCAL, 1...]
  transfers between devices with their start and end apart: 8 -> 8, of which waited for: 5 -> 5; matrix products, arithmetic and copies ran while one was open for 1% -> 2% of each run, Pallas kernels for 0% -> 0%
where the time goes in v6:
time: 135 us
  Pallas kernels  91.4 us (68%)
  waiting for transfers between devices  18.3 us (14%)
  starting transfers between devices  16.4 us (12%)
  other arithmetic  4.19 us (3%)
  local copies, waits for them, and re-layouts  3.43 us (3%)
    pallas_call x1, Pallas kernels, run_rates(): pl.pallas_call(rate_kernel, out_shape=(jax.ShapeDtypeStruct((LOCAL, 128),...  59.6 us
    pallas_call x1, Pallas kernels, run_moments(): pl.pallas_call(moment_kernel, out_shape=jax.ShapeDtypeStruct((6, LOCAL, 1...  31.7 us
    ppermute x4, waiting for transfers between devices, exchange(): across = lax.ppermute(jnp.where(odd, last, first), axis, outer)  16.2 us
    ppermute x4, starting transfers between devices, exchange(): across = lax.ppermute(jnp.where(odd, last, first), axis, outer)  15.9 us
  transfers between devices with their start and end apart: 8, of which 5 were waited for; matrix products, arithmetic and copies ran while one was open for 2% of the time, Pallas kernels for 0%

profile of v6, /device:TPU:6, one launch (start us, length us, event | category | flops | bytes accessed | tf_op | source)
XLA Modules:
  0.0 134.5 jit_solution(13927185412833259574)
XLA Ops:
  0.6 0.0 copy-start.3
  0.7 0.9 fusion.7
  1.5 0.0 copy-done.3
  1.5 1.0 pad_maximum_fusion.1
  2.6 6.2 %collective-permute-start.1 = (f32[8,4,1,4,128]{4,3,2,1,0:T(4,128)S(1)}, f32[8,4,1,4,128]{4,3,2,1,0:T(4,128)S(1)}, u32[]{:S(2)}, u32[]{:S(2)}) collective-permute-start(f32[8,4,1,4,128]{4,3,2,1,0:T(4,128)S(1)} %get-tuple-element.8), channel_id=1, source_target_pairs={{1,2},{3,4},{5,6},{2,1},{4,3},{6,5},{9,10},{11,12},{13,14},{10,9},... | collective-permute-start | bytes 196616 | tf_op jit(solution)/shard_map/ppermute | solution.py:487
  8.8 0.0 copy-start.6
  8.8 0.0 copy-start.7
  8.8 0.1 collective-permute-start
  8.9 0.6 copy-done.6
  9.5 0.0 copy-done.7
  9.5 0.1 fusion
  9.6 1.4 %collective-permute-done.1 = f32[8,4,1,4,128]{4,3,2,1,0:T(4,128)S(1)} collective-permute-done((f32[8,4,1,4,128]{4,3,2,1,0:T(4,128)S(1)}, f32[8,4,1,4,128]{4,3,2,1,0:T(4,128)S(1)}, u32[]{:S(2)}, u32[]{:S(2)}) %collective-permute-start.1) | collective-permute-done | bytes 65568 | tf_op jit(solution)/shard_map/ppermute | solution.py:487
  11.0 2.1 %collective-permute-done = f32[8,4,1,4,128]{4,3,2,1,0:T(4,128)S(1)} collective-permute-done((f32[8,4,1,4,128]{4,3,2,1,0:T(4,128)S(1)}, f32[8,4,1,4,128]{4,3,2,1,0:T(4,128)S(1)}, u32[]{:S(2)}, u32[]{:S(2)}) %collective-permute-start) | collective-permute-done | bytes 65568 | tf_op jit(solution)/shard_map/ppermute | solution.py:488
  13.2 0.0 copy-start.1
  13.2 0.0 copy-start.2
  13.2 0.6 copy-done.1
  13.8 0.0 copy-done.2
  13.8 0.0 copy-start.4
  13.8 0.0 copy-start.5
  13.9 3.5 %collective-permute-start.3 = (f32[8,1,6,4,128]{4,3,2,1,0:T(4,128)S(1)}, f32[8,1,6,4,128]{4,3,2,1,0:T(4,128)S(1)}, u32[]{:S(2)}, u32[]{:S(2)}) collective-permute-start(f32[8,1,6,4,128]{4,3,2,1,0:T(4,128)S(1)} %get-tuple-element.16), channel_id=1, source_target_pairs={{8,16},{24,32},{40,48},{56,64},{72,80},{88,96},{104,112},{16,8},{3... | collective-permute-start | bytes 294920 | tf_op jit(solution)/shard_map/ppermute | solution.py:487
  17.4 0.2 collective-permute-start.2
  17.6 0.0 copy-done.4
  17.6 0.0 copy-done.5
  17.6 0.7 pad_maximum_fusion.local
  18.3 5.1 %collective-permute-done.3 = f32[8,1,6,4,128]{4,3,2,1,0:T(4,128)S(1)} collective-permute-done((f32[8,1,6,4,128]{4,3,2,1,0:T(4,128)S(1)}, f32[8,1,6,4,128]{4,3,2,1,0:T(4,128)S(1)}, u32[]{:S(2)}, u32[]{:S(2)}) %collective-permute-start.3) | collective-permute-done | bytes 98336 | tf_op jit(solution)/shard_map/ppermute | solution.py:487
  23.4 0.0 collective-permute-done.2
  23.4 0.7 broadcast_select_fusion
  24.1 31.7 %moments.1.corr0 = f32[6,64,128]{2,1,0:T(8,128)} custom-call(s32[1760]{0:T(1024)} %constant.37.clone.tab, bf16[32,256]{1,0:T(8,128)(2,1)} %constant.38.clone.spread_ref, f32[8,64,128]{2,1,0:T(8,128)} %pad_maximum_fusion.local, f32[8,16,128]{2,1,0:T(8,128)} %bitcast.38, f32[8,16,128]{2,1,0:T(8,128)} %bitcast.36, f32[8,24,128]{2,1,0:T(8,128)} %bitcast.34, ...), custom_call_target="tpu_custom_call" | custom-call | tf_op jit(solution)/shard_map/moments/pallas_call | solution.py:437
  55.9 0.0 copy-start
  55.9 0.9 fusion.2
  56.8 3.9 %collective-permute-start.5 = (f32[6,4,1,4,128]{4,3,2,0,1:T(4,128)S(1)}, f32[6,4,1,4,128]{4,3,2,0,1:T(4,128)S(1)}, u32[]{:S(2)}, u32[]{:S(2)}) collective-permute-start(f32[6,4,1,4,128]{4,3,2,0,1:T(4,128)S(1)} %get-tuple-element.26), channel_id=1, source_target_pairs={{1,2},{3,4},{5,6},{2,1},{4,3},{6,5},{9,10},{11,12},{13,14},{10,9},... | collective-permute-start | bytes 147464 | tf_op jit(solution)/shard_map/ppermute | solution.py:487
  60.7 0.1 collective-permute-start.4
  60.8 0.0 copy-done
  60.8 4.1 %collective-permute-done.5 = f32[6,4,1,4,128]{4,3,2,0,1:T(4,128)S(1)} collective-permute-done((f32[6,4,1,4,128]{4,3,2,0,1:T(4,128)S(1)}, f32[6,4,1,4,128]{4,3,2,0,1:T(4,128)S(1)}, u32[]{:S(2)}, u32[]{:S(2)}) %collective-permute-start.5) | collective-permute-done | bytes 49184 | tf_op jit(solution)/shard_map/ppermute | solution.py:487
  64.9 0.0 collective-permute-done.4
  65.0 2.3 %collective-permute-start.7 = (f32[6,1,6,4,128]{4,3,2,0,1:T(4,128)S(1)}, f32[6,1,6,4,128]{4,3,2,0,1:T(4,128)S(1)}, u32[]{:S(2)}, u32[]{:S(2)}) collective-permute-start(f32[6,1,6,4,128]{4,3,2,0,1:T(4,128)S(1)} %get-tuple-element.20), channel_id=1, source_target_pairs={{8,16},{24,32},{40,48},{56,64},{72,80},{88,96},{104,112},{16,8},{3... | collective-permute-start | bytes 221192 | tf_op jit(solution)/shard_map/ppermute | solution.py:487
  67.3 0.1 collective-permute-start.6
  67.4 0.6 copy.13
  68.0 0.6 copy.12
  68.6 5.6 %collective-permute-done.7 = f32[6,1,6,4,128]{4,3,2,0,1:T(4,128)S(1)} collective-permute-done((f32[6,1,6,4,128]{4,3,2,0,1:T(4,128)S(1)}, f32[6,1,6,4,128]{4,3,2,0,1:T(4,128)S(1)}, u32[]{:S(2)}, u32[]{:S(2)}) %collective-permute-start.7) | collective-permute-done | bytes 73760 | tf_op jit(solution)/shard_map/ppermute | solution.py:487
  74.2 0.0 collective-permute-done.6
  74.2 0.7 broadcast_select_fusion.4
  74.9 59.6 %rates.1 = (f32[64,128]{1,0:T(8,128)}, f32[3,64,128]{2,1,0:T(8,128)}) custom-call(s32[1760]{0:T(1024)} %constant.37.clone.tab, bf16[32,256]{1,0:T(8,128)(2,1)} %constant.38.clone.spread_ref, f32[8,64,128]{2,1,0:T(8,128)} %pad_maximum_fusion.local, f32[8,16,128]{2,1,0:T(8,128)} %bitcast.39, f32[8,16,128]{2,1,0:T(8,128)} %bitcast.37, f32[8,24,128]{2,1,0:T(8,128)} %bitcast.35, ...), custom_call_target="tpu_custom_call" | custom-call | tf_op jit(solution)/shard_map/rates/pallas_call | solution.py:458
  (11 shorter events, 0.2 us)
Async XLA Ops:
  0.6 0.9 copy-start.3
  2.6 8.4 %collective-permute-start.1 = (f32[8,4,1,4,128]{4,3,2,1,0:T(4,128)S(1)}, f32[8,4,1,4,128]{4,3,2,1,0:T(4,128)S(1)}, u32[]{:S(2)}, u32[]{:S(2)}) collective-permute-start(f32[8,4,1,4,128]{4,3,2,1,0:T(4,128)S(1)} %get-tuple-element.8), channel_id=1, source_target_pairs={{1,2},{3,4},{5,6},{2,1},{4,3},{6,5},{9,10},{11,12},{13,14},{10,9},... | collective-permute-start | bytes 196616 | tf_op jit(solution)/shard_map/ppermute | solution.py:487
  8.8 0.8 copy-start.6
  8.8 0.8 copy-start.7
  8.8 4.3 %collective-permute-start = (f32[8,4,1,4,128]{4,3,2,1,0:T(4,128)S(1)}, f32[8,4,1,4,128]{4,3,2,1,0:T(4,128)S(1)}, u32[]{:S(2)}, u32[]{:S(2)}) collective-permute-start(f32[8,4,1,4,128]{4,3,2,1,0:T(4,128)S(1)} %get-tuple-element.9), channel_id=1, source_target_pairs={{0,1},{1,0},{2,3},{3,2},{4,5},{5,4},{6,7},{7,6},{8,9},{9,8},{10,11... | collective-permute-start | bytes 196616 | tf_op jit(solution)/shard_map/ppermute | solution.py:488
  13.2 0.6 copy-start.1
  13.2 0.6 copy-start.2
  13.8 3.7 %copy-start.4 = (f32[3,4,4,4,128]{4,3,2,1,0:T(4,128)S(1)}, f32[3,4,4,4,128]{4,3,2,1,0:T(4,128)}, u32[]{:S(2)}) copy-start(f32[3,4,4,4,128]{4,3,2,1,0:T(4,128)} %param.8) | copy-start | bytes 294916
  13.8 3.7 %copy-start.5 = (f32[4,4,4,128]{3,2,1,0:T(4,128)S(1)}, f32[4,4,4,128]{3,2,1,0:T(4,128)}, u32[]{:S(2)}) copy-start(f32[4,4,4,128]{3,2,1,0:T(4,128)} %param.10) | copy-start | bytes 98308
  13.9 9.5 %collective-permute-start.3 = (f32[8,1,6,4,128]{4,3,2,1,0:T(4,128)S(1)}, f32[8,1,6,4,128]{4,3,2,1,0:T(4,128)S(1)}, u32[]{:S(2)}, u32[]{:S(2)}) collective-permute-start(f32[8,1,6,4,128]{4,3,2,1,0:T(4,128)S(1)} %get-tuple-element.16), channel_id=1, source_target_pairs={{8,16},{24,32},{40,48},{56,64},{72,80},{88,96},{104,112},{16,8},{3... | collective-permute-start | bytes 294920 | tf_op jit(solution)/shard_map/ppermute | solution.py:487
  17.4 6.1 %collective-permute-start.2 = (f32[8,1,6,4,128]{4,3,2,1,0:T(4,128)S(1)}, f32[8,1,6,4,128]{4,3,2,1,0:T(4,128)S(1)}, u32[]{:S(2)}, u32[]{:S(2)}) collective-permute-start(f32[8,1,6,4,128]{4,3,2,1,0:T(4,128)S(1)} %get-tuple-element.17), channel_id=1, source_target_pairs={{0,8},{8,0},{16,24},{24,16},{32,40},{40,32},{48,56},{56,48},{64,72... | collective-permute-start | bytes 294920 | tf_op jit(solution)/shard_map/ppermute | solution.py:488
  55.9 4.9 %copy-start = (f32[6,64,128]{2,1,0:T(8,128)S(1)}, f32[6,64,128]{2,1,0:T(8,128)}, u32[]{:S(2)}) copy-start(f32[6,64,128]{2,1,0:T(8,128)} %moments.1.corr0) | copy-start | bytes 589828
  56.8 8.1 %collective-permute-start.5 = (f32[6,4,1,4,128]{4,3,2,0,1:T(4,128)S(1)}, f32[6,4,1,4,128]{4,3,2,0,1:T(4,128)S(1)}, u32[]{:S(2)}, u32[]{:S(2)}) collective-permute-start(f32[6,4,1,4,128]{4,3,2,0,1:T(4,128)S(1)} %get-tuple-element.26), channel_id=1, source_target_pairs={{1,2},{3,4},{5,6},{2,1},{4,3},{6,5},{9,10},{11,12},{13,14},{10,9},... | collective-permute-start | bytes 147464 | tf_op jit(solution)/shard_map/ppermute | solution.py:487
  60.7 4.2 %collective-permute-start.4 = (f32[6,4,1,4,128]{4,3,2,0,1:T(4,128)S(1)}, f32[6,4,1,4,128]{4,3,2,0,1:T(4,128)S(1)}, u32[]{:S(2)}, u32[]{:S(2)}) collective-permute-start(f32[6,4,1,4,128]{4,3,2,0,1:T(4,128)S(1)} %get-tuple-element.27), channel_id=1, source_target_pairs={{0,1},{1,0},{2,3},{3,2},{4,5},{5,4},{6,7},{7,6},{8,9},{9,8},{10,11... | collective-permute-start | bytes 147464 | tf_op jit(solution)/shard_map/ppermute | solution.py:488
  65.0 9.3 %collective-permute-start.7 = (f32[6,1,6,4,128]{4,3,2,0,1:T(4,128)S(1)}, f32[6,1,6,4,128]{4,3,2,0,1:T(4,128)S(1)}, u32[]{:S(2)}, u32[]{:S(2)}) collective-permute-start(f32[6,1,6,4,128]{4,3,2,0,1:T(4,128)S(1)} %get-tuple-element.20), channel_id=1, source_target_pairs={{8,16},{24,32},{40,48},{56,64},{72,80},{88,96},{104,112},{16,8},{3... | collective-permute-start | bytes 221192 | tf_op jit(solution)/shard_map/ppermute | solution.py:487
  67.3 7.0 %collective-permute-start.6 = (f32[6,1,6,4,128]{4,3,2,0,1:T(4,128)S(1)}, f32[6,1,6,4,128]{4,3,2,0,1:T(4,128)S(1)}, u32[]{:S(2)}, u32[]{:S(2)}) collective-permute-start(f32[6,1,6,4,128]{4,3,2,0,1:T(4,128)S(1)} %get-tuple-element.21), channel_id=1, source_target_pairs={{0,8},{8,0},{16,24},{24,16},{32,40},{40,32},{48,56},{56,48},{64,72... | collective-permute-start | bytes 221192 | tf_op jit(solution)/shard_map/ppermute | solution.py:488

commit v7 on v6

--- a/solution.py
+++ b/solution.py
@@ -382,7 +382,7 @@
         part = jnp.dot(lhs[:MW], jnp.concatenate(viscous, 0), preferred_element_type=F32)
         accw[pl.ds(pl.multiple_of(i * MW, MW), MW), :] += part[:, :128] + part[:, 128:]
 
-    for_items(n, 8, one, rest)
+    for_items(n, 16, one, rest)
 
     def finish(k, carry):
         unfold(acc, M2, k, feat_ref)

time: 135 us -> 134 us (level)
  no operation moved by 1% of the time
where the time goes in v7:
time: 134 us
  Pallas kernels  90.8 us (68%)
  waiting for transfers between devices  18.3 us (14%)
  starting transfers between devices  16.4 us (12%)
  other arithmetic  4.19 us (3%)
  local copies, waits for them, and re-layouts  3.43 us (3%)
    pallas_call x1, Pallas kernels, run_rates(): pl.pallas_call(rate_kernel, out_shape=(jax.ShapeDtypeStruct((LOCAL, 128),...  59.1 us
    pallas_call x1, Pallas kernels, run_moments(): pl.pallas_call(moment_kernel, out_shape=jax.ShapeDtypeStruct((6, LOCAL, 1...  31.7 us
    ppermute x4, waiting for transfers between devices, exchange(): across = lax.ppermute(jnp.where(odd, last, first), axis, outer)  16.2 us
    ppermute x4, starting transfers between devices, exchange(): across = lax.ppermute(jnp.where(odd, last, first), axis, outer)  15.9 us
  transfers between devices with their start and end apart: 8, of which 5 were waited for; matrix products, arithmetic and copies ran while one was open for 2% of the time, Pallas kernels for 0%

profile of v7, /device:TPU:6, one launch (start us, length us, event | category | flops | bytes accessed | tf_op | source)
XLA Modules:
  0.0 134.0 jit_solution(8267024582578536278)
XLA Ops:
  0.6 0.0 copy-start.3
  0.7 0.9 fusion.7
  1.5 0.0 copy-done.3
  1.5 1.0 pad_maximum_fusion.1
  2.6 6.2 %collective-permute-start.1 = (f32[8,4,1,4,128]{4,3,2,1,0:T(4,128)S(1)}, f32[8,4,1,4,128]{4,3,2,1,0:T(4,128)S(1)}, u32[]{:S(2)}, u32[]{:S(2)}) collective-permute-start(f32[8,4,1,4,128]{4,3,2,1,0:T(4,128)S(1)} %get-tuple-element.8), channel_id=1, source_target_pairs={{1,2},{3,4},{5,6},{2,1},{4,3},{6,5},{9,10},{11,12},{13,14},{10,9},... | collective-permute-start | bytes 196616 | tf_op jit(solution)/shard_map/ppermute | solution.py:487
  8.8 0.0 copy-start.6
  8.8 0.0 copy-start.7
  8.8 0.1 collective-permute-start
  8.9 0.6 copy-done.6
  9.5 0.0 copy-done.7
  9.5 0.1 fusion
  9.6 1.4 %collective-permute-done.1 = f32[8,4,1,4,128]{4,3,2,1,0:T(4,128)S(1)} collective-permute-done((f32[8,4,1,4,128]{4,3,2,1,0:T(4,128)S(1)}, f32[8,4,1,4,128]{4,3,2,1,0:T(4,128)S(1)}, u32[]{:S(2)}, u32[]{:S(2)}) %collective-permute-start.1) | collective-permute-done | bytes 65568 | tf_op jit(solution)/shard_map/ppermute | solution.py:487
  11.0 2.1 %collective-permute-done = f32[8,4,1,4,128]{4,3,2,1,0:T(4,128)S(1)} collective-permute-done((f32[8,4,1,4,128]{4,3,2,1,0:T(4,128)S(1)}, f32[8,4,1,4,128]{4,3,2,1,0:T(4,128)S(1)}, u32[]{:S(2)}, u32[]{:S(2)}) %collective-permute-start) | collective-permute-done | bytes 65568 | tf_op jit(solution)/shard_map/ppermute | solution.py:488
  13.2 0.0 copy-start.1
  13.2 0.0 copy-start.2
  13.2 0.6 copy-done.1
  13.8 0.0 copy-done.2
  13.8 0.0 copy-start.4
  13.8 0.0 copy-start.5
  13.9 3.5 %collective-permute-start.3 = (f32[8,1,6,4,128]{4,3,2,1,0:T(4,128)S(1)}, f32[8,1,6,4,128]{4,3,2,1,0:T(4,128)S(1)}, u32[]{:S(2)}, u32[]{:S(2)}) collective-permute-start(f32[8,1,6,4,128]{4,3,2,1,0:T(4,128)S(1)} %get-tuple-element.16), channel_id=1, source_target_pairs={{8,16},{24,32},{40,48},{56,64},{72,80},{88,96},{104,112},{16,8},{3... | collective-permute-start | bytes 294920 | tf_op jit(solution)/shard_map/ppermute | solution.py:487
  17.4 0.2 collective-permute-start.2
  17.6 0.0 copy-done.4
  17.6 0.0 copy-done.5
  17.6 0.7 pad_maximum_fusion.local
  18.3 5.1 %collective-permute-done.3 = f32[8,1,6,4,128]{4,3,2,1,0:T(4,128)S(1)} collective-permute-done((f32[8,1,6,4,128]{4,3,2,1,0:T(4,128)S(1)}, f32[8,1,6,4,128]{4,3,2,1,0:T(4,128)S(1)}, u32[]{:S(2)}, u32[]{:S(2)}) %collective-permute-start.3) | collective-permute-done | bytes 98336 | tf_op jit(solution)/shard_map/ppermute | solution.py:487
  23.4 0.0 collective-permute-done.2
  23.4 0.7 broadcast_select_fusion
  24.1 31.7 %moments.1.corr0 = f32[6,64,128]{2,1,0:T(8,128)} custom-call(s32[1760]{0:T(1024)} %constant.37.clone.tab, bf16[32,256]{1,0:T(8,128)(2,1)} %constant.38.clone.spread_ref, f32[8,64,128]{2,1,0:T(8,128)} %pad_maximum_fusion.local, f32[8,16,128]{2,1,0:T(8,128)} %bitcast.38, f32[8,16,128]{2,1,0:T(8,128)} %bitcast.36, f32[8,24,128]{2,1,0:T(8,128)} %bitcast.34, ...), custom_call_target="tpu_custom_call" | custom-call | tf_op jit(solution)/shard_map/moments/pallas_call | solution.py:437
  55.9 0.0 copy-start
  55.9 0.9 fusion.2
  56.8 3.9 %collective-permute-start.5 = (f32[6,4,1,4,128]{4,3,2,0,1:T(4,128)S(1)}, f32[6,4,1,4,128]{4,3,2,0,1:T(4,128)S(1)}, u32[]{:S(2)}, u32[]{:S(2)}) collective-permute-start(f32[6,4,1,4,128]{4,3,2,0,1:T(4,128)S(1)} %get-tuple-element.26), channel_id=1, source_target_pairs={{1,2},{3,4},{5,6},{2,1},{4,3},{6,5},{9,10},{11,12},{13,14},{10,9},... | collective-permute-start | bytes 147464 | tf_op jit(solution)/shard_map/ppermute | solution.py:487
  60.7 0.1 collective-permute-start.4
  60.8 0.0 copy-done
  60.8 4.1 %collective-permute-done.5 = f32[6,4,1,4,128]{4,3,2,0,1:T(4,128)S(1)} collective-permute-done((f32[6,4,1,4,128]{4,3,2,0,1:T(4,128)S(1)}, f32[6,4,1,4,128]{4,3,2,0,1:T(4,128)S(1)}, u32[]{:S(2)}, u32[]{:S(2)}) %collective-permute-start.5) | collective-permute-done | bytes 49184 | tf_op jit(solution)/shard_map/ppermute | solution.py:487
  64.9 0.0 collective-permute-done.4
  64.9 2.3 %collective-permute-start.7 = (f32[6,1,6,4,128]{4,3,2,0,1:T(4,128)S(1)}, f32[6,1,6,4,128]{4,3,2,0,1:T(4,128)S(1)}, u32[]{:S(2)}, u32[]{:S(2)}) collective-permute-start(f32[6,1,6,4,128]{4,3,2,0,1:T(4,128)S(1)} %get-tuple-element.20), channel_id=1, source_target_pairs={{8,16},{24,32},{40,48},{56,64},{72,80},{88,96},{104,112},{16,8},{3... | collective-permute-start | bytes 221192 | tf_op jit(solution)/shard_map/ppermute | solution.py:487
  67.3 0.1 collective-permute-start.6
  67.4 0.6 copy.13
  68.0 0.6 copy.12
  68.6 5.6 %collective-permute-done.7 = f32[6,1,6,4,128]{4,3,2,0,1:T(4,128)S(1)} collective-permute-done((f32[6,1,6,4,128]{4,3,2,0,1:T(4,128)S(1)}, f32[6,1,6,4,128]{4,3,2,0,1:T(4,128)S(1)}, u32[]{:S(2)}, u32[]{:S(2)}) %collective-permute-start.7) | collective-permute-done | bytes 73760 | tf_op jit(solution)/shard_map/ppermute | solution.py:487
  74.2 0.0 collective-permute-done.6
  74.2 0.7 broadcast_select_fusion.4
  74.9 59.1 %rates.1 = (f32[64,128]{1,0:T(8,128)}, f32[3,64,128]{2,1,0:T(8,128)}) custom-call(s32[1760]{0:T(1024)} %constant.37.clone.tab, bf16[32,256]{1,0:T(8,128)(2,1)} %constant.38.clone.spread_ref, f32[8,64,128]{2,1,0:T(8,128)} %pad_maximum_fusion.local, f32[8,16,128]{2,1,0:T(8,128)} %bitcast.39, f32[8,16,128]{2,1,0:T(8,128)} %bitcast.37, f32[8,24,128]{2,1,0:T(8,128)} %bitcast.35, ...), custom_call_target="tpu_custom_call" | custom-call | tf_op jit(solution)/shard_map/rates/pallas_call | solution.py:458
  (11 shorter events, 0.2 us)
Async XLA Ops:
  0.6 0.9 copy-start.3
  2.6 8.4 %collective-permute-start.1 = (f32[8,4,1,4,128]{4,3,2,1,0:T(4,128)S(1)}, f32[8,4,1,4,128]{4,3,2,1,0:T(4,128)S(1)}, u32[]{:S(2)}, u32[]{:S(2)}) collective-permute-start(f32[8,4,1,4,128]{4,3,2,1,0:T(4,128)S(1)} %get-tuple-element.8), channel_id=1, source_target_pairs={{1,2},{3,4},{5,6},{2,1},{4,3},{6,5},{9,10},{11,12},{13,14},{10,9},... | collective-permute-start | bytes 196616 | tf_op jit(solution)/shard_map/ppermute | solution.py:487
  8.8 0.8 copy-start.6
  8.8 0.8 copy-start.7
  8.8 4.3 %collective-permute-start = (f32[8,4,1,4,128]{4,3,2,1,0:T(4,128)S(1)}, f32[8,4,1,4,128]{4,3,2,1,0:T(4,128)S(1)}, u32[]{:S(2)}, u32[]{:S(2)}) collective-permute-start(f32[8,4,1,4,128]{4,3,2,1,0:T(4,128)S(1)} %get-tuple-element.9), channel_id=1, source_target_pairs={{0,1},{1,0},{2,3},{3,2},{4,5},{5,4},{6,7},{7,6},{8,9},{9,8},{10,11... | collective-permute-start | bytes 196616 | tf_op jit(solution)/shard_map/ppermute | solution.py:488
  13.2 0.6 copy-start.1
  13.2 0.6 copy-start.2
  13.8 3.7 %copy-start.4 = (f32[3,4,4,4,128]{4,3,2,1,0:T(4,128)S(1)}, f32[3,4,4,4,128]{4,3,2,1,0:T(4,128)}, u32[]{:S(2)}) copy-start(f32[3,4,4,4,128]{4,3,2,1,0:T(4,128)} %param.8) | copy-start | bytes 294916
  13.8 3.7 %copy-start.5 = (f32[4,4,4,128]{3,2,1,0:T(4,128)S(1)}, f32[4,4,4,128]{3,2,1,0:T(4,128)}, u32[]{:S(2)}) copy-start(f32[4,4,4,128]{3,2,1,0:T(4,128)} %param.10) | copy-start | bytes 98308
  13.9 9.5 %collective-permute-start.3 = (f32[8,1,6,4,128]{4,3,2,1,0:T(4,128)S(1)}, f32[8,1,6,4,128]{4,3,2,1,0:T(4,128)S(1)}, u32[]{:S(2)}, u32[]{:S(2)}) collective-permute-start(f32[8,1,6,4,128]{4,3,2,1,0:T(4,128)S(1)} %get-tuple-element.16), channel_id=1, source_target_pairs={{8,16},{24,32},{40,48},{56,64},{72,80},{88,96},{104,112},{16,8},{3... | collective-permute-start | bytes 294920 | tf_op jit(solution)/shard_map/ppermute | solution.py:487
  17.4 6.1 %collective-permute-start.2 = (f32[8,1,6,4,128]{4,3,2,1,0:T(4,128)S(1)}, f32[8,1,6,4,128]{4,3,2,1,0:T(4,128)S(1)}, u32[]{:S(2)}, u32[]{:S(2)}) collective-permute-start(f32[8,1,6,4,128]{4,3,2,1,0:T(4,128)S(1)} %get-tuple-element.17), channel_id=1, source_target_pairs={{0,8},{8,0},{16,24},{24,16},{32,40},{40,32},{48,56},{56,48},{64,72... | collective-permute-start | bytes 294920 | tf_op jit(solution)/shard_map/ppermute | solution.py:488
  55.9 4.9 %copy-start = (f32[6,64,128]{2,1,0:T(8,128)S(1)}, f32[6,64,128]{2,1,0:T(8,128)}, u32[]{:S(2)}) copy-start(f32[6,64,128]{2,1,0:T(8,128)} %moments.1.corr0) | copy-start | bytes 589828
  56.8 8.1 %collective-permute-start.5 = (f32[6,4,1,4,128]{4,3,2,0,1:T(4,128)S(1)}, f32[6,4,1,4,128]{4,3,2,0,1:T(4,128)S(1)}, u32[]{:S(2)}, u32[]{:S(2)}) collective-permute-start(f32[6,4,1,4,128]{4,3,2,0,1:T(4,128)S(1)} %get-tuple-element.26), channel_id=1, source_target_pairs={{1,2},{3,4},{5,6},{2,1},{4,3},{6,5},{9,10},{11,12},{13,14},{10,9},... | collective-permute-start | bytes 147464 | tf_op jit(solution)/shard_map/ppermute | solution.py:487
  60.7 4.2 %collective-permute-start.4 = (f32[6,4,1,4,128]{4,3,2,0,1:T(4,128)S(1)}, f32[6,4,1,4,128]{4,3,2,0,1:T(4,128)S(1)}, u32[]{:S(2)}, u32[]{:S(2)}) collective-permute-start(f32[6,4,1,4,128]{4,3,2,0,1:T(4,128)S(1)} %get-tuple-element.27), channel_id=1, source_target_pairs={{0,1},{1,0},{2,3},{3,2},{4,5},{5,4},{6,7},{7,6},{8,9},{9,8},{10,11... | collective-permute-start | bytes 147464 | tf_op jit(solution)/shard_map/ppermute | solution.py:488
  64.9 9.3 %collective-permute-start.7 = (f32[6,1,6,4,128]{4,3,2,0,1:T(4,128)S(1)}, f32[6,1,6,4,128]{4,3,2,0,1:T(4,128)S(1)}, u32[]{:S(2)}, u32[]{:S(2)}) collective-permute-start(f32[6,1,6,4,128]{4,3,2,0,1:T(4,128)S(1)} %get-tuple-element.20), channel_id=1, source_target_pairs={{8,16},{24,32},{40,48},{56,64},{72,80},{88,96},{104,112},{16,8},{3... | collective-permute-start | bytes 221192 | tf_op jit(solution)/shard_map/ppermute | solution.py:487
  67.3 7.0 %collective-permute-start.6 = (f32[6,1,6,4,128]{4,3,2,0,1:T(4,128)S(1)}, f32[6,1,6,4,128]{4,3,2,0,1:T(4,128)S(1)}, u32[]{:S(2)}, u32[]{:S(2)}) collective-permute-start(f32[6,1,6,4,128]{4,3,2,0,1:T(4,128)S(1)} %get-tuple-element.21), channel_id=1, source_target_pairs={{0,8},{8,0},{16,24},{24,16},{32,40},{40,32},{48,56},{56,48},{64,72... | collective-permute-start | bytes 221192 | tf_op jit(solution)/shard_map/ppermute | solution.py:488
